TPU v7x, 128 devices: a whole 4x4x4 slice. The times are simulated.
128 devices in a mesh: row: 16 (over z, y), col: 8 (over x, core).
Axes of the slice: x: 4, y: 4, z: 4, core: 2. Of those that a mesh axis runs over, the one named last changes fastest.
Arguments:
- design: bfloat16 [32768, 4096], P(('row', 'col')), may hold values from -6 to 6
- weight: float32 [32768], P(('row', 'col')), may hold values from 0.2 to 5
- counts: int32 [1024], P(('row', 'col')), may hold values from 1 to 32, as said below
- column_map: int32 [4096], replicated, may hold values from 0 to 4095, each once
Outputs:
- normal: float32 [4096, 4096], P('row', 'col')
Inputs may be any that keep to these rules, and one draw needn't show every extreme that they name: column_map names each of the 4096 unknowns exactly once. `counts`: an arc may hold anything from one observation to all 32 slots.
All inputs are finite; a program needn't handle non-finite values.
Results may differ from a plain program's by a relative error of at most 0.0022.
Values may be sent and summed in bfloat16 or wider, within the bound.
No kernel may reach another device: no remote copies, remote signals or barrier semaphores. Data moves between devices by JAX's collectives and lax.ppermute only.
A program may use at most 128 MiB of HBM per device.

v0:
```python
import jax
import jax.numpy as jnp
from jax import lax
from jax.sharding import PartitionSpec as P

ARC_ROWS = 32


def transposed_product(left_cols, right_cols):
    return lax.dot_general(
        left_cols, right_cols, (((0,), (0,)), ((), ())), preferred_element_type=jnp.float32
    )


def local(design, weight, counts, column_map):
    rows_here = design.shape[0]
    slot_index = jnp.arange(rows_here, dtype=jnp.int32)
    arc_of = slot_index // ARC_ROWS
    arc_table = jnp.arange(counts.shape[0], dtype=jnp.int32)
    count_of_row = jnp.sum(
        jnp.where(arc_of[:, None] == arc_table[None, :], counts[None, :], 0), axis=1
    )
    live_rows = slot_index % ARC_ROWS < count_of_row
    row_scale = jnp.sqrt(jnp.where(live_rows, weight, jnp.zeros_like(weight)))
    scaled = (design.astype(jnp.float32) * row_scale[:, None]).astype(jnp.bfloat16)
    mapped = jnp.take(scaled, column_map, axis=1)
    total_rows = rows_here * lax.axis_size("row") * lax.axis_size("col")
    regrouped = lax.all_to_all(mapped, "row", split_axis=1, concat_axis=0, tiled=True)
    partial_value = transposed_product(
        regrouped, lax.all_gather(regrouped, "row", axis=1, tiled=True)
    )
    block_sum = lax.psum_scatter(partial_value, "col", scatter_dimension=1, tiled=True)
    return block_sum * (1.0 / total_rows)


def solution(mesh):
    return jax.shard_map(
        local,
        mesh=mesh,
        in_specs=(P(("row", "col"), None), P(("row", "col")), P(("row", "col")), P()),
        out_specs=P("row", "col"),
        check_vma=False,
    )
```

profile of v0, /device:TPU:6, one launch (start us, length us, event | category | flops | bytes accessed | tf_op | source)
XLA Modules:
  0.0 334.5 jit_solution(7011327164575581868)
XLA Ops:
  6.5 0.0 all-gather.2.cloned.1.call-start
  6.5 0.7 compare_and_fusion
  7.3 0.7 fusion
  8.0 0.0 copy-start.2
  8.0 0.0 copy-start.1
  8.0 4.1 %copy.8 = bf16[256,4096]{0,1:T(8,128)(2,1)} copy(bf16[256,4096]{1,0:T(8,128)(2,1)} %param.4) | data formatting | bytes 4194304 | tf_op args[0]
  12.1 0.0 copy-done.2
  12.1 0.1 select_reduce_fusion
  12.2 0.0 copy-done.1
  12.2 2.0 multiply_convert_fusion
  14.2 16.9 %gather_fusion = bf16[4096,256]{1,0:T(8,128)(2,1)} fusion(bf16[256,4096]{0,1:T(8,128)(2,1)S(1)} %multiply_convert_fusion, s32[4096]{0:T(1024)S(1)} %fusion), kind=kCustom, calls=%fused_computation | custom fusion | bytes 4210688 | tf_op jit(solution)/shard_map/jit(_take)/gather | solution.py:26
  31.1 2.8 copy.9
  34.0 0.2 broadcast_select_fusion
  34.2 36.3 %all_to_all.16 = bf16[256,16,256]{2,0,1:T(8,128)(2,1)} all-to-all(bf16[256,16,256]{2,0,1:T(8,128)(2,1)S(1)} %broadcast_select_fusion), channel_id=1, replica_groups=mesh['row'=16,'col'=8] {'row'}, dimensions={1} | all-to-all | bytes 4194304 | tf_op jit(solution)/shard_map/all_to_all | solution.py:28
  70.5 0.0 copy-start
  70.5 0.0 all-gather.2.cloned.1.call-update
  70.6 0.0 reduce-scatter.2.cloned.1.call-start
  70.6 204.2 %all-gather.2.cloned.1.call-done = bf16[4096,4096]{1,0:T(8,128)(2,1)} async-done(((bf16[4096,256]{1,0:T(8,128)(2,1)}), bf16[4096,4096]{1,0:T(8,128)(2,1)}) %all-gather.2.cloned.1.call-update) | async-done | bytes 33554448 | tf_op jit(solution)/shard_map/all_gather | solution.py:30
  274.8 0.0 copy-done
  274.8 17.2 %fusion.3 = f32[256,4096]{1,0:T(8,128)} fusion(bf16[4096,256]{1,0:T(8,128)(2,1)S(1)} %bitcast.9, bf16[4096,4096]{1,0:T(8,128)(2,1)} %all-gather.2.cloned.1.call-done), kind=kOutput, calls=%fused_computation.17 | convolution fusion | flops 8589934592 | bytes 39845888 | tf_op jit(solution)/shard_map/dot_general | solution.py:10
  292.0 0.0 reduce-scatter.2.cloned.1.call-update
  292.0 33.7 %reduce-scatter.2.cloned.1.call-done = f32[256,512]{1,0:T(8,128)} async-done(((f32[256,4096]{1,0:T(8,128)}), f32[256,512]{1,0:T(8,128)}) %reduce-scatter.2.cloned.1.call-update) | async-done | bytes 524304 | tf_op jit(solution)/shard_map/reduce_scatter | solution.py:32
  325.7 1.9 broadcast_multiply_fusion
  (3 shorter events, 0.0 us)
Async XLA Ops:
  6.5 268.3 %all-gather.2.cloned.1.call-start = ((), (), s32[]{:S(2)}) async-start(), calls=%async_computation.2 | async-start | bytes 35651584 | tf_op jit(solution)/shard_map/all_gather | solution.py:30
  8.0 4.1 %copy-start.2 = (s32[8]{0:T(128)S(1)}, s32[8]{0:T(128)}, u32[]{:S(2)}) copy-start(s32[8]{0:T(128)} %param.6) | copy-start | bytes 100
  8.0 4.2 %copy-start.1 = (f32[256]{0:T(256)S(1)}, f32[256]{0:T(256)}, u32[]{:S(2)}) copy-start(f32[256]{0:T(256)} %param.5) | copy-start | bytes 3076
  70.5 204.3 %copy-start = (bf16[256,16,256]{2,0,1:T(8,128)(2,1)S(1)}, bf16[256,16,256]{2,0,1:T(8,128)(2,1)}, u32[]{:S(2)}) copy-start(bf16[256,16,256]{2,0,1:T(8,128)(2,1)} %all_to_all.16) | copy-start | bytes 6291460
  70.6 255.2 %reduce-scatter.2.cloned.1.call-start = ((), (), s32[]{:S(2)}) async-start(), calls=%async_computation.3 | async-start | bytes 4718592 | tf_op jit(solution)/shard_map/reduce_scatter | solution.py:32
Sparse Core Ops, SparseCore 0:
  70.7 204.0 all-gather.1
  292.1 33.5 reduce-scatter.1
where the time goes:
time: 339 us; the launch traced here: 334 us
  waiting for transfers between devices  238 us (70%)
  blocking collectives  36.3 us (11%)
  local copies, waits for them, and re-layouts  23.9 us (7%)
  matrix products  17.2 us (5%)
  between operations  13.4 us (4%)
  other arithmetic  5.63 us (2%)
    all_gather x1, waiting for transfers between devices, local(): lax.all_gather(regrouped, 'row', axis=1, tiled=True)  204 us
    all_to_all x1, blocking collectives, local(): lax.all_to_all(mapped, 'row', split_axis=1, concat_axis=0, tiled=True)  36.3 us
    reduce_scatter x1, waiting for transfers between devices, local(): lax.psum_scatter(partial_value, 'col', scatter_dimension=1, tiled=True)  33.7 us
    gather x2, local copies, waits for them, and re-layouts, local(): mapped = jnp.take(scaled, column_map, axis=1)  19.8 us
    dot_general x1, matrix products, transposed_product(): lax.dot_general(left_cols, right_cols, (((0,), (0,)), ((), ())), preferre...  17.2 us
  transfers between devices with their start and end apart: 2, of which 2 were waited for; matrix products, arithmetic and copies ran while one was open for 0% of the time, Pallas kernels for 0%

commit v1 on v0

v1 whole, which is shorter than its diff:
```python
import functools

import jax
import jax.numpy as jnp
import numpy as np
from jax import lax
from jax.experimental import pallas as pl
from jax.experimental.pallas import tpu as pltpu
from jax.sharding import Mesh, PartitionSpec as P

ARC_ROWS = 32
AXES = ("z", "y", "x", "core")
BLK = 256
MAIN = 176
REST = BLK - MAIN
BF = jnp.bfloat16
F32 = jnp.float32


def linear(z, y, x, q):
    return ((z % 4 * 4 + y % 4) * 4 + x % 4) * 2 + q


def shift_pairs(order0, order1, sign1, stage, step):
    pairs = []
    for z in range(4):
        for y in range(4):
            for x in range(4):
                for q in range(2):
                    axis = (order0, order1)[q][stage]
                    by = step * (1, sign1)[q]
                    to = {"z": z, "y": y, "x": x}
                    to[axis] += by
                    pairs.append((linear(z, y, x, q), linear(to["z"], to["y"], to["x"], q)))
    return pairs


def mirror_pairs():
    pairs = []
    for z in range(4):
        for y in range(4):
            for x in range(4):
                for q in range(2):
                    r, c = 4 * z + y, 2 * x + q
                    i, h = r // 2, r % 2
                    if i < c:
                        to_r, to_c = 2 * c + h, i
                    elif i > c:
                        to_r, to_c = 2 * c + 1 - h, i
                    else:
                        to_r, to_c = 2 * i + 1 - h, i
                    to = linear(to_r // 4, to_r % 4, to_c // 2, to_c % 2)
                    pairs.append((linear(z, y, x, q), to))
    return pairs


MAIN_ORDER = (("x", "z", "y"), ("z", "y", "x"), 1)
REST_ORDER = (("y", "x", "z"), ("y", "x", "z"), -1)


def block_table(order, offsets, place, core):
    order0, order1, sign1 = order
    d = np.asarray(offsets, np.int32)
    at = {}
    for name in ("z", "y", "x"):
        d0 = d[:, order0.index(name)]
        d1 = d[:, order1.index(name)] * sign1
        at[name] = (place[name] + jnp.where(core == 0, d0, d1)) % 4
    r, c = 4 * at["z"] + at["y"], 2 * at["x"] + core
    i, h = r // 2, r % 2
    s = jnp.where(i <= c, h, 1 - h)
    fold = (i == c).astype(jnp.int32)
    return jnp.stack([r, 2 * c + s, 2 * c + 1 - s, fold], axis=1).reshape(-1).astype(jnp.int32)


def product_kernel(plan, table, own_ref, other_ref, *outs):
    dims = (((1,), (1,)), ((), ()))

    def dot(a, b, rows_at, rows, cols_at):
        left = a[pl.ds(rows_at, rows), :]
        right = b[pl.ds(cols_at, BLK), :]
        return lax.dot_general(left, right, dims, preferred_element_type=F32)

    for out, (first, row0, rows) in zip(outs, plan):

        @pl.loop(0, out.shape[0])
        def _(o, out=out, first=first, row0=row0, rows=rows):
            at = 4 * (first + o)
            rows_at = pl.multiple_of(table[at] * BLK + row0, 16)
            cols_at = pl.multiple_of(table[at + 1] * BLK, BLK)
            value = dot(own_ref, own_ref, rows_at, rows, cols_at)
            value += dot(other_ref, other_ref, rows_at, rows, cols_at)
            out[o] = value.astype(out.dtype)

            @pl.when(table[at + 3] == 1)
            def _():
                mixed_at = pl.multiple_of(table[at + 2] * BLK, BLK)
                mixed = dot(own_ref, own_ref, rows_at, rows, mixed_at)
                mixed += dot(other_ref, other_ref, rows_at, rows, mixed_at)
                i = lax.broadcasted_iota(jnp.int32, (rows, BLK), 0) + row0
                j = lax.broadcasted_iota(jnp.int32, (rows, BLK), 1)
                out[o] = jnp.where(i >= j, value, mixed).astype(out.dtype)


def products(own, other, parts, place, core):
    tables, plan, shapes, first = [], [], [], 0
    for order, offsets, row0, rows, kind in parts:
        tables.append(block_table(order, offsets, place, core))
        plan.append((first, row0, rows))
        shapes.append(jax.ShapeDtypeStruct((len(offsets), rows, BLK), kind))
        first += len(offsets)
    flops = sum(2 * s.shape[0] * s.shape[1] * BLK * 2 * own.shape[1] for s in shapes)
    return pl.pallas_call(
        functools.partial(product_kernel, plan),
        out_shape=shapes,
        grid_spec=pltpu.PrefetchScalarGridSpec(
            num_scalar_prefetch=1,
            grid=(1,),
            in_specs=[pl.BlockSpec(own.shape, lambda g, t: (0, 0))] * 2,
            out_specs=[pl.BlockSpec(s.shape, lambda g, t: (0, 0, 0)) for s in shapes],
        ),
        compiler_params=pltpu.CompilerParams(vmem_limit_bytes=48 * 1024 * 1024),
        cost_estimate=pl.CostEstimate(flops=flops, bytes_accessed=8 << 20, transcendentals=0),
    )(jnp.concatenate(tables), own, other)


def finish_kernel(state, scale, main_ref, rest_ref, got_ref, diag_ref, out_ref):
    s, fold = state[0], state[1] == 1
    here = jnp.concatenate([main_ref[...], rest_ref[...]], axis=0)
    got = got_ref[...].T
    mine = here.T
    i = lax.broadcasted_iota(jnp.int32, (BLK, BLK), 0)
    j = lax.broadcasted_iota(jnp.int32, (BLK, BLK), 1)
    on = jnp.logical_and(fold, i == j)
    low = jnp.logical_or(jnp.logical_not(fold), i > j)
    first = jnp.where(on, diag_ref[0:1, :], jnp.where(low, here, mine)) * scale
    second = jnp.where(on, diag_ref[1:2, :], jnp.where(low, got, here)) * scale

    @pl.when(s == 0)
    def _():
        out_ref[:, 0:BLK] = first
        out_ref[:, BLK : 2 * BLK] = second

    @pl.when(s == 1)
    def _():
        out_ref[:, BLK : 2 * BLK] = first
        out_ref[:, 0:BLK] = second


def local(design, weight, counts, column_map):
    rows_here = design.shape[0]
    core = lax.axis_index("core")
    place = {name: lax.axis_index(name) for name in ("z", "y", "x")}
    total_rows = rows_here * 128

    slot_index = jnp.arange(rows_here, dtype=jnp.int32)
    arc_of = slot_index // ARC_ROWS
    arc_table = jnp.arange(counts.shape[0], dtype=jnp.int32)
    count_of_row = jnp.sum(
        jnp.where(arc_of[:, None] == arc_table[None, :], counts[None, :], 0), axis=1
    )
    live_rows = slot_index % ARC_ROWS < count_of_row
    row_scale = jnp.sqrt(jnp.where(live_rows, weight, jnp.zeros_like(weight)))
    scaled = (design.astype(F32) * row_scale[:, None]).astype(BF)
    own = jnp.take(scaled, column_map, axis=1, mode="clip").T

    def move(array, pairs):
        return lax.ppermute(array, AXES, pairs)

    other = lax.ppermute(own, "core", [(0, 1), (1, 0)])

    wide = own.astype(F32).reshape(8, 2, BLK, rows_here)
    same = jnp.sum(wide * wide, axis=-1)
    crossed = jnp.sum(wide[:, 0] * wide[:, 1], axis=-1)
    ends = lax.psum(jnp.concatenate([same, crossed[:, None]], axis=1), AXES)

    plus = [(a, b) for a in (0, 1) for b in range(4)]
    minus = [(a, b) for a in (2, 3) for b in range(4)]
    every = plus + minus

    def offs(d, rest):
        return [(d,) + p for p in rest]

    M, R = MAIN_ORDER, REST_ORDER
    first_p, first_m, ring = products(own, other, [
        (M, offs(2, plus), 0, MAIN, BF),
        (M, offs(2, minus), 0, MAIN, BF),
        (R, offs(3, every), MAIN, REST, BF),
    ], place, core)
    side_p, side_m, ring_2 = products(own, other, [
        (M, offs(1, minus), 0, MAIN, BF),
        (M, offs(3, plus), 0, MAIN, BF),
        (R, offs(2, every), MAIN, REST, F32),
    ], place, core)
    relay_p, relay_m, ring_1, home, ring_0 = products(own, other, [
        (M, offs(1, plus), 0, MAIN, F32),
        (M, offs(3, minus), 0, MAIN, F32),
        (R, offs(1, every), MAIN, REST, F32),
        (M, offs(0, every), 0, MAIN, F32),
        (R, offs(0, every), MAIN, REST, F32),
    ], place, core)

    def main_to(stage, step):
        return shift_pairs(*M, stage, step)

    def rest_to(stage, step):
        return shift_pairs(*R, stage, step)

    got_1p = move(first_p, main_to(0, 1))
    got_1m = move(first_m, main_to(0, -1))
    got_r = move(ring, rest_to(0, 1))
    got_2p = move(side_p, main_to(0, 1))
    got_2m = move(side_m, main_to(0, -1))
    got_r = move((ring_2 + got_r.astype(F32)).astype(BF), rest_to(0, 1))
    got_3p = move((relay_p + got_1p.astype(F32)).astype(BF), main_to(0, 1))
    got_3m = move((relay_m + got_1m.astype(F32)).astype(BF), main_to(0, -1))
    got_r = move((ring_1 + got_r.astype(F32)).astype(BF), rest_to(0, 1))
    sum_p = home[:8] + got_3p.astype(F32) + got_2m.astype(F32)
    sum_m = home[8:] + got_2p.astype(F32) + got_3m.astype(F32)
    rest_sum = ring_0 + got_r.astype(F32)

    part = [sum_p[0:4], sum_p[4:8], sum_m[0:4], sum_m[4:8]]
    main_2 = part[0]
    for d in (2, 1, 3):
        main_2 = main_2 + move(part[d].astype(BF), main_to(1, d)).astype(F32)
    rest_2 = rest_sum[0:4]
    for d in (2, 1, 3):
        rest_2 = rest_2 + move(rest_sum[4 * d : 4 * d + 4].astype(BF), rest_to(1, d)).astype(F32)

    main_3 = main_2[0]
    for d in (2, 1, 3):
        main_3 = main_3 + move(main_2[d], main_to(2, d))
    rest_3 = rest_2[0]
    for d in (2, 1, 3):
        rest_3 = rest_3 + move(rest_2[d], rest_to(2, d))

    got = move(jnp.concatenate([main_3, rest_3], axis=0), mirror_pairs())

    r, c = 4 * place["z"] + place["y"], 2 * place["x"] + core
    i, h = r // 2, r % 2
    s = jnp.where(i <= c, h, 1 - h)
    state = jnp.stack([s, (i == c).astype(jnp.int32)]).astype(jnp.int32)
    picked = lax.dynamic_index_in_dim(ends, i, 0, keepdims=False)
    diag = jnp.stack([jnp.where(h == 0, picked[0], picked[1]), picked[2]])
    vmem = pl.BlockSpec(memory_space=pltpu.VMEM)
    return pl.pallas_call(
        lambda *refs: finish_kernel(refs[0], 1.0 / total_rows, *refs[1:]),
        out_shape=jax.ShapeDtypeStruct((BLK, 2 * BLK), F32),
        in_specs=[pl.BlockSpec(memory_space=pltpu.SMEM)] + [vmem] * 4,
        out_specs=vmem,
        compiler_params=pltpu.CompilerParams(vmem_limit_bytes=16 * 1024 * 1024),
    )(state, main_3, rest_3, got, diag)


def solution(mesh):
    fine = Mesh(mesh.devices.reshape(4, 4, 4, 2), AXES)
    return jax.shard_map(
        local,
        mesh=fine,
        in_specs=(P(AXES, None), P(AXES), P(AXES), P()),
        out_specs=P(("z", "y"), ("x", "core")),
        check_vma=False,
    )
```

time: 339 us -> 214 us (0.63)
  waiting for transfers between devices: 238 us -> 28 us
  Pallas kernels: 0 us -> 44 us
  starting transfers between devices: 0.04 us -> 35.5 us
  blocking collectives: 36.3 us -> 69.2 us
  matrix products: 17.2 us -> 0 us
  between operations: 13.4 us -> 0.66 us
  other arithmetic: 5.63 us -> 12.7 us
    all_gather x1 -> x0, waiting for transfers between devices: 204 us -> none  [local(): lax.all_gather(regrouped, 'row', axis=1, tiled=True)]
    psum x0 -> x1, blocking collectives: none -> 69.2 us  [local(): ends = lax.psum(jnp.concatenate([same, crossed[:, None]], axis=1), AXES)]
    pallas_call x0 -> x4, Pallas kernels: none -> 44 us  [the longest x3 42.5 us: products(): pl.pallas_call(functools.partial(product_kernel, plan), out_shape=shapes,...]
    all_to_all x1 -> x0, blocking collectives: 36.3 us -> none  [local(): lax.all_to_all(mapped, 'row', split_axis=1, concat_axis=0, tiled=True)]
    ppermute x0 -> x23, starting transfers between devices: none -> 35.5 us  [the longest x22 35.4 us: move(): return lax.ppermute(array, AXES, pairs)]
    reduce_scatter x1 -> x0, waiting for transfers between devices: 33.7 us -> none  [local(): lax.psum_scatter(partial_value, 'col', scatter_dimension=1, tiled=True)]
    ppermute x0 -> x23, waiting for transfers between devices: none -> 28 us  [the longest x22 25.4 us: move(): return lax.ppermute(array, AXES, pairs)]
    dot_general x1 -> x0, matrix products: 17.2 us -> none  [transposed_product(): lax.dot_general(left_cols, right_cols, (((0,), (0,)), ((), ())), preferre...]
  transfers between devices with their start and end apart: 2 -> 23, of which waited for: 2 -> 10; matrix products, arithmetic and copies ran while one was open for 0% -> 6% of each run, Pallas kernels for 0% -> 15%
where the time goes in v1:
time: 214 us; the launch traced here: 212 us
  blocking collectives  69.2 us (32%)
  Pallas kernels  44 us (21%)
  starting transfers between devices  35.5 us (17%)
  waiting for transfers between devices  28 us (13%)
  local copies, waits for them, and re-layouts  22.1 us (10%)
  other arithmetic  12.7 us (6%)
    psum x1, blocking collectives, local(): ends = lax.psum(jnp.concatenate([same, crossed[:, None]], axis=1), AXES)  69.2 us
    pallas_call x3, Pallas kernels, products(): pl.pallas_call(functools.partial(product_kernel, plan), out_shape=shapes,...  42.5 us
    ppermute x22, starting transfers between devices, move(): return lax.ppermute(array, AXES, pairs)  35.4 us
    ppermute x22, waiting for transfers between devices, move(): return lax.ppermute(array, AXES, pairs)  25.4 us
    gather x1, local copies, waits for them, and re-layouts, local(): own = jnp.take(scaled, column_map, axis=1, mode='clip').T  14.9 us
  transfers between devices with their start and end apart: 23, of which 10 were waited for; matrix products, arithmetic and copies ran while one was open for 6% of the time, Pallas kernels for 15%

profile of v1, /device:TPU:6, one launch (start us, length us, event | category | flops | bytes accessed | tf_op | source)
XLA Modules:
  0.0 212.2 jit_solution(1155000772746631286)
XLA Ops:
  0.0 3.3 %copy.100 = bf16[256,4096]{0,1:T(8,128)(2,1)S(1)} copy(bf16[256,4096]{1,0:T(8,128)(2,1)} %param.70) | data formatting | bytes 4194304 | tf_op args[0]
  3.4 0.1 select_reduce_fusion
  3.5 1.8 multiply_convert_fusion
  5.3 14.9 %gather_fusion = bf16[4096,256]{1,0:T(8,128)(2,1)S(1)} fusion(bf16[256,4096]{0,1:T(8,128)(2,1)} %multiply_convert_fusion, s32[4096]{0:T(1024)S(1)} %broadcast_clamp_fusion), kind=kCustom, calls=%fused_computation | custom fusion | bytes 4210688 | tf_op jit(solution)/shard_map/jit(_take)/gather | solution.py:165
  20.2 0.1 collective-permute-start
  20.6 0.1 copy.103
  20.7 0.1 reshape.84
  20.9 0.1 copy.102
  21.0 0.1 reshape.83
  21.1 0.1 copy.101
  21.2 0.1 reshape.82
  21.3 0.1 copy.106
  21.4 0.1 reshape.87
  21.6 0.1 copy.105
  21.7 0.1 reshape.86
  22.0 2.6 %collective-permute-done.other_ref = bf16[4096,256]{1,0:T(8,128)(2,1)} collective-permute-done((bf16[4096,256]{1,0:T(8,128)(2,1)S(1)}, bf16[4096,256]{1,0:T(8,128)(2,1)}, u32[]{:S(2)}, u32[]{:S(2)}) %collective-permute-start) | collective-permute-done | bytes 2097184 | tf_op jit(solution)/shard_map/ppermute | solution.py:170
  24.6 11.3 %shard_map.641 = (bf16[8,176,256]{2,1,0:T(8,128)(2,1)}, bf16[8,176,256]{2,1,0:T(8,128)(2,1)}, bf16[16,80,256]{2,1,0:T(8,128)(2,1)}) custom-call(s32[128]{0:T(128)S(1)} %get-tuple-element.134.table, bf16[4096,256]{1,0:T(8,128)(2,1)S(1)} %gather_fusion, bf16[4096,256]{1,0:T(8,128)(2,1)} %collective-permute-done.other_ref), custom_call_target="tpu_custom_call" | custom-call | flops 1073741824 | bytes 8388608 | tf_op jit(solution)/shard_map/pallas_call | solution.py:113
  35.9 2.4 %collective-permute-start.13 = (bf16[16,80,256]{2,1,0:T(8,128)(2,1)}, bf16[16,80,256]{2,1,0:T(8,128)(2,1)}, u32[]{:S(2)}, u32[]{:S(2)}) collective-permute-start(bf16[16,80,256]{2,1,0:T(8,128)(2,1)} %get-tuple-element.26), channel_id=1, source_target_pairs={{0,8},{1,25},{2,10},{3,27},{4,12},{5,29},{6,14},{7,31},{8,16},{9,1... | collective-permute-start | bytes 1966088 | tf_op jit(solution)/shard_map/ppermute | solution.py:168
  38.3 0.9 collective-permute-start.5
  39.5 0.1 copy.97
  39.6 0.1 reshape.79
  39.7 0.1 copy.98
  39.8 0.1 reshape.80
  39.9 0.1 copy.99
  40.0 0.1 reshape.81
  40.1 9.4 %shard_map.642 = (bf16[8,176,256]{2,1,0:T(8,128)(2,1)S(1)}, bf16[8,176,256]{2,1,0:T(8,128)(2,1)S(1)}, f32[16,80,256]{2,1,0:T(8,128)S(1)}) custom-call(s32[128]{0:T(128)S(1)} %get-tuple-element.135.table, bf16[4096,256]{1,0:T(8,128)(2,1)S(1)} %gather_fusion, bf16[4096,256]{1,0:T(8,128)(2,1)} %collective-permute-done.other_ref), custom_call_target="tpu_custom_call" | custom-call | flops 1073741824 | bytes 8388608 | tf_op jit(solution)/shard_map/pallas_call | solution.py:113
  49.5 2.5 %collective-permute-start.4 = (bf16[8,176,256]{2,1,0:T(8,128)(2,1)S(1)}, bf16[8,176,256]{2,1,0:T(8,128)(2,1)}, u32[]{:S(2)}, u32[]{:S(2)}) collective-permute-start(bf16[8,176,256]{2,1,0:T(8,128)(2,1)S(1)} %get-tuple-element.20), channel_id=1, source_target_pairs={{0,2},{1,33},{2,4},{3,35},{4,6},{5,37},{6,0},{7,39},{8,10},{9,41},... | collective-permute-start | bytes 2162696 | tf_op jit(solution)/shard_map/ppermute | solution.py:168
  52.0 3.2 %collective-permute-start.1 = (bf16[8,176,256]{2,1,0:T(8,128)(2,1)}, bf16[8,176,256]{2,1,0:T(8,128)(2,1)S(1)}, u32[]{:S(2)}, u32[]{:S(2)}) collective-permute-start(bf16[8,176,256]{2,1,0:T(8,128)(2,1)} %get-tuple-element.18), channel_id=1, source_target_pairs={{0,2},{1,33},{2,4},{3,35},{4,6},{5,37},{6,0},{7,39},{8,10},{9,41},... | collective-permute-start | bytes 2162696 | tf_op jit(solution)/shard_map/ppermute | solution.py:168
  55.3 21.8 %shard_map.640 = (f32[8,176,256]{2,1,0:T(8,128)S(1)}, f32[8,176,256]{2,1,0:T(8,128)S(1)}, f32[16,80,256]{2,1,0:T(8,128)S(1)}, f32[16,176,256]{2,1,0:T(8,128)}, f32[16,80,256]{2,1,0:T(8,128)S(1)}) custom-call(s32[256]{0:T(256)S(1)} %concatenate.15.table, bf16[4096,256]{1,0:T(8,128)(2,1)} %copy-done, bf16[4096,256]{1,0:T(8,128)(2,1)} %collective-permute-done.other_ref), custom_call_target="tpu_custom_call" | custom-call | flops 2147483648 | bytes 8388608 | tf_op jit(solution)/shard_map/pallas_call | solution.py:113
  77.1 1.3 add_convert_fusion.4
  78.4 0.9 collective-permute-start.14
  79.3 1.3 add_convert_fusion.1
  80.7 0.2 add_convert_fusion.2
  80.9 3.3 %collective-permute-start.2 = (bf16[8,176,256]{2,1,0:T(8,128)(2,1)S(1)}, bf16[8,176,256]{2,1,0:T(8,128)(2,1)S(1)}, u32[]{:S(2)}, u32[]{:S(2)}) collective-permute-start(bf16[8,176,256]{2,1,0:T(8,128)(2,1)S(1)} %add_convert_fusion.2), channel_id=1, source_target_pairs={{0,2},{1,33},{2,4},{3,35},{4,6},{5,37},{6,0},{7,39},{8,10},{9,41},... | collective-permute-start | bytes 2162696 | tf_op jit(solution)/shard_map/ppermute | solution.py:168
  84.2 0.4 bitcast_convert_fusion
  84.7 5.6 %collective-permute-done.14 = bf16[16,80,256]{2,1,0:T(8,128)(2,1)S(1)} collective-permute-done((bf16[16,80,256]{2,1,0:T(8,128)(2,1)S(1)}, bf16[16,80,256]{2,1,0:T(8,128)(2,1)S(1)}, u32[]{:S(2)}, u32[]{:S(2)}) %collective-permute-start.14) | collective-permute-done | bytes 655392 | tf_op jit(solution)/shard_map/ppermute | solution.py:168
  90.2 1.0 add_convert_fusion.3
  91.3 1.9 collective-permute-done.6
  93.2 1.9 add_convert_fusion
  95.1 1.0 fusion.100
  96.1 5.1 %collective-permute-start.9 = (bf16[4,176,256]{2,1,0:T(8,128)(2,1)}, bf16[4,176,256]{2,1,0:T(8,128)(2,1)}, u32[]{:S(2)}, u32[]{:S(2)}) collective-permute-start(bf16[4,176,256]{2,1,0:T(8,128)(2,1)} %get-tuple-element.84), channel_id=1, source_target_pairs={{0,96},{1,25},{2,98},{3,27},{4,100},{5,29},{6,102},{7,31},{8,104},... | collective-permute-start | bytes 1081352 | tf_op jit(solution)/shard_map/ppermute | solution.py:168
  101.2 0.8 slice.161
  102.0 1.8 collective-permute-start.7
  103.9 0.3 fusion
  104.3 0.6 multiply_reduce_fusion
  104.9 1.6 collective-permute-done.9
  106.5 8.3 %collective-permute-done.8 = bf16[4,176,256]{2,1,0:T(8,128)(2,1)} collective-permute-done((bf16[4,176,256]{2,1,0:T(8,128)(2,1)}, bf16[4,176,256]{2,1,0:T(8,128)(2,1)}, u32[]{:S(2)}, u32[]{:S(2)}) %collective-permute-start.8) | collective-permute-done | bytes 360480 | tf_op jit(solution)/shard_map/ppermute | solution.py:168
  114.8 1.6 fusion.2
  116.4 1.3 fusion.86
  117.9 3.6 %collective-permute-start.17 = (bf16[4,80,256]{2,1,0:T(8,128)(2,1)S(1)}, bf16[4,80,256]{2,1,0:T(8,128)(2,1)S(1)}, u32[]{:S(2)}, u32[]{:S(2)}) collective-permute-start(bf16[4,80,256]{2,1,0:T(8,128)(2,1)S(1)} %get-tuple-element.87), channel_id=1, source_target_pairs={{0,2},{1,7},{2,4},{3,1},{4,6},{5,3},{6,0},{7,5},{8,10},{9,15},{10,... | collective-permute-start | bytes 491528 | tf_op jit(solution)/shard_map/ppermute | solution.py:168
  121.4 1.4 collective-permute-start.16
  122.9 2.4 %collective-permute-start.12 = (f32[176,256]{1,0:T(8,128)S(1)}, f32[176,256]{1,0:T(8,128)S(1)}, u32[]{:S(2)}, u32[]{:S(2)}) collective-permute-start(f32[176,256]{1,0:T(8,128)S(1)} %get-tuple-element.81), channel_id=1, source_target_pairs={{0,24},{1,7},{2,26},{3,1},{4,28},{5,3},{6,30},{7,5},{8,0},{9,15},{... | collective-permute-start | bytes 540680 | tf_op jit(solution)/shard_map/ppermute | solution.py:168
  125.3 2.7 %collective-permute-done.18 = bf16[4,80,256]{2,1,0:T(8,128)(2,1)S(1)} collective-permute-done((bf16[4,80,256]{2,1,0:T(8,128)(2,1)S(1)}, bf16[4,80,256]{2,1,0:T(8,128)(2,1)S(1)}, u32[]{:S(2)}, u32[]{:S(2)}) %collective-permute-start.18) | collective-permute-done | bytes 163872 | tf_op jit(solution)/shard_map/ppermute | solution.py:168
  128.0 1.3 collective-permute-start.10
  129.3 0.9 collective-permute-done.16
  130.3 0.1 collective-permute-start.21
  130.5 2.0 collective-permute-start.20
  132.4 1.5 collective-permute-start.19
  134.0 1.0 collective-permute-done.10
  135.0 1.2 collective-permute-done.20
  136.3 2.1 collective-permute-done.19
  138.4 2.9 %collective-permute-start.22 = (f32[256,256]{1,0:T(8,128)S(1)}, f32[256,256]{1,0:T(8,128)S(1)}, u32[]{:S(2)}, u32[]{:S(2)}) collective-permute-start(f32[256,256]{1,0:T(8,128)S(1)} %pad_maximum_fusion), channel_id=1, source_target_pairs={{0,8},{1,16},{2,32},{3,48},{4,64},{5,80},{6,96},{7,112},{8,0},{9,2... | collective-permute-start | bytes 786440 | tf_op jit(solution)/shard_map/ppermute | solution.py:168
  141.4 69.2 %psum.7 = f32[8,3,256]{2,1,0:T(4,128)S(1)} all-reduce(f32[8,3,256]{2,1,0:T(4,128)S(1)} %pad_maximum_fusion.1), channel_id=1, replica_groups=mesh['z'=4,'y'=4,'x'=4,'core'=2] {'z','y','x','core'}, use_global_device_ids=true, to_apply=%region_3.4 | all-reduce | flops 6144 | bytes 49152 | tf_op jit(solution)/shard_map/psum | solution.py:175
  210.6 1.6 shard_map.643
  (98 shorter events, 1.7 us)
Async XLA Ops:
  0.0 3.3 %copy-start.4 = (s32[4096]{0:T(1024)S(1)}, s32[4096]{0:T(1024)}, u32[]{:S(2)}) copy-start(s32[4096]{0:T(1024)} %param.73) | copy-start | bytes 49156
  0.0 3.3 %copy-start.10 = (s32[8]{0:T(128)S(1)}, s32[8]{0:T(128)}, u32[]{:S(2)}) copy-start(s32[8]{0:T(128)} %param.72) | copy-start | bytes 100
  0.0 3.4 %copy-start.9 = (f32[256]{0:T(256)S(1)}, f32[256]{0:T(256)}, u32[]{:S(2)}) copy-start(f32[256]{0:T(256)} %param.71) | copy-start | bytes 3076
  5.3 15.1 %copy-start.8 = (s32[16]{0:T(128)S(1)}, s32[16]{0:T(128)}, u32[]{:S(2)}) copy-start(s32[16]{0:T(128)} %constant.438.clone) | copy-start | bytes 196
  5.3 15.2 %copy-start.11 = (s32[16]{0:T(128)S(1)}, s32[16]{0:T(128)}, u32[]{:S(2)}) copy-start(s32[16]{0:T(128)} %constant.434.clone) | copy-start | bytes 196
  5.3 15.2 %copy-start.12 = (s32[16]{0:T(128)S(1)}, s32[16]{0:T(128)}, u32[]{:S(2)}) copy-start(s32[16]{0:T(128)} %constant.435.clone) | copy-start | bytes 196
  5.3 15.2 %copy-start.13 = (s32[16]{0:T(128)S(1)}, s32[16]{0:T(128)}, u32[]{:S(2)}) copy-start(s32[16]{0:T(128)} %constant.439.clone) | copy-start | bytes 196
  5.3 15.5 %copy-start.5 = (s32[8]{0:T(128)S(1)}, s32[8]{0:T(128)}, u32[]{:S(2)}) copy-start(s32[8]{0:T(128)} %constant.430.clone) | copy-start | bytes 100
  5.3 15.5 %copy-start.6 = (s32[8]{0:T(128)S(1)}, s32[8]{0:T(128)}, u32[]{:S(2)}) copy-start(s32[8]{0:T(128)} %constant.432.clone) | copy-start | bytes 100
  5.3 15.5 %copy-start.7 = (s32[8]{0:T(128)S(1)}, s32[8]{0:T(128)}, u32[]{:S(2)}) copy-start(s32[8]{0:T(128)} %constant.433.clone) | copy-start | bytes 100
  20.2 19.9 %copy-start = (bf16[4096,256]{1,0:T(8,128)(2,1)}, bf16[4096,256]{1,0:T(8,128)(2,1)S(1)}, u32[]{:S(2)}) copy-start(bf16[4096,256]{1,0:T(8,128)(2,1)S(1)} %gather_fusion) | copy-start | bytes 6291460
  20.2 4.4 %collective-permute-start = (bf16[4096,256]{1,0:T(8,128)(2,1)S(1)}, bf16[4096,256]{1,0:T(8,128)(2,1)}, u32[]{:S(2)}, u32[]{:S(2)}) collective-permute-start(bf16[4096,256]{1,0:T(8,128)(2,1)S(1)} %gather_fusion), channel_id=1, source_target_pairs={{0,1},{1,0},{2,3},{3,2},{4,5},{5,4},{6,7},{7,6},{8,9},{9,8},{10,11... | collective-permute-start | bytes 6291464 | tf_op jit(solution)/shard_map/ppermute | solution.py:170
  35.9 41.2 %collective-permute-start.13 = (bf16[16,80,256]{2,1,0:T(8,128)(2,1)}, bf16[16,80,256]{2,1,0:T(8,128)(2,1)}, u32[]{:S(2)}, u32[]{:S(2)}) collective-permute-start(bf16[16,80,256]{2,1,0:T(8,128)(2,1)} %get-tuple-element.26), channel_id=1, source_target_pairs={{0,8},{1,25},{2,10},{3,27},{4,12},{5,29},{6,14},{7,31},{8,16},{9,1... | collective-permute-start | bytes 1966088 | tf_op jit(solution)/shard_map/ppermute | solution.py:168
  38.3 41.0 %collective-permute-start.5 = (bf16[8,176,256]{2,1,0:T(8,128)(2,1)}, bf16[8,176,256]{2,1,0:T(8,128)(2,1)}, u32[]{:S(2)}, u32[]{:S(2)}) collective-permute-start(bf16[8,176,256]{2,1,0:T(8,128)(2,1)} %get-tuple-element.22), channel_id=1, source_target_pairs={{0,6},{1,97},{2,0},{3,99},{4,2},{5,101},{6,4},{7,103},{8,14},{9,10... | collective-permute-start | bytes 2162696 | tf_op jit(solution)/shard_map/ppermute | solution.py:168
  49.5 41.7 %collective-permute-start.4 = (bf16[8,176,256]{2,1,0:T(8,128)(2,1)S(1)}, bf16[8,176,256]{2,1,0:T(8,128)(2,1)}, u32[]{:S(2)}, u32[]{:S(2)}) collective-permute-start(bf16[8,176,256]{2,1,0:T(8,128)(2,1)S(1)} %get-tuple-element.20), channel_id=1, source_target_pairs={{0,2},{1,33},{2,4},{3,35},{4,6},{5,37},{6,0},{7,39},{8,10},{9,41},... | collective-permute-start | bytes 2162696 | tf_op jit(solution)/shard_map/ppermute | solution.py:168
  52.0 39.3 %collective-permute-start.3 = (bf16[8,176,256]{2,1,0:T(8,128)(2,1)S(1)}, bf16[8,176,256]{2,1,0:T(8,128)(2,1)}, u32[]{:S(2)}, u32[]{:S(2)}) collective-permute-start(bf16[8,176,256]{2,1,0:T(8,128)(2,1)S(1)} %get-tuple-element.19), channel_id=1, source_target_pairs={{0,6},{1,97},{2,0},{3,99},{4,2},{5,101},{6,4},{7,103},{8,14},{9,10... | collective-permute-start | bytes 2162696 | tf_op jit(solution)/shard_map/ppermute | solution.py:168
  52.0 28.7 %collective-permute-start.1 = (bf16[8,176,256]{2,1,0:T(8,128)(2,1)}, bf16[8,176,256]{2,1,0:T(8,128)(2,1)S(1)}, u32[]{:S(2)}, u32[]{:S(2)}) collective-permute-start(bf16[8,176,256]{2,1,0:T(8,128)(2,1)} %get-tuple-element.18), channel_id=1, source_target_pairs={{0,2},{1,33},{2,4},{3,35},{4,6},{5,37},{6,0},{7,39},{8,10},{9,41},... | collective-permute-start | bytes 2162696 | tf_op jit(solution)/shard_map/ppermute | solution.py:168
  78.4 11.9 %collective-permute-start.14 = (bf16[16,80,256]{2,1,0:T(8,128)(2,1)S(1)}, bf16[16,80,256]{2,1,0:T(8,128)(2,1)S(1)}, u32[]{:S(2)}, u32[]{:S(2)}) collective-permute-start(bf16[16,80,256]{2,1,0:T(8,128)(2,1)S(1)} %add_convert_fusion.4), channel_id=1, source_target_pairs={{0,8},{1,25},{2,10},{3,27},{4,12},{5,29},{6,14},{7,31},{8,16},{9,1... | collective-permute-start | bytes 1966088 | tf_op jit(solution)/shard_map/ppermute | solution.py:168
  80.6 12.6 %collective-permute-start.6 = (bf16[8,176,256]{2,1,0:T(8,128)(2,1)S(1)}, bf16[8,176,256]{2,1,0:T(8,128)(2,1)S(1)}, u32[]{:S(2)}, u32[]{:S(2)}) collective-permute-start(bf16[8,176,256]{2,1,0:T(8,128)(2,1)S(1)} %add_convert_fusion.1), channel_id=1, source_target_pairs={{0,6},{1,97},{2,0},{3,99},{4,2},{5,101},{6,4},{7,103},{8,14},{9,10... | collective-permute-start | bytes 2162696 | tf_op jit(solution)/shard_map/ppermute | solution.py:168
  80.7 3.5 %copy-start.1 = (bf16[4096,256]{1,0:T(8,128)(2,1)S(1)}, bf16[4096,256]{1,0:T(8,128)(2,1)}, u32[]{:S(2)}) copy-start(bf16[4096,256]{1,0:T(8,128)(2,1)} %copy-done) | copy-start | bytes 6291460
  80.9 12.3 %collective-permute-start.2 = (bf16[8,176,256]{2,1,0:T(8,128)(2,1)S(1)}, bf16[8,176,256]{2,1,0:T(8,128)(2,1)S(1)}, u32[]{:S(2)}, u32[]{:S(2)}) collective-permute-start(bf16[8,176,256]{2,1,0:T(8,128)(2,1)S(1)} %add_convert_fusion.2), channel_id=1, source_target_pairs={{0,2},{1,33},{2,4},{3,35},{4,6},{5,37},{6,0},{7,39},{8,10},{9,41},... | collective-permute-start | bytes 2162696 | tf_op jit(solution)/shard_map/ppermute | solution.py:168
  84.2 9.0 %copy-start.3 = (f32[16,176,256]{2,1,0:T(8,128)S(1)}, f32[16,176,256]{2,1,0:T(8,128)}, u32[]{:S(2)}) copy-start(f32[16,176,256]{2,1,0:T(8,128)} %get-tuple-element.16) | copy-start | bytes 8650756
  91.3 25.1 %collective-permute-start.15 = (bf16[16,80,256]{2,1,0:T(8,128)(2,1)}, bf16[16,80,256]{2,1,0:T(8,128)(2,1)}, u32[]{:S(2)}, u32[]{:S(2)}) collective-permute-start(bf16[16,80,256]{2,1,0:T(8,128)(2,1)} %add_convert_fusion.3), channel_id=1, source_target_pairs={{0,8},{1,25},{2,10},{3,27},{4,12},{5,29},{6,14},{7,31},{8,16},{9,1... | collective-permute-start | bytes 1966088 | tf_op jit(solution)/shard_map/ppermute | solution.py:168
  95.1 6.1 %copy-start.2 = (f32[8,176,256]{2,1,0:T(8,128)}, f32[8,176,256]{2,1,0:T(8,128)S(1)}, u32[]{:S(2)}) copy-start(f32[8,176,256]{2,1,0:T(8,128)S(1)} %get-tuple-element.79) | copy-start | bytes 4325380
  96.1 10.4 %collective-permute-start.9 = (bf16[4,176,256]{2,1,0:T(8,128)(2,1)}, bf16[4,176,256]{2,1,0:T(8,128)(2,1)}, u32[]{:S(2)}, u32[]{:S(2)}) collective-permute-start(bf16[4,176,256]{2,1,0:T(8,128)(2,1)} %get-tuple-element.84), channel_id=1, source_target_pairs={{0,96},{1,25},{2,98},{3,27},{4,100},{5,29},{6,102},{7,31},{8,104},... | collective-permute-start | bytes 1081352 | tf_op jit(solution)/shard_map/ppermute | solution.py:168
  102.0 12.8 %collective-permute-start.8 = (bf16[4,176,256]{2,1,0:T(8,128)(2,1)}, bf16[4,176,256]{2,1,0:T(8,128)(2,1)}, u32[]{:S(2)}, u32[]{:S(2)}) collective-permute-start(bf16[4,176,256]{2,1,0:T(8,128)(2,1)} %slice.161), channel_id=1, source_target_pairs={{0,32},{1,9},{2,34},{3,11},{4,36},{5,13},{6,38},{7,15},{8,40},{9,1... | collective-permute-start | bytes 1081352 | tf_op jit(solution)/shard_map/ppermute | solution.py:168
  102.0 12.8 %collective-permute-start.7 = (bf16[4,176,256]{2,1,0:T(8,128)(2,1)}, bf16[4,176,256]{2,1,0:T(8,128)(2,1)}, u32[]{:S(2)}, u32[]{:S(2)}) collective-permute-start(bf16[4,176,256]{2,1,0:T(8,128)(2,1)} %get-tuple-element.83), channel_id=1, source_target_pairs={{0,64},{1,17},{2,66},{3,19},{4,68},{5,21},{6,70},{7,23},{8,72},{9,... | collective-permute-start | bytes 1081352 | tf_op jit(solution)/shard_map/ppermute | solution.py:168
  117.8 10.2 %collective-permute-start.18 = (bf16[4,80,256]{2,1,0:T(8,128)(2,1)S(1)}, bf16[4,80,256]{2,1,0:T(8,128)(2,1)S(1)}, u32[]{:S(2)}, u32[]{:S(2)}) collective-permute-start(bf16[4,80,256]{2,1,0:T(8,128)(2,1)S(1)} %get-tuple-element.86), channel_id=1, source_target_pairs={{0,6},{1,3},{2,0},{3,5},{4,2},{5,7},{6,4},{7,1},{8,14},{9,11},{10,... | collective-permute-start | bytes 491528 | tf_op jit(solution)/shard_map/ppermute | solution.py:168
  117.9 11.4 %collective-permute-start.17 = (bf16[4,80,256]{2,1,0:T(8,128)(2,1)S(1)}, bf16[4,80,256]{2,1,0:T(8,128)(2,1)S(1)}, u32[]{:S(2)}, u32[]{:S(2)}) collective-permute-start(bf16[4,80,256]{2,1,0:T(8,128)(2,1)S(1)} %get-tuple-element.87), channel_id=1, source_target_pairs={{0,2},{1,7},{2,4},{3,1},{4,6},{5,3},{6,0},{7,5},{8,10},{9,15},{10,... | collective-permute-start | bytes 491528 | tf_op jit(solution)/shard_map/ppermute | solution.py:168
  121.4 8.8 %collective-permute-start.16 = (bf16[4,80,256]{2,1,0:T(8,128)(2,1)S(1)}, bf16[4,80,256]{2,1,0:T(8,128)(2,1)S(1)}, u32[]{:S(2)}, u32[]{:S(2)}) collective-permute-start(bf16[4,80,256]{2,1,0:T(8,128)(2,1)S(1)} %get-tuple-element.85), channel_id=1, source_target_pairs={{0,4},{1,5},{2,6},{3,7},{4,0},{5,1},{6,2},{7,3},{8,12},{9,13},{10,... | collective-permute-start | bytes 491528 | tf_op jit(solution)/shard_map/ppermute | solution.py:168
  122.9 9.6 %collective-permute-start.12 = (f32[176,256]{1,0:T(8,128)S(1)}, f32[176,256]{1,0:T(8,128)S(1)}, u32[]{:S(2)}, u32[]{:S(2)}) collective-permute-start(f32[176,256]{1,0:T(8,128)S(1)} %get-tuple-element.81), channel_id=1, source_target_pairs={{0,24},{1,7},{2,26},{3,1},{4,28},{5,3},{6,30},{7,5},{8,0},{9,15},{... | collective-permute-start | bytes 540680 | tf_op jit(solution)/shard_map/ppermute | solution.py:168
  125.3 8.7 %collective-permute-start.11 = (f32[176,256]{1,0:T(8,128)S(1)}, f32[176,256]{1,0:T(8,128)S(1)}, u32[]{:S(2)}, u32[]{:S(2)}) collective-permute-start(f32[176,256]{1,0:T(8,128)S(1)} %get-tuple-element.82), channel_id=1, source_target_pairs={{0,8},{1,3},{2,10},{3,5},{4,12},{5,7},{6,14},{7,1},{8,16},{9,11},{... | collective-permute-start | bytes 540680 | tf_op jit(solution)/shard_map/ppermute | solution.py:168
  128.0 7.0 %collective-permute-start.10 = (f32[176,256]{1,0:T(8,128)S(1)}, f32[176,256]{1,0:T(8,128)S(1)}, u32[]{:S(2)}, u32[]{:S(2)}) collective-permute-start(f32[176,256]{1,0:T(8,128)S(1)} %get-tuple-element.80), channel_id=1, source_target_pairs={{0,16},{1,5},{2,18},{3,7},{4,20},{5,1},{6,22},{7,3},{8,24},{9,13},... | collective-permute-start | bytes 540680 | tf_op jit(solution)/shard_map/ppermute | solution.py:168
  130.3 4.7 %collective-permute-start.21 = (f32[80,256]{1,0:T(8,128)S(1)}, f32[80,256]{1,0:T(8,128)S(1)}, u32[]{:S(2)}, u32[]{:S(2)}) collective-permute-start(f32[80,256]{1,0:T(8,128)S(1)} %get-tuple-element.89), channel_id=1, source_target_pairs={{0,96},{1,33},{2,98},{3,35},{4,100},{5,37},{6,102},{7,39},{8,104},... | collective-permute-start | bytes 245768 | tf_op jit(solution)/shard_map/ppermute | solution.py:168
  130.5 5.8 %collective-permute-start.20 = (f32[80,256]{1,0:T(8,128)S(1)}, f32[80,256]{1,0:T(8,128)S(1)}, u32[]{:S(2)}, u32[]{:S(2)}) collective-permute-start(f32[80,256]{1,0:T(8,128)S(1)} %get-tuple-element.90), channel_id=1, source_target_pairs={{0,32},{1,97},{2,34},{3,99},{4,36},{5,101},{6,38},{7,103},{8,40},{... | collective-permute-start | bytes 245768 | tf_op jit(solution)/shard_map/ppermute | solution.py:168
  132.4 5.9 %collective-permute-start.19 = (f32[80,256]{1,0:T(8,128)S(1)}, f32[80,256]{1,0:T(8,128)S(1)}, u32[]{:S(2)}, u32[]{:S(2)}) collective-permute-start(f32[80,256]{1,0:T(8,128)S(1)} %get-tuple-element.88), channel_id=1, source_target_pairs={{0,64},{1,65},{2,66},{3,67},{4,68},{5,69},{6,70},{7,71},{8,72},{9,... | collective-permute-start | bytes 245768 | tf_op jit(solution)/shard_map/ppermute | solution.py:168
  138.4 72.2 %collective-permute-start.22 = (f32[256,256]{1,0:T(8,128)S(1)}, f32[256,256]{1,0:T(8,128)S(1)}, u32[]{:S(2)}, u32[]{:S(2)}) collective-permute-start(f32[256,256]{1,0:T(8,128)S(1)} %pad_maximum_fusion), channel_id=1, source_target_pairs={{0,8},{1,16},{2,32},{3,48},{4,64},{5,80},{6,96},{7,112},{8,0},{9,2... | collective-permute-start | bytes 786440 | tf_op jit(solution)/shard_map/ppermute | solution.py:168

commit v2 on v1

v2 whole, which is shorter than its diff:
```python
import functools

import jax
import jax.numpy as jnp
import numpy as np
from jax import lax
from jax.experimental import pallas as pl
from jax.experimental.pallas import tpu as pltpu
from jax.sharding import Mesh, PartitionSpec as P

ARC_ROWS = 32
AXES = ("z", "y", "x", "core")
BLK = 256
MAIN = 176
REST = BLK - MAIN
EXTRA = 16
BF = jnp.bfloat16
F32 = jnp.float32


def linear(z, y, x, q):
    return ((z % 4 * 4 + y % 4) * 4 + x % 4) * 2 + q


def shift_pairs(order0, order1, sign1, stage, step):
    pairs = []
    for z in range(4):
        for y in range(4):
            for x in range(4):
                for q in range(2):
                    axis = (order0, order1)[q][stage]
                    by = step * (1, sign1)[q]
                    to = {"z": z, "y": y, "x": x}
                    to[axis] += by
                    pairs.append((linear(z, y, x, q), linear(to["z"], to["y"], to["x"], q)))
    return pairs


def mirror_pairs():
    pairs = []
    for z in range(4):
        for y in range(4):
            for x in range(4):
                for q in range(2):
                    r, c = 4 * z + y, 2 * x + q
                    i, h = r // 2, r % 2
                    if i < c:
                        to_r, to_c = 2 * c + h, i
                    elif i > c:
                        to_r, to_c = 2 * c + 1 - h, i
                    else:
                        to_r, to_c = 2 * i + 1 - h, i
                    to = linear(to_r // 4, to_r % 4, to_c // 2, to_c % 2)
                    pairs.append((linear(z, y, x, q), to))
    return pairs


MAIN_ORDER = (("x", "z", "y"), ("z", "y", "x"), 1)
REST_ORDER = (("y", "x", "z"), ("y", "x", "z"), -1)


def block_table(order, offsets, place, core):
    order0, order1, sign1 = order
    d = np.asarray(offsets, np.int32)
    at = {}
    for name in ("z", "y", "x"):
        d0 = d[:, order0.index(name)]
        d1 = d[:, order1.index(name)] * sign1
        at[name] = (place[name] + jnp.where(core == 0, d0, d1)) % 4
    r, c = 4 * at["z"] + at["y"], 2 * at["x"] + core
    i, h = r // 2, r % 2
    s = jnp.where(i <= c, h, 1 - h)
    fold = (i == c).astype(jnp.int32)
    return jnp.stack([r, 2 * c + s, 2 * c + 1 - s, fold], axis=1).reshape(-1).astype(jnp.int32)


def gather_kernel(map_ref, scale_ref, design_ref, out_ref, turned, picked):
    width, half = design_ref.shape[0], design_ref.shape[0] // 2
    tiles, unroll = design_ref.shape[1] // width, 32

    @pl.loop(0, tiles)
    def _(t):
        at = pl.multiple_of(t * width, width)
        block = (design_ref[:, pl.ds(at, width)].astype(F32) * scale_ref[...]).astype(BF)
        wide = block.T.astype(F32)
        for h in range(2):
            turned[pl.ds(2 * at + h, width, 2), :] = wide[:, h * half : (h + 1) * half]

    @pl.loop(0, out_ref.shape[0] // unroll)
    def _(g):
        rows = [turned[pl.ds(2 * map_ref[g * unroll + u], 2), :] for u in range(unroll)]
        for u in range(unroll):
            picked[pl.ds(2 * (g * unroll + u), 2), :] = rows[u]

    @pl.loop(0, tiles)
    def _(t):
        at = pl.multiple_of(t * width, width)
        for h in range(2):
            out_ref[pl.ds(at, width), pl.ds(h * half, half)] = picked[
                pl.ds(2 * at + h, width, 2), :
            ].astype(BF)


def scaled_rows(column_map, row_scale, design):
    rows, unknowns = design.shape
    vmem = pl.BlockSpec(memory_space=pltpu.VMEM)
    return pl.pallas_call(
        gather_kernel,
        out_shape=jax.ShapeDtypeStruct((unknowns, rows), BF),
        in_specs=[pl.BlockSpec(memory_space=pltpu.SMEM), vmem, vmem],
        out_specs=vmem,
        scratch_shapes=[pltpu.VMEM((2 * unknowns, rows // 2), F32)] * 2,
        compiler_params=pltpu.CompilerParams(vmem_limit_bytes=20 * 1024 * 1024),
        cost_estimate=pl.CostEstimate(flops=0, bytes_accessed=16 << 20, transcendentals=0),
    )(column_map, row_scale[:, None], design)


def product_kernel(plan, turn, table, own_ref, other_ref, *refs):
    outs = refs[: len(plan)]
    both = (own_ref, other_ref)
    if turn:
        turned = refs[len(plan) :]

        @pl.loop(0, own_ref.shape[0] // BLK)
        def _(t):
            at = pl.multiple_of(t * BLK, BLK)
            for ref, to in zip(both, turned):
                to[:, pl.ds(at, BLK)] = ref[pl.ds(at, BLK), :].T

    def dot(rows_at, rows, cols_at):
        total = None
        for k, ref in enumerate(both):
            left = ref[pl.ds(rows_at, rows), :]
            if turn:
                part = jnp.dot(left, turned[k][:, pl.ds(cols_at, BLK)], preferred_element_type=F32)
            else:
                right = ref[pl.ds(cols_at, BLK), :]
                part = lax.dot_general(left, right, (((1,), (1,)), ((), ())), preferred_element_type=F32)
            total = part if total is None else total + part
        return total

    i = lax.broadcasted_iota(jnp.int32, (BLK, BLK), 0)
    j = lax.broadcasted_iota(jnp.int32, (BLK, BLK), 1)
    end = max(first + count for first, count, _, _, _ in plan)
    if any(ring for _, _, _, _, ring in plan):
        lines = []
        for e in range(4):
            at = 4 * (end + e)
            cross = dot(pl.multiple_of(table[at] * BLK, BLK), BLK, pl.multiple_of(table[at + 1] * BLK, BLK))
            lines.append(jnp.sum(jnp.where(i == j, cross, 0.0), axis=0, keepdims=True))
        lines = jnp.concatenate(lines + [jnp.zeros((EXTRA - 4, BLK), F32)], axis=0)

    for out, (first, count, row0, rows, ring) in zip(outs, plan):

        def put(o, value, out=out, rows=rows, ring=ring):
            if ring:
                out[pl.ds(pl.multiple_of(o * rows, 16), rows), :] = value.astype(out.dtype)
            else:
                out[o] = value.astype(out.dtype)

        @pl.loop(0, count // 4)
        def _(g, first=first, row0=row0, rows=rows, put=put):
            starts, values = [], []
            for u in range(4):
                at = 4 * (first + g * 4 + u)
                rows_at = pl.multiple_of(table[at] * BLK + row0, 16)
                starts.append(rows_at)
                values.append(dot(rows_at, rows, pl.multiple_of(table[at + 1] * BLK, BLK)))
            for u in range(4):
                put(g * 4 + u, values[u])
            for u in range(4):
                at = 4 * (first + g * 4 + u)

                @pl.when(table[at + 3] == 1)
                def _(u=u, at=at):
                    cols_at = pl.multiple_of(table[at + 1] * BLK, BLK)
                    mixed_at = pl.multiple_of(table[at + 2] * BLK, BLK)
                    value = dot(starts[u], rows, cols_at)
                    mixed = dot(starts[u], rows, mixed_at)
                    low = i[:rows] + row0 >= j[:rows]
                    put(g * 4 + u, jnp.where(low, value, mixed))

        if ring:
            out[pl.ds(count * rows, EXTRA), :] = lines.astype(out.dtype)


def products(own, other, parts, place, core, turn):
    tables, plan, shapes, first, flops = [], [], [], 0, 0
    for order, offsets, row0, rows, kind, ring in parts:
        count = len(offsets)
        tables.append(block_table(order, offsets, place, core))
        plan.append((first, count, row0, rows, ring))
        shape = (count * rows + EXTRA, BLK) if ring else (count, rows, BLK)
        shapes.append(jax.ShapeDtypeStruct(shape, kind))
        first += count
        flops += 4 * count * rows * BLK * own.shape[1]
    step = jnp.where(core == 0, 1, REST_ORDER[2]) * jnp.arange(4, dtype=jnp.int32)
    pair = 2 * (2 * ((place["x"] + step) % 4) + core)
    none = jnp.zeros_like(pair)
    tables.append(jnp.stack([pair, pair + 1, none, none], axis=1).reshape(-1).astype(jnp.int32))
    scratch = [pltpu.VMEM(own.shape[::-1], BF)] * 2 if turn else []
    vmem = pl.BlockSpec(memory_space=pltpu.VMEM)
    return pl.pallas_call(
        functools.partial(product_kernel, plan, turn),
        out_shape=shapes,
        in_specs=[pl.BlockSpec(memory_space=pltpu.SMEM), vmem, vmem],
        out_specs=[vmem] * len(shapes),
        scratch_shapes=scratch,
        compiler_params=pltpu.CompilerParams(vmem_limit_bytes=28 * 1024 * 1024),
        cost_estimate=pl.CostEstimate(flops=flops, bytes_accessed=8 << 20, transcendentals=0),
    )(jnp.concatenate(tables), own, other)


def finish_kernel(state, scale, main_ref, rest_ref, got_ref, cross_ref, out_ref):
    s, fold = state[0], state[1] == 1
    here = jnp.concatenate([main_ref[...], rest_ref[...]], axis=0)
    got = got_ref[...].T
    mine = here.T
    i = lax.broadcasted_iota(jnp.int32, (BLK, BLK), 0)
    j = lax.broadcasted_iota(jnp.int32, (BLK, BLK), 1)
    on = jnp.logical_and(fold, i == j)
    low = jnp.logical_or(jnp.logical_not(fold), i >= j)
    first = jnp.where(low, here, mine) * scale
    second = jnp.where(on, cross_ref[0:1, :], jnp.where(low, got, here)) * scale

    @pl.when(s == 0)
    def _():
        out_ref[:, 0:BLK] = first
        out_ref[:, BLK : 2 * BLK] = second

    @pl.when(s == 1)
    def _():
        out_ref[:, BLK : 2 * BLK] = first
        out_ref[:, 0:BLK] = second


def local(design, weight, counts, column_map):
    rows_here = design.shape[0]
    core = lax.axis_index("core")
    place = {name: lax.axis_index(name) for name in ("z", "y", "x")}
    total_rows = rows_here * 128

    slot_index = jnp.arange(rows_here, dtype=jnp.int32)
    arc_of = slot_index // ARC_ROWS
    arc_table = jnp.arange(counts.shape[0], dtype=jnp.int32)
    count_of_row = jnp.sum(
        jnp.where(arc_of[:, None] == arc_table[None, :], counts[None, :], 0), axis=1
    )
    live_rows = slot_index % ARC_ROWS < count_of_row
    row_scale = jnp.sqrt(jnp.where(live_rows, weight, jnp.zeros_like(weight)))
    own = scaled_rows(column_map, row_scale, design)

    def move(array, pairs):
        return lax.ppermute(array, AXES, pairs)

    other = lax.ppermute(own, "core", [(0, 1), (1, 0)])

    plus = [(a, b) for a in (0, 1) for b in range(4)]
    minus = [(a, b) for a in (2, 3) for b in range(4)]
    every = plus + minus

    def offs(d, rest):
        return [(d,) + p for p in rest]

    M, R = MAIN_ORDER, REST_ORDER
    first_p, first_m, ring = products(own, other, [
        (M, offs(2, plus), 0, MAIN, BF, False),
        (M, offs(2, minus), 0, MAIN, BF, False),
        (R, offs(3, every), MAIN, REST, BF, True),
    ], place, core, False)
    side_p, side_m, ring_2 = products(own, other, [
        (M, offs(1, minus), 0, MAIN, BF, False),
        (M, offs(3, plus), 0, MAIN, BF, False),
        (R, offs(2, every), MAIN, REST, F32, True),
    ], place, core, True)
    relay_p, relay_m, ring_1, home, ring_0 = products(own, other, [
        (M, offs(1, plus), 0, MAIN, F32, False),
        (M, offs(3, minus), 0, MAIN, F32, False),
        (R, offs(1, every), MAIN, REST, F32, True),
        (M, offs(0, every), 0, MAIN, F32, False),
        (R, offs(0, every), MAIN, REST, F32, True),
    ], place, core, True)

    def main_to(stage, step):
        return shift_pairs(*M, stage, step)

    def rest_to(stage, step):
        return shift_pairs(*R, stage, step)

    got_1p = move(first_p, main_to(0, 1))
    got_1m = move(first_m, main_to(0, -1))
    got_r = move(ring, rest_to(0, 1))
    got_2p = move(side_p, main_to(0, 1))
    got_2m = move(side_m, main_to(0, -1))
    got_r = move((ring_2 + got_r.astype(F32)).astype(BF), rest_to(0, 1))
    got_3p = move((relay_p + got_1p.astype(F32)).astype(BF), main_to(0, 1))
    got_3m = move((relay_m + got_1m.astype(F32)).astype(BF), main_to(0, -1))
    got_r = move((ring_1 + got_r.astype(F32)).astype(BF), rest_to(0, 1))
    sum_p = home[:8] + got_3p.astype(F32) + got_2m.astype(F32)
    sum_m = home[8:] + got_2p.astype(F32) + got_3m.astype(F32)
    rest_sum = ring_0 + got_r.astype(F32)

    part = [sum_p[0:4], sum_p[4:8], sum_m[0:4], sum_m[4:8]]
    main_2 = part[0]
    for d in (2, 1, 3):
        main_2 = main_2 + move(part[d].astype(BF), main_to(1, d)).astype(F32)
    quarter = 4 * REST
    rest_2, cross = rest_sum[:quarter], rest_sum[4 * quarter : 4 * quarter + 1]
    tail = rest_sum[4 * quarter :]
    for d in (2, 1, 3):
        piece = jnp.concatenate([rest_sum[d * quarter : (d + 1) * quarter], tail], axis=0)
        piece = move(piece.astype(BF), rest_to(1, d)).astype(F32)
        rest_2 = rest_2 + piece[:quarter]
        cross = cross + piece[quarter + d : quarter + d + 1]

    main_3 = main_2[0]
    for d in (2, 1, 3):
        main_3 = main_3 + move(main_2[d], main_to(2, d))
    rest_3, extra = rest_2[:REST], jnp.broadcast_to(cross, (8, BLK))
    cross = extra
    for d in (2, 1, 3):
        piece = jnp.concatenate([rest_2[d * REST : (d + 1) * REST], extra], axis=0)
        piece = move(piece, rest_to(2, d))
        rest_3 = rest_3 + piece[:REST]
        cross = cross + piece[REST:]

    got = move(jnp.concatenate([main_3, rest_3], axis=0), mirror_pairs())

    r, c = 4 * place["z"] + place["y"], 2 * place["x"] + core
    i, h = r // 2, r % 2
    s = jnp.where(i <= c, h, 1 - h)
    state = jnp.stack([s, (i == c).astype(jnp.int32)]).astype(jnp.int32)
    vmem = pl.BlockSpec(memory_space=pltpu.VMEM)
    return pl.pallas_call(
        lambda *refs: finish_kernel(refs[0], 1.0 / total_rows, *refs[1:]),
        out_shape=jax.ShapeDtypeStruct((BLK, 2 * BLK), F32),
        in_specs=[pl.BlockSpec(memory_space=pltpu.SMEM)] + [vmem] * 4,
        out_specs=vmem,
        compiler_params=pltpu.CompilerParams(vmem_limit_bytes=16 * 1024 * 1024),
    )(state, main_3, rest_3, got, cross)


def solution(mesh):
    fine = Mesh(mesh.devices.reshape(4, 4, 4, 2), AXES)
    return jax.shard_map(
        local,
        mesh=fine,
        in_specs=(P(AXES, None), P(AXES), P(AXES), P()),
        out_specs=P(("z", "y"), ("x", "core")),
        check_vma=False,
    )
```

time: 214 us -> 142 us (0.66)
  blocking collectives: 69.2 us -> 0 us
  waiting for transfers between devices: 28 us -> 49.9 us
  local copies, waits for them, and re-layouts: 22.1 us -> 6.35 us
  Pallas kernels: 44 us -> 38.8 us
  other arithmetic: 12.7 us -> 8.2 us
    psum x1 -> x0, blocking collectives: 69.2 us -> none  [local(): ends = lax.psum(jnp.concatenate([same, crossed[:, None]], axis=1), AXES)]
    ppermute x22, waiting for transfers between devices: 25.4 us -> 47.6 us  [move(): return lax.ppermute(array, AXES, pairs)]
    gather x1 -> x0, local copies, waits for them, and re-layouts: 14.9 us -> none  [local(): own = jnp.take(scaled, column_map, axis=1, mode='clip').T]
    pallas_call x3 -> x4, Pallas kernels: 42.5 us -> 37.3 us  [the longest x3 28.6 us: products(): pl.pallas_call(functools.partial(product_kernel, plan, turn), out_shape=s...]
  transfers between devices with their start and end apart: 23 -> 23, of which waited for: 10 -> 11; matrix products, arithmetic and copies ran while one was open for 6% -> 7% of each run, Pallas kernels for 15% -> 15%
where the time goes in v2:
time: 142 us; the launch traced here: 141 us
  waiting for transfers between devices  49.9 us (35%)
  Pallas kernels  38.8 us (27%)
  starting transfers between devices  37.3 us (26%)
  other arithmetic  8.2 us (6%)
  local copies, waits for them, and re-layouts  6.35 us (4%)
    ppermute x22, waiting for transfers between devices, move(): return lax.ppermute(array, AXES, pairs)  47.6 us
    ppermute x22, starting transfers between devices, move(): return lax.ppermute(array, AXES, pairs)  37.2 us
    pallas_call x3, Pallas kernels, products(): pl.pallas_call(functools.partial(product_kernel, plan, turn), out_shape=s...  28.6 us
    pallas_call x1, Pallas kernels, scaled_rows(): pl.pallas_call(gather_kernel, out_shape=jax.ShapeDtypeStruct((unknowns, r...  8.64 us
  transfers between devices with their start and end apart: 23, of which 11 were waited for; matrix products, arithmetic and copies ran while one was open for 7% of the time, Pallas kernels for 15%

profile of v2, /device:TPU:6, one launch (start us, length us, event | category | flops | bytes accessed | tf_op | source)
XLA Modules:
  0.0 141.2 jit_solution(16679184565990979970)
XLA Ops:
  0.0 0.7 select_reduce_fusion
  0.7 0.7 fusion.10
  1.4 0.1 copy.99.scale_ref
  1.6 1.6 %copy-done = bf16[256,4096]{1,0:T(8,128)(2,1)S(1)} copy-done((bf16[256,4096]{1,0:T(8,128)(2,1)S(1)}, bf16[256,4096]{1,0:T(8,128)(2,1)}, u32[]{:S(2)}) %copy-start) | copy-done | bytes 2097176
  3.2 0.7 copy-done.1
  3.9 8.6 %shard_map.640.own_ref = bf16[4096,256]{1,0:T(8,128)(2,1)S(1)} custom-call(s32[4096]{0:T(1024)S(1)} %copy-done.1, f32[256,1]{1,0:T(8,128)S(1)} %copy.99.scale_ref, bf16[256,4096]{1,0:T(8,128)(2,1)S(1)} %copy-done), custom_call_target="tpu_custom_call" | custom-call | bytes 16777216 | tf_op jit(solution)/shard_map/pallas_call | solution.py:107
  12.6 0.1 collective-permute-start
  13.0 0.1 reshape.113
  13.4 0.1 copy.102
  13.5 0.1 reshape.116
  13.6 0.1 copy.101
  13.7 0.1 reshape.115
  13.8 0.1 copy.100
  13.9 0.1 reshape.114
  14.0 0.1 copy.105
  14.1 0.1 reshape.119
  14.2 0.1 copy.104
  14.3 0.1 reshape.118
  14.7 2.3 %collective-permute-done.other_ref = bf16[4096,256]{1,0:T(8,128)(2,1)} collective-permute-done((bf16[4096,256]{1,0:T(8,128)(2,1)S(1)}, bf16[4096,256]{1,0:T(8,128)(2,1)}, u32[]{:S(2)}, u32[]{:S(2)}) %collective-permute-start) | collective-permute-done | bytes 2097184 | tf_op jit(solution)/shard_map/ppermute | solution.py:256
  17.0 8.1 %shard_map.642 = (bf16[8,176,256]{2,1,0:T(8,128)(2,1)}, bf16[8,176,256]{2,1,0:T(8,128)(2,1)}, bf16[1296,256]{1,0:T(8,128)(2,1)}) custom-call(s32[144]{0:T(256)S(1)} %get-tuple-element.106.table, bf16[4096,256]{1,0:T(8,128)(2,1)S(1)} %shard_map.640.own_ref, bf16[4096,256]{1,0:T(8,128)(2,1)} %collective-permute-done.other_ref), custom_call_target="tpu_custom_call" | custom-call | flops 1073741824 | bytes 8388608 | tf_op jit(solution)/shard_map/pallas_call | solution.py:203
  25.1 2.7 %collective-permute-start.13 = (bf16[1296,256]{1,0:T(8,128)(2,1)}, bf16[1296,256]{1,0:T(8,128)(2,1)}, u32[]{:S(2)}, u32[]{:S(2)}) collective-permute-start(bf16[1296,256]{1,0:T(8,128)(2,1)} %get-tuple-element.26), channel_id=1, source_target_pairs={{0,8},{1,25},{2,10},{3,27},{4,12},{5,29},{6,14},{7,31},{8,16},{9,1... | collective-permute-start | bytes 1990664 | tf_op jit(solution)/shard_map/ppermute | solution.py:254
  28.1 0.1 copy.96
  28.2 0.1 reshape.110
  28.3 0.1 copy.97
  28.4 0.1 reshape.111
  28.4 0.1 copy.98
  28.5 0.1 reshape.112
  28.7 0.8 collective-permute-start.5
  29.5 7.1 %shard_map.643 = (bf16[8,176,256]{2,1,0:T(8,128)(2,1)S(1)}, bf16[8,176,256]{2,1,0:T(8,128)(2,1)S(1)}, f32[1296,256]{1,0:T(8,128)S(1)}) custom-call(s32[144]{0:T(256)S(1)} %get-tuple-element.107.table, bf16[4096,256]{1,0:T(8,128)(2,1)S(1)} %shard_map.640.own_ref, bf16[4096,256]{1,0:T(8,128)(2,1)} %collective-permute-done.other_ref), custom_call_target="tpu_custom_call" | custom-call | flops 1073741824 | bytes 8388608 | tf_op jit(solution)/shard_map/pallas_call | solution.py:203
  36.7 2.5 %collective-permute-start.4 = (bf16[8,176,256]{2,1,0:T(8,128)(2,1)S(1)}, bf16[8,176,256]{2,1,0:T(8,128)(2,1)S(1)}, u32[]{:S(2)}, u32[]{:S(2)}) collective-permute-start(bf16[8,176,256]{2,1,0:T(8,128)(2,1)S(1)} %get-tuple-element.20), channel_id=1, source_target_pairs={{0,2},{1,33},{2,4},{3,35},{4,6},{5,37},{6,0},{7,39},{8,10},{9,41},... | collective-permute-start | bytes 2162696 | tf_op jit(solution)/shard_map/ppermute | solution.py:254
  39.1 3.2 %collective-permute-start.1 = (bf16[8,176,256]{2,1,0:T(8,128)(2,1)}, bf16[8,176,256]{2,1,0:T(8,128)(2,1)S(1)}, u32[]{:S(2)}, u32[]{:S(2)}) collective-permute-start(bf16[8,176,256]{2,1,0:T(8,128)(2,1)} %get-tuple-element.18), channel_id=1, source_target_pairs={{0,2},{1,33},{2,4},{3,35},{4,6},{5,37},{6,0},{7,39},{8,10},{9,41},... | collective-permute-start | bytes 2162696 | tf_op jit(solution)/shard_map/ppermute | solution.py:254
  42.4 13.4 %shard_map.641 = (f32[8,176,256]{2,1,0:T(8,128)S(1)}, f32[8,176,256]{2,1,0:T(8,128)S(1)}, f32[1296,256]{1,0:T(8,128)S(1)}, f32[16,176,256]{2,1,0:T(8,128)S(1)}, f32[1296,256]{1,0:T(8,128)S(1)}) custom-call(s32[272]{0:T(512)S(1)} %concatenate.32.table, bf16[4096,256]{1,0:T(8,128)(2,1)S(1)} %shard_map.640.own_ref, bf16[4096,256]{1,0:T(8,128)(2,1)} %collective-permute-done.other_ref), custom_call_target="tpu_custom_call" | custom-call | flops 2147483648 | bytes 8388608 | tf_op jit(solution)/shard_map/pallas_call | solution.py:203
  55.8 1.2 add_convert_fusion.4
  57.1 0.8 collective-permute-start.14
  57.8 0.2 add_convert_fusion.1
  58.1 0.2 add_convert_fusion.2
  58.4 3.3 %collective-permute-start.2 = (bf16[8,176,256]{2,1,0:T(8,128)(2,1)S(1)}, bf16[8,176,256]{2,1,0:T(8,128)(2,1)S(1)}, u32[]{:S(2)}, u32[]{:S(2)}) collective-permute-start(bf16[8,176,256]{2,1,0:T(8,128)(2,1)S(1)} %add_convert_fusion.2), channel_id=1, source_target_pairs={{0,2},{1,33},{2,4},{3,35},{4,6},{5,37},{6,0},{7,39},{8,10},{9,41},... | collective-permute-start | bytes 2162696 | tf_op jit(solution)/shard_map/ppermute | solution.py:254
  61.6 7.4 %collective-permute-done.14 = bf16[1296,256]{1,0:T(8,128)(2,1)S(1)} collective-permute-done((bf16[1296,256]{1,0:T(8,128)(2,1)S(1)}, bf16[1296,256]{1,0:T(8,128)(2,1)S(1)}, u32[]{:S(2)}, u32[]{:S(2)}) %collective-permute-start.14) | collective-permute-done | bytes 663584 | tf_op jit(solution)/shard_map/ppermute | solution.py:254
  69.0 1.1 add_convert_fusion.3
  70.1 0.5 collective-permute-done.6
  70.6 0.6 add_convert_fusion
  71.2 0.9 fusion.97
  72.1 5.1 %collective-permute-start.9 = (bf16[4,176,256]{2,1,0:T(8,128)(2,1)}, bf16[4,176,256]{2,1,0:T(8,128)(2,1)S(1)}, u32[]{:S(2)}, u32[]{:S(2)}) collective-permute-start(bf16[4,176,256]{2,1,0:T(8,128)(2,1)} %get-tuple-element.84), channel_id=1, source_target_pairs={{0,96},{1,25},{2,98},{3,27},{4,100},{5,29},{6,102},{7,31},{8,104},... | collective-permute-start | bytes 1081352 | tf_op jit(solution)/shard_map/ppermute | solution.py:254
  77.2 0.8 slice.211
  78.0 1.5 %collective-permute-start.7 = (bf16[4,176,256]{2,1,0:T(8,128)(2,1)}, bf16[4,176,256]{2,1,0:T(8,128)(2,1)}, u32[]{:S(2)}, u32[]{:S(2)}) collective-permute-start(bf16[4,176,256]{2,1,0:T(8,128)(2,1)} %get-tuple-element.83), channel_id=1, source_target_pairs={{0,64},{1,17},{2,66},{3,19},{4,68},{5,21},{6,70},{7,23},{8,72},{9,... | collective-permute-start | bytes 1081352 | tf_op jit(solution)/shard_map/ppermute | solution.py:254
  79.5 3.0 %collective-permute-done.9 = bf16[4,176,256]{2,1,0:T(8,128)(2,1)S(1)} collective-permute-done((bf16[4,176,256]{2,1,0:T(8,128)(2,1)}, bf16[4,176,256]{2,1,0:T(8,128)(2,1)S(1)}, u32[]{:S(2)}, u32[]{:S(2)}) %collective-permute-start.9) | collective-permute-done | bytes 360480 | tf_op jit(solution)/shard_map/ppermute | solution.py:254
  82.5 8.3 %collective-permute-done.8 = bf16[4,176,256]{2,1,0:T(8,128)(2,1)} collective-permute-done((bf16[4,176,256]{2,1,0:T(8,128)(2,1)}, bf16[4,176,256]{2,1,0:T(8,128)(2,1)}, u32[]{:S(2)}, u32[]{:S(2)}) %collective-permute-start.8) | collective-permute-done | bytes 360480 | tf_op jit(solution)/shard_map/ppermute | solution.py:254
  90.8 1.2 fusion.1
  92.1 1.3 fusion.83
  93.6 3.6 %collective-permute-start.17 = (bf16[336,256]{1,0:T(8,128)(2,1)S(1)}, bf16[336,256]{1,0:T(8,128)(2,1)S(1)}, u32[]{:S(2)}, u32[]{:S(2)}) collective-permute-start(bf16[336,256]{1,0:T(8,128)(2,1)S(1)} %get-tuple-element.94), channel_id=1, source_target_pairs={{0,2},{1,7},{2,4},{3,1},{4,6},{5,3},{6,0},{7,5},{8,10},{9,15},{10,... | collective-permute-start | bytes 516104 | tf_op jit(solution)/shard_map/ppermute | solution.py:254
  97.2 1.5 %collective-permute-start.16 = (bf16[336,256]{1,0:T(8,128)(2,1)S(1)}, bf16[336,256]{1,0:T(8,128)(2,1)S(1)}, u32[]{:S(2)}, u32[]{:S(2)}) collective-permute-start(bf16[336,256]{1,0:T(8,128)(2,1)S(1)} %get-tuple-element.93), channel_id=1, source_target_pairs={{0,4},{1,5},{2,6},{3,7},{4,0},{5,1},{6,2},{7,3},{8,12},{9,13},{10,... | collective-permute-start | bytes 516104 | tf_op jit(solution)/shard_map/ppermute | solution.py:254
  98.7 2.6 %collective-permute-start.12 = (f32[176,256]{1,0:T(8,128)S(1)}, f32[176,256]{1,0:T(8,128)S(1)}, u32[]{:S(2)}, u32[]{:S(2)}) collective-permute-start(f32[176,256]{1,0:T(8,128)S(1)} %get-tuple-element.81), channel_id=1, source_target_pairs={{0,24},{1,7},{2,26},{3,1},{4,28},{5,3},{6,30},{7,5},{8,0},{9,15},{... | collective-permute-start | bytes 540680 | tf_op jit(solution)/shard_map/ppermute | solution.py:254
  101.3 3.2 %collective-permute-done.18 = bf16[336,256]{1,0:T(8,128)(2,1)S(1)} collective-permute-done((bf16[336,256]{1,0:T(8,128)(2,1)S(1)}, bf16[336,256]{1,0:T(8,128)(2,1)S(1)}, u32[]{:S(2)}, u32[]{:S(2)}) %collective-permute-start.18) | collective-permute-done | bytes 172064 | tf_op jit(solution)/shard_map/ppermute | solution.py:254
  104.5 0.6 collective-permute-start.10
  105.2 1.2 collective-permute-done.17
  106.4 1.1 collective-permute-done.16
  107.6 0.1 slice_add_fusion.1
  107.7 3.3 %collective-permute-start.21 = (f32[88,256]{1,0:T(8,128)S(1)}, f32[88,256]{1,0:T(8,128)S(1)}, u32[]{:S(2)}, u32[]{:S(2)}) collective-permute-start(f32[88,256]{1,0:T(8,128)S(1)} %get-tuple-element.91), channel_id=1, source_target_pairs={{0,96},{1,33},{2,98},{3,35},{4,100},{5,37},{6,102},{7,39},{8,104},... | collective-permute-start | bytes 270344 | tf_op jit(solution)/shard_map/ppermute | solution.py:254
  111.0 1.5 %collective-permute-start.19 = (f32[88,256]{1,0:T(8,128)S(1)}, f32[88,256]{1,0:T(8,128)S(1)}, u32[]{:S(2)}, u32[]{:S(2)}) collective-permute-start(f32[88,256]{1,0:T(8,128)S(1)} %get-tuple-element.90), channel_id=1, source_target_pairs={{0,64},{1,65},{2,66},{3,67},{4,68},{5,69},{6,70},{7,71},{8,72},{9,... | collective-permute-start | bytes 270344 | tf_op jit(solution)/shard_map/ppermute | solution.py:254
  112.6 0.7 collective-permute-done.21
  113.3 4.4 %collective-permute-done.20 = f32[88,256]{1,0:T(8,128)S(1)} collective-permute-done((f32[88,256]{1,0:T(8,128)S(1)}, f32[88,256]{1,0:T(8,128)S(1)}, u32[]{:S(2)}, u32[]{:S(2)}) %collective-permute-start.20) | collective-permute-done | bytes 90144 | tf_op jit(solution)/shard_map/ppermute | solution.py:254
  117.8 4.0 %collective-permute-start.22 = (f32[256,256]{1,0:T(8,128)S(1)}, f32[256,256]{1,0:T(8,128)S(1)}, u32[]{:S(2)}, u32[]{:S(2)}) collective-permute-start(f32[256,256]{1,0:T(8,128)S(1)} %pad_maximum_fusion), channel_id=1, source_target_pairs={{0,8},{1,16},{2,32},{3,48},{4,64},{5,80},{6,96},{7,112},{8,0},{9,2... | collective-permute-start | bytes 786440 | tf_op jit(solution)/shard_map/ppermute | solution.py:254
  121.9 17.7 %collective-permute-done.22.refs_3_ = f32[256,256]{1,0:T(8,128)S(1)} collective-permute-done((f32[256,256]{1,0:T(8,128)S(1)}, f32[256,256]{1,0:T(8,128)S(1)}, u32[]{:S(2)}, u32[]{:S(2)}) %collective-permute-start.22) | collective-permute-done | bytes 262176 | tf_op jit(solution)/shard_map/ppermute | solution.py:254
  139.6 1.6 %shard_map.644 = f32[256,512]{1,0:T(8,128)} custom-call(s32[2]{0:T(128)S(1)} %pad_add_fusion.13.refs_0_, f32[176,256]{1,0:T(8,128)S(1)} %fusion.4.refs_1_, f32[80,256]{1,0:T(8,128)S(1)} %slice_add_fusion.4.refs_2_, f32[256,256]{1,0:T(8,128)S(1)} %collective-permute-done.22.refs_3_, f32[8,256]{1,0:T(8,128)S(1)} %slice_add_fusion.7.refs_4_), custom_call_target="tpu_custom_call" | custom-call | tf_op jit(solution)/shard_map/pallas_call | solution.py:334
  (89 shorter events, 1.8 us)
Async XLA Ops:
  1.6 1.6 %copy-start = (bf16[256,4096]{1,0:T(8,128)(2,1)S(1)}, bf16[256,4096]{1,0:T(8,128)(2,1)}, u32[]{:S(2)}) copy-start(bf16[256,4096]{1,0:T(8,128)(2,1)} %design_ref.1) | copy-start | bytes 6291460
  3.2 0.7 copy-start.1
  3.9 8.9 %copy-start.5 = (s32[16]{0:T(128)S(1)}, s32[16]{0:T(128)}, u32[]{:S(2)}) copy-start(s32[16]{0:T(128)} %constant.450.clone) | copy-start | bytes 196
  3.9 8.9 %copy-start.6 = (s32[16]{0:T(128)S(1)}, s32[16]{0:T(128)}, u32[]{:S(2)}) copy-start(s32[16]{0:T(128)} %constant.446.clone) | copy-start | bytes 196
  3.9 8.9 %copy-start.7 = (s32[16]{0:T(128)S(1)}, s32[16]{0:T(128)}, u32[]{:S(2)}) copy-start(s32[16]{0:T(128)} %constant.447.clone) | copy-start | bytes 196
  3.9 9.2 %copy-start.2 = (s32[8]{0:T(128)S(1)}, s32[8]{0:T(128)}, u32[]{:S(2)}) copy-start(s32[8]{0:T(128)} %constant.442.clone) | copy-start | bytes 100
  3.9 9.2 %copy-start.3 = (s32[8]{0:T(128)S(1)}, s32[8]{0:T(128)}, u32[]{:S(2)}) copy-start(s32[8]{0:T(128)} %constant.444.clone) | copy-start | bytes 100
  3.9 9.2 %copy-start.4 = (s32[8]{0:T(128)S(1)}, s32[8]{0:T(128)}, u32[]{:S(2)}) copy-start(s32[8]{0:T(128)} %constant.445.clone) | copy-start | bytes 100
  3.9 9.3 %copy-start.8 = (s32[16]{0:T(128)S(1)}, s32[16]{0:T(128)}, u32[]{:S(2)}) copy-start(s32[16]{0:T(128)} %constant.451.clone) | copy-start | bytes 196
  12.6 4.4 %collective-permute-start = (bf16[4096,256]{1,0:T(8,128)(2,1)S(1)}, bf16[4096,256]{1,0:T(8,128)(2,1)}, u32[]{:S(2)}, u32[]{:S(2)}) collective-permute-start(bf16[4096,256]{1,0:T(8,128)(2,1)S(1)} %shard_map.640.own_ref), channel_id=1, source_target_pairs={{0,1},{1,0},{2,3},{3,2},{4,5},{5,4},{6,7},{7,6},{8,9},{9,8},{10,11... | collective-permute-start | bytes 6291464 | tf_op jit(solution)/shard_map/ppermute | solution.py:256
  25.1 30.8 %collective-permute-start.13 = (bf16[1296,256]{1,0:T(8,128)(2,1)}, bf16[1296,256]{1,0:T(8,128)(2,1)}, u32[]{:S(2)}, u32[]{:S(2)}) collective-permute-start(bf16[1296,256]{1,0:T(8,128)(2,1)} %get-tuple-element.26), channel_id=1, source_target_pairs={{0,8},{1,25},{2,10},{3,27},{4,12},{5,29},{6,14},{7,31},{8,16},{9,1... | collective-permute-start | bytes 1990664 | tf_op jit(solution)/shard_map/ppermute | solution.py:254
  28.7 29.1 %collective-permute-start.5 = (bf16[8,176,256]{2,1,0:T(8,128)(2,1)}, bf16[8,176,256]{2,1,0:T(8,128)(2,1)S(1)}, u32[]{:S(2)}, u32[]{:S(2)}) collective-permute-start(bf16[8,176,256]{2,1,0:T(8,128)(2,1)} %get-tuple-element.22), channel_id=1, source_target_pairs={{0,6},{1,97},{2,0},{3,99},{4,2},{5,101},{6,4},{7,103},{8,14},{9,10... | collective-permute-start | bytes 2162696 | tf_op jit(solution)/shard_map/ppermute | solution.py:254
  36.7 33.4 %collective-permute-start.4 = (bf16[8,176,256]{2,1,0:T(8,128)(2,1)S(1)}, bf16[8,176,256]{2,1,0:T(8,128)(2,1)S(1)}, u32[]{:S(2)}, u32[]{:S(2)}) collective-permute-start(bf16[8,176,256]{2,1,0:T(8,128)(2,1)S(1)} %get-tuple-element.20), channel_id=1, source_target_pairs={{0,2},{1,33},{2,4},{3,35},{4,6},{5,37},{6,0},{7,39},{8,10},{9,41},... | collective-permute-start | bytes 2162696 | tf_op jit(solution)/shard_map/ppermute | solution.py:254
  39.1 31.0 %collective-permute-start.3 = (bf16[8,176,256]{2,1,0:T(8,128)(2,1)S(1)}, bf16[8,176,256]{2,1,0:T(8,128)(2,1)S(1)}, u32[]{:S(2)}, u32[]{:S(2)}) collective-permute-start(bf16[8,176,256]{2,1,0:T(8,128)(2,1)S(1)} %get-tuple-element.19), channel_id=1, source_target_pairs={{0,6},{1,97},{2,0},{3,99},{4,2},{5,101},{6,4},{7,103},{8,14},{9,10... | collective-permute-start | bytes 2162696 | tf_op jit(solution)/shard_map/ppermute | solution.py:254
  39.1 19.0 %collective-permute-start.1 = (bf16[8,176,256]{2,1,0:T(8,128)(2,1)}, bf16[8,176,256]{2,1,0:T(8,128)(2,1)S(1)}, u32[]{:S(2)}, u32[]{:S(2)}) collective-permute-start(bf16[8,176,256]{2,1,0:T(8,128)(2,1)} %get-tuple-element.18), channel_id=1, source_target_pairs={{0,2},{1,33},{2,4},{3,35},{4,6},{5,37},{6,0},{7,39},{8,10},{9,41},... | collective-permute-start | bytes 2162696 | tf_op jit(solution)/shard_map/ppermute | solution.py:254
  57.1 12.0 %collective-permute-start.14 = (bf16[1296,256]{1,0:T(8,128)(2,1)S(1)}, bf16[1296,256]{1,0:T(8,128)(2,1)S(1)}, u32[]{:S(2)}, u32[]{:S(2)}) collective-permute-start(bf16[1296,256]{1,0:T(8,128)(2,1)S(1)} %add_convert_fusion.4), channel_id=1, source_target_pairs={{0,8},{1,25},{2,10},{3,27},{4,12},{5,29},{6,14},{7,31},{8,16},{9,1... | collective-permute-start | bytes 1990664 | tf_op jit(solution)/shard_map/ppermute | solution.py:254
  58.1 12.6 %collective-permute-start.6 = (bf16[8,176,256]{2,1,0:T(8,128)(2,1)S(1)}, bf16[8,176,256]{2,1,0:T(8,128)(2,1)S(1)}, u32[]{:S(2)}, u32[]{:S(2)}) collective-permute-start(bf16[8,176,256]{2,1,0:T(8,128)(2,1)S(1)} %add_convert_fusion.1), channel_id=1, source_target_pairs={{0,6},{1,97},{2,0},{3,99},{4,2},{5,101},{6,4},{7,103},{8,14},{9,10... | collective-permute-start | bytes 2162696 | tf_op jit(solution)/shard_map/ppermute | solution.py:254
  58.4 12.3 %collective-permute-start.2 = (bf16[8,176,256]{2,1,0:T(8,128)(2,1)S(1)}, bf16[8,176,256]{2,1,0:T(8,128)(2,1)S(1)}, u32[]{:S(2)}, u32[]{:S(2)}) collective-permute-start(bf16[8,176,256]{2,1,0:T(8,128)(2,1)S(1)} %add_convert_fusion.2), channel_id=1, source_target_pairs={{0,2},{1,33},{2,4},{3,35},{4,6},{5,37},{6,0},{7,39},{8,10},{9,41},... | collective-permute-start | bytes 2162696 | tf_op jit(solution)/shard_map/ppermute | solution.py:254
  70.1 22.0 %collective-permute-start.15 = (bf16[1296,256]{1,0:T(8,128)(2,1)}, bf16[1296,256]{1,0:T(8,128)(2,1)}, u32[]{:S(2)}, u32[]{:S(2)}) collective-permute-start(bf16[1296,256]{1,0:T(8,128)(2,1)} %add_convert_fusion.3), channel_id=1, source_target_pairs={{0,8},{1,25},{2,10},{3,27},{4,12},{5,29},{6,14},{7,31},{8,16},{9,1... | collective-permute-start | bytes 1990664 | tf_op jit(solution)/shard_map/ppermute | solution.py:254
  72.1 10.4 %collective-permute-start.9 = (bf16[4,176,256]{2,1,0:T(8,128)(2,1)}, bf16[4,176,256]{2,1,0:T(8,128)(2,1)S(1)}, u32[]{:S(2)}, u32[]{:S(2)}) collective-permute-start(bf16[4,176,256]{2,1,0:T(8,128)(2,1)} %get-tuple-element.84), channel_id=1, source_target_pairs={{0,96},{1,25},{2,98},{3,27},{4,100},{5,29},{6,102},{7,31},{8,104},... | collective-permute-start | bytes 1081352 | tf_op jit(solution)/shard_map/ppermute | solution.py:254
  78.0 12.8 %collective-permute-start.8 = (bf16[4,176,256]{2,1,0:T(8,128)(2,1)}, bf16[4,176,256]{2,1,0:T(8,128)(2,1)}, u32[]{:S(2)}, u32[]{:S(2)}) collective-permute-start(bf16[4,176,256]{2,1,0:T(8,128)(2,1)} %slice.211), channel_id=1, source_target_pairs={{0,32},{1,9},{2,34},{3,11},{4,36},{5,13},{6,38},{7,15},{8,40},{9,1... | collective-permute-start | bytes 1081352 | tf_op jit(solution)/shard_map/ppermute | solution.py:254
  78.0 12.8 %collective-permute-start.7 = (bf16[4,176,256]{2,1,0:T(8,128)(2,1)}, bf16[4,176,256]{2,1,0:T(8,128)(2,1)}, u32[]{:S(2)}, u32[]{:S(2)}) collective-permute-start(bf16[4,176,256]{2,1,0:T(8,128)(2,1)} %get-tuple-element.83), channel_id=1, source_target_pairs={{0,64},{1,17},{2,66},{3,19},{4,68},{5,21},{6,70},{7,23},{8,72},{9,... | collective-permute-start | bytes 1081352 | tf_op jit(solution)/shard_map/ppermute | solution.py:254
  93.4 11.1 %collective-permute-start.18 = (bf16[336,256]{1,0:T(8,128)(2,1)S(1)}, bf16[336,256]{1,0:T(8,128)(2,1)S(1)}, u32[]{:S(2)}, u32[]{:S(2)}) collective-permute-start(bf16[336,256]{1,0:T(8,128)(2,1)S(1)} %concatenate.42), channel_id=1, source_target_pairs={{0,6},{1,3},{2,0},{3,5},{4,2},{5,7},{6,4},{7,1},{8,14},{9,11},{10,... | collective-permute-start | bytes 516104 | tf_op jit(solution)/shard_map/ppermute | solution.py:254
  93.6 12.8 %collective-permute-start.17 = (bf16[336,256]{1,0:T(8,128)(2,1)S(1)}, bf16[336,256]{1,0:T(8,128)(2,1)S(1)}, u32[]{:S(2)}, u32[]{:S(2)}) collective-permute-start(bf16[336,256]{1,0:T(8,128)(2,1)S(1)} %get-tuple-element.94), channel_id=1, source_target_pairs={{0,2},{1,7},{2,4},{3,1},{4,6},{5,3},{6,0},{7,5},{8,10},{9,15},{10,... | collective-permute-start | bytes 516104 | tf_op jit(solution)/shard_map/ppermute | solution.py:254
  97.2 10.4 %collective-permute-start.16 = (bf16[336,256]{1,0:T(8,128)(2,1)S(1)}, bf16[336,256]{1,0:T(8,128)(2,1)S(1)}, u32[]{:S(2)}, u32[]{:S(2)}) collective-permute-start(bf16[336,256]{1,0:T(8,128)(2,1)S(1)} %get-tuple-element.93), channel_id=1, source_target_pairs={{0,4},{1,5},{2,6},{3,7},{4,0},{5,1},{6,2},{7,3},{8,12},{9,13},{10,... | collective-permute-start | bytes 516104 | tf_op jit(solution)/shard_map/ppermute | solution.py:254
  98.7 12.3 %collective-permute-start.12 = (f32[176,256]{1,0:T(8,128)S(1)}, f32[176,256]{1,0:T(8,128)S(1)}, u32[]{:S(2)}, u32[]{:S(2)}) collective-permute-start(f32[176,256]{1,0:T(8,128)S(1)} %get-tuple-element.81), channel_id=1, source_target_pairs={{0,24},{1,7},{2,26},{3,1},{4,28},{5,3},{6,30},{7,5},{8,0},{9,15},{... | collective-permute-start | bytes 540680 | tf_op jit(solution)/shard_map/ppermute | solution.py:254
  101.3 11.3 %collective-permute-start.11 = (f32[176,256]{1,0:T(8,128)S(1)}, f32[176,256]{1,0:T(8,128)S(1)}, u32[]{:S(2)}, u32[]{:S(2)}) collective-permute-start(f32[176,256]{1,0:T(8,128)S(1)} %get-tuple-element.82), channel_id=1, source_target_pairs={{0,8},{1,3},{2,10},{3,5},{4,12},{5,7},{6,14},{7,1},{8,16},{9,11},{... | collective-permute-start | bytes 540680 | tf_op jit(solution)/shard_map/ppermute | solution.py:254
  104.5 8.1 %collective-permute-start.10 = (f32[176,256]{1,0:T(8,128)S(1)}, f32[176,256]{1,0:T(8,128)S(1)}, u32[]{:S(2)}, u32[]{:S(2)}) collective-permute-start(f32[176,256]{1,0:T(8,128)S(1)} %get-tuple-element.80), channel_id=1, source_target_pairs={{0,16},{1,5},{2,18},{3,7},{4,20},{5,1},{6,22},{7,3},{8,24},{9,13},... | collective-permute-start | bytes 540680 | tf_op jit(solution)/shard_map/ppermute | solution.py:254
  107.7 5.5 %collective-permute-start.21 = (f32[88,256]{1,0:T(8,128)S(1)}, f32[88,256]{1,0:T(8,128)S(1)}, u32[]{:S(2)}, u32[]{:S(2)}) collective-permute-start(f32[88,256]{1,0:T(8,128)S(1)} %get-tuple-element.91), channel_id=1, source_target_pairs={{0,96},{1,33},{2,98},{3,35},{4,100},{5,37},{6,102},{7,39},{8,104},... | collective-permute-start | bytes 270344 | tf_op jit(solution)/shard_map/ppermute | solution.py:254
  111.0 6.7 %collective-permute-start.20 = (f32[88,256]{1,0:T(8,128)S(1)}, f32[88,256]{1,0:T(8,128)S(1)}, u32[]{:S(2)}, u32[]{:S(2)}) collective-permute-start(f32[88,256]{1,0:T(8,128)S(1)} %get-tuple-element.92), channel_id=1, source_target_pairs={{0,32},{1,97},{2,34},{3,99},{4,36},{5,101},{6,38},{7,103},{8,40},{... | collective-permute-start | bytes 270344 | tf_op jit(solution)/shard_map/ppermute | solution.py:254
  111.0 6.7 %collective-permute-start.19 = (f32[88,256]{1,0:T(8,128)S(1)}, f32[88,256]{1,0:T(8,128)S(1)}, u32[]{:S(2)}, u32[]{:S(2)}) collective-permute-start(f32[88,256]{1,0:T(8,128)S(1)} %get-tuple-element.90), channel_id=1, source_target_pairs={{0,64},{1,65},{2,66},{3,67},{4,68},{5,69},{6,70},{7,71},{8,72},{9,... | collective-permute-start | bytes 270344 | tf_op jit(solution)/shard_map/ppermute | solution.py:254
  117.8 21.8 %collective-permute-start.22 = (f32[256,256]{1,0:T(8,128)S(1)}, f32[256,256]{1,0:T(8,128)S(1)}, u32[]{:S(2)}, u32[]{:S(2)}) collective-permute-start(f32[256,256]{1,0:T(8,128)S(1)} %pad_maximum_fusion), channel_id=1, source_target_pairs={{0,8},{1,16},{2,32},{3,48},{4,64},{5,80},{6,96},{7,112},{8,0},{9,2... | collective-permute-start | bytes 786440 | tf_op jit(solution)/shard_map/ppermute | solution.py:254

commit v3 on v2

v3 whole, which is shorter than its diff:
```python
import functools

import jax
import jax.numpy as jnp
import numpy as np
from jax import lax
from jax.experimental import pallas as pl
from jax.experimental.pallas import tpu as pltpu
from jax.sharding import Mesh, PartitionSpec as P

ARC_ROWS = 32
AXES = ("z", "y", "x", "core")
BLK = 256
MAIN = 176
REST = BLK - MAIN
EXTRA = 16
BF = jnp.bfloat16
F32 = jnp.float32


def linear(z, y, x, q):
    return ((z % 4 * 4 + y % 4) * 4 + x % 4) * 2 + q


def shift_pairs(order0, order1, sign1, stage, step):
    pairs = []
    for z in range(4):
        for y in range(4):
            for x in range(4):
                for q in range(2):
                    axis = (order0, order1)[q][stage]
                    by = step * (1, sign1)[q]
                    to = {"z": z, "y": y, "x": x}
                    to[axis] += by
                    pairs.append((linear(z, y, x, q), linear(to["z"], to["y"], to["x"], q)))
    return pairs


def mirror_pairs():
    pairs = []
    for z in range(4):
        for y in range(4):
            for x in range(4):
                for q in range(2):
                    r, c = 4 * z + y, 2 * x + q
                    i, h = r // 2, r % 2
                    if i < c:
                        to_r, to_c = 2 * c + h, i
                    elif i > c:
                        to_r, to_c = 2 * c + 1 - h, i
                    else:
                        to_r, to_c = 2 * i + 1 - h, i
                    to = linear(to_r // 4, to_r % 4, to_c // 2, to_c % 2)
                    pairs.append((linear(z, y, x, q), to))
    return pairs


MAIN_ORDER = (("x", "z", "y"), ("z", "y", "x"), 1)
REST_ORDER = (("y", "x", "z"), ("y", "x", "z"), -1)


def block_table(order, offsets):
    order0, order1, sign1 = order
    rows = []
    for device in range(128):
        place = {"z": device // 32, "y": device // 8 % 4, "x": device // 2 % 4}
        core = device % 2
        for d in offsets:
            at = dict(place)
            for name, by in zip((order0, order1)[core], d):
                at[name] = (place[name] + by * (1, sign1)[core]) % 4
            r, c = 4 * at["z"] + at["y"], 2 * at["x"] + core
            i, h = r // 2, r % 2
            s = h if i <= c else 1 - h
            rows += [r, 2 * c + s, 2 * c + 1 - s, int(i == c)]
    return np.asarray(rows, np.int32).reshape(128, -1)


def cross_table():
    rows = []
    for device in range(128):
        x, core = device // 2 % 4, device % 2
        for d in range(4):
            first = 2 * (2 * ((x + d * (1, REST_ORDER[2])[core]) % 4) + core)
            rows += [first, first + 1, 0, 0]
    return np.asarray(rows, np.int32).reshape(128, -1)


def gather_kernel(map_ref, counts_ref, weight_ref, design_ref, out_ref, held, turned, picked, sems):
    width, half = held.shape[0], held.shape[0] // 2
    tiles, unroll, loads = held.shape[1] // width, 32, sems.shape[0]
    copies = []
    for n in range(loads):
        part = pl.ds(n * (held.shape[1] // loads), held.shape[1] // loads)
        copies.append(pltpu.make_async_copy(design_ref.at[:, part], held.at[:, part], sems.at[n]))
        copies[-1].start()

    slot = lax.broadcasted_iota(jnp.int32, (1, width), 1)
    count = jnp.zeros((1, width), jnp.int32)
    for arc in range(width // ARC_ROWS):
        count = jnp.where(slot // ARC_ROWS == arc, counts_ref[arc], count)
    weight = weight_ref[...]
    scale = jnp.sqrt(jnp.where(slot % ARC_ROWS < count, weight, jnp.zeros_like(weight)))

    for n in range(loads):
        copies[n].wait()

        @pl.loop(n * (tiles // loads), (n + 1) * (tiles // loads))
        def _(t):
            at = pl.multiple_of(t * width, width)
            wide = (held[:, pl.ds(at, width)].T.astype(F32) * scale).astype(BF).astype(F32)
            for h in range(2):
                turned[pl.ds(2 * at + h, width, 2), :] = wide[:, h * half : (h + 1) * half]

    @pl.loop(0, out_ref.shape[0] // unroll)
    def _(g):
        rows = [turned[pl.ds(2 * map_ref[g * unroll + u], 2), :] for u in range(unroll)]
        for u in range(unroll):
            picked[pl.ds(2 * (g * unroll + u), 2), :] = rows[u]

    @pl.loop(0, tiles)
    def _(t):
        at = pl.multiple_of(t * width, width)
        for h in range(2):
            out_ref[pl.ds(at, width), pl.ds(h * half, half)] = picked[
                pl.ds(2 * at + h, width, 2), :
            ].astype(BF)


def scaled_rows(column_map, counts, weight, design):
    rows, unknowns = design.shape
    vmem, smem = pl.BlockSpec(memory_space=pltpu.VMEM), pl.BlockSpec(memory_space=pltpu.SMEM)
    return pl.pallas_call(
        gather_kernel,
        out_shape=jax.ShapeDtypeStruct((unknowns, rows), BF),
        in_specs=[smem, smem, vmem, pl.BlockSpec(memory_space=pl.ANY)],
        out_specs=vmem,
        scratch_shapes=[
            pltpu.VMEM((rows, unknowns), BF),
            pltpu.VMEM((2 * unknowns, rows // 2), F32),
            pltpu.VMEM((2 * unknowns, rows // 2), F32),
            pltpu.SemaphoreType.DMA((4,)),
        ],
        compiler_params=pltpu.CompilerParams(vmem_limit_bytes=60 * 1024 * 1024),
        cost_estimate=pl.CostEstimate(flops=0, bytes_accessed=16 << 20, transcendentals=0),
    )(column_map, counts, weight[None, :], design)


def turn_kernel(rows_ref, out_ref):
    @pl.loop(0, rows_ref.shape[0] // BLK)
    def _(t):
        at = pl.multiple_of(t * BLK, BLK)
        out_ref[:, pl.ds(at, BLK)] = rows_ref[pl.ds(at, BLK), :].T


def turned_rows(rows):
    vmem = pl.BlockSpec(memory_space=pltpu.VMEM)
    return pl.pallas_call(
        turn_kernel,
        out_shape=jax.ShapeDtypeStruct(rows.shape[::-1], rows.dtype),
        in_specs=[vmem],
        out_specs=vmem,
        compiler_params=pltpu.CompilerParams(vmem_limit_bytes=12 * 1024 * 1024),
        cost_estimate=pl.CostEstimate(flops=0, bytes_accessed=4 << 20, transcendentals=0),
    )(rows)


def product_kernel(plan, table, *refs):
    if len(refs) > 2 + len(plan):
        own_ref, other_ref, own_turned_ref, *outs, held, turned, sems = refs
        deep = own_ref.shape[1]
        copies = [
            pltpu.make_async_copy(other_ref, held.at[:, pl.ds(deep, deep)], sems.at[0]),
            pltpu.make_async_copy(own_ref, held.at[:, pl.ds(0, deep)], sems.at[1]),
            pltpu.make_async_copy(own_turned_ref, turned.at[pl.ds(0, deep), :], sems.at[2]),
        ]
        for copy in copies:
            copy.start()
        copies[0].wait()

        @pl.loop(0, held.shape[0] // BLK)
        def _(t):
            at = pl.multiple_of(t * BLK, BLK)
            turned[pl.ds(deep, deep), pl.ds(at, BLK)] = held[pl.ds(at, BLK), pl.ds(deep, deep)].T

        copies[1].wait()
        copies[2].wait()
    else:
        held, turned, *outs = refs

    def dot(rows_at, rows, cols_at):
        return jnp.dot(
            held[pl.ds(rows_at, rows), :], turned[:, pl.ds(cols_at, BLK)], preferred_element_type=F32
        )

    i = lax.broadcasted_iota(jnp.int32, (BLK, BLK), 0)
    j = lax.broadcasted_iota(jnp.int32, (BLK, BLK), 1)
    if any(ring for _, _, _, _, ring in plan):
        lines = []
        for e in range(4):
            at = 4 * e
            cross = dot(pl.multiple_of(table[at] * BLK, BLK), BLK, pl.multiple_of(table[at + 1] * BLK, BLK))
            lines.append(jnp.sum(jnp.where(i == j, cross, 0.0), axis=0, keepdims=True))
        lines = jnp.concatenate(lines + [jnp.zeros((EXTRA - 4, BLK), F32)], axis=0)

    for out, (first, count, row0, rows, ring) in zip(outs, plan):

        def put(o, value, out=out, rows=rows, ring=ring):
            if ring:
                out[pl.ds(pl.multiple_of(o * rows, 16), rows), :] = value.astype(out.dtype)
            else:
                out[o] = value.astype(out.dtype)

        batch = 8 if count % 8 == 0 else 4

        @pl.loop(0, count // batch)
        def _(g, batch=batch, first=first, row0=row0, rows=rows, put=put, out=out):
            starts, values = [], []
            for u in range(batch):
                at = 4 * (first + g * batch + u)
                rows_at = pl.multiple_of(table[at] * BLK + row0, 16)
                starts.append(rows_at)
                value = dot(rows_at, rows, pl.multiple_of(table[at + 1] * BLK, BLK))
                values.append(value.astype(out.dtype))
            for u in range(batch):
                put(g * batch + u, values[u])
            for u in range(batch):
                at = 4 * (first + g * batch + u)

                @pl.when(table[at + 3] == 1)
                def _(u=u, at=at):
                    cols_at = pl.multiple_of(table[at + 1] * BLK, BLK)
                    mixed_at = pl.multiple_of(table[at + 2] * BLK, BLK)
                    value = dot(starts[u], rows, cols_at)
                    mixed = dot(starts[u], rows, mixed_at)
                    low = i[:rows] + row0 >= j[:rows]
                    put(g * batch + u, jnp.where(low, value, mixed))

        if ring:
            out[pl.ds(count * rows, EXTRA), :] = lines.astype(out.dtype)


def products(operands, parts, tables, plan, grant):
    shapes = []
    for offsets, rows, kind, ring in parts:
        count = len(offsets)
        shape = (count * rows + EXTRA, BLK) if ring else (count, rows, BLK)
        shapes.append(jax.ShapeDtypeStruct(shape, kind))
    vmem, whole = pl.BlockSpec(memory_space=pltpu.VMEM), pl.BlockSpec(memory_space=pl.ANY)
    opening = len(operands) == 3
    if opening:
        unknowns, deep = operands[0].shape
        shapes += [jax.ShapeDtypeStruct((unknowns, 2 * deep), BF), jax.ShapeDtypeStruct((2 * deep, unknowns), BF)]
    return pl.pallas_call(
        functools.partial(product_kernel, plan),
        out_shape=shapes,
        in_specs=[pl.BlockSpec(memory_space=pltpu.SMEM)] + ([vmem, whole, vmem] if opening else [vmem] * 2),
        out_specs=[vmem] * len(shapes),
        scratch_shapes=[pltpu.SemaphoreType.DMA((3,))] if opening else [],
        compiler_params=pltpu.CompilerParams(vmem_limit_bytes=grant * 1024 * 1024),
        cost_estimate=pl.CostEstimate(flops=0, bytes_accessed=1 << 20, transcendentals=0),
    )(tables, *operands)


def finish_kernel(state, scale, main_ref, rest_ref, got_main_ref, got_rest_ref, cross_ref, out_ref):
    s, fold = state[0], state[1] == 1
    here = jnp.concatenate([main_ref[...], rest_ref[...]], axis=0)
    got = jnp.concatenate([got_main_ref[...].astype(F32), got_rest_ref[...].astype(F32)], axis=0).T
    mine = here.T
    i = lax.broadcasted_iota(jnp.int32, (BLK, BLK), 0)
    j = lax.broadcasted_iota(jnp.int32, (BLK, BLK), 1)
    on = jnp.logical_and(fold, i == j)
    low = jnp.logical_or(jnp.logical_not(fold), i >= j)
    first = jnp.where(low, here, mine) * scale
    second = jnp.where(on, cross_ref[0:1, :], jnp.where(low, got, here)) * scale

    @pl.when(s == 0)
    def _():
        out_ref[:, 0:BLK] = first
        out_ref[:, BLK : 2 * BLK] = second

    @pl.when(s == 1)
    def _():
        out_ref[:, BLK : 2 * BLK] = first
        out_ref[:, 0:BLK] = second


def local(design, weight, counts, column_map):
    rows_here = design.shape[0]
    core = lax.axis_index("core")
    place = {name: lax.axis_index(name) for name in ("z", "y", "x")}
    total_rows = rows_here * 128

    own = scaled_rows(column_map, counts, weight, design)

    def move(array, pairs):
        return lax.ppermute(array, AXES, pairs)

    other = lax.ppermute(own, "core", [(0, 1), (1, 0)])

    plus = [(a, b) for a in (0, 1) for b in range(4)]
    minus = [(a, b) for a in (2, 3) for b in range(4)]
    every = plus + minus

    def offs(d, rest):
        return [(d,) + p for p in rest]

    M, R = MAIN_ORDER, REST_ORDER
    calls = [
        [(M, offs(2, plus), BF), (M, offs(2, minus), BF), (R, offs(3, every), BF)],
        [(M, offs(1, minus), BF), (M, offs(3, plus), BF), (R, offs(2, every), F32)],
        [(M, offs(1, plus), F32), (M, offs(3, minus), F32), (R, offs(1, every), F32)]
        + [(M, offs(0, every[4 * d : 4 * d + 4]), F32) for d in range(4)]
        + [(R, offs(0, every), F32)],
    ]
    tables, first, made = [cross_table()], 4, []
    device = ((place["z"] * 4 + place["y"]) * 4 + place["x"]) * 2 + core
    plans = []
    for call in calls:
        plan = []
        for order, offsets, _ in call:
            tables.append(block_table(order, offsets))
            row0, rows = (0, MAIN) if order is M else (MAIN, REST)
            plan.append((first, len(offsets), row0, rows, order is R))
            first += len(offsets)
        plans.append(plan)
    table = lax.dynamic_index_in_dim(
        jnp.asarray(np.concatenate(tables, axis=1)), device, 0, keepdims=False
    )
    operands = (own, other, turned_rows(own))
    for call, plan, grant in zip(calls, plans, (18, 18, 24)):
        parts = [(offsets, rows, kind, ring) for (_, offsets, kind), (_, _, _, rows, ring) in zip(call, plan)]
        got = products(operands, parts, table, plan, grant)
        if len(operands) == 3:
            operands = got[len(parts) :]
        made.append(got[: len(parts)])
        if len(made) == 2:
            operands, made[1] = lax.optimization_barrier((operands, made[1]))
    first_p, first_m, ring = made[0]
    side_p, side_m, ring_2 = made[1]
    relay_p, relay_m, ring_1, *home, ring_0 = made[2]

    def main_to(stage, step):
        return shift_pairs(*M, stage, step)

    def rest_to(stage, step):
        return shift_pairs(*R, stage, step)

    got_1p = move(first_p, main_to(0, 1))
    got_1m = move(first_m, main_to(0, -1))
    got_r = move(ring, rest_to(0, 1))
    got_2p = move(side_p, main_to(0, 1))
    got_2m = move(side_m, main_to(0, -1))
    got_r = move((ring_2 + got_r.astype(F32)).astype(BF), rest_to(0, 1))
    got_3p = move((relay_p + got_1p.astype(F32)).astype(BF), main_to(0, 1))
    got_3m = move((relay_m + got_1m.astype(F32)).astype(BF), main_to(0, -1))
    got_r = move((ring_1 + got_r.astype(F32)).astype(BF), rest_to(0, 1))
    part = []
    for d in range(4):
        pair = (got_3p, got_2m) if d < 2 else (got_2p, got_3m)
        half = slice(4 * (d % 2), 4 * (d % 2) + 4)
        part.append(home[d] + pair[0][half].astype(F32) + pair[1][half].astype(F32))
    rest_sum = ring_0 + got_r.astype(F32)

    main_2 = part[0]
    for d in (2, 1, 3):
        main_2 = main_2 + move(part[d].astype(BF), main_to(1, d)).astype(F32)
    quarter = 4 * REST
    rest_2, cross = rest_sum[:quarter], rest_sum[4 * quarter : 4 * quarter + 1]
    tail = rest_sum[4 * quarter :]
    for d in (2, 1, 3):
        piece = jnp.concatenate([rest_sum[d * quarter : (d + 1) * quarter], tail], axis=0)
        piece = move(piece.astype(BF), rest_to(1, d)).astype(F32)
        rest_2 = rest_2 + piece[:quarter]
        cross = cross + piece[quarter + d : quarter + d + 1]

    main_3 = main_2[0]
    for d in (2, 1, 3):
        main_3 = main_3 + move(main_2[d], main_to(2, d))
    rest_3, extra = rest_2[:REST], jnp.broadcast_to(cross, (8, BLK))
    cross = extra
    for d in (2, 1, 3):
        piece = jnp.concatenate([rest_2[d * REST : (d + 1) * REST], extra], axis=0)
        piece = move(piece, rest_to(2, d))
        rest_3 = rest_3 + piece[:REST]
        cross = cross + piece[REST:]

    got_main = move(main_3.astype(BF), mirror_pairs())
    got_rest = move(rest_3.astype(BF), mirror_pairs())

    r, c = 4 * place["z"] + place["y"], 2 * place["x"] + core
    i, h = r // 2, r % 2
    s = jnp.where(i <= c, h, 1 - h)
    state = jnp.stack([s, (i == c).astype(jnp.int32)]).astype(jnp.int32)
    vmem = pl.BlockSpec(memory_space=pltpu.VMEM)
    return pl.pallas_call(
        lambda *refs: finish_kernel(refs[0], 1.0 / total_rows, *refs[1:]),
        out_shape=jax.ShapeDtypeStruct((BLK, 2 * BLK), F32),
        in_specs=[pl.BlockSpec(memory_space=pltpu.SMEM)] + [vmem] * 5,
        out_specs=vmem,
        compiler_params=pltpu.CompilerParams(vmem_limit_bytes=16 * 1024 * 1024),
    )(state, main_3, rest_3, got_main, got_rest, cross)


def solution(mesh):
    fine = Mesh(mesh.devices.reshape(4, 4, 4, 2), AXES)
    return jax.shard_map(
        local,
        mesh=fine,
        in_specs=(P(AXES, None), P(AXES), P(AXES), P()),
        out_specs=P(("z", "y"), ("x", "core")),
        check_vma=False,
    )
```

time: 142 us -> 113 us (0.80)
  waiting for transfers between devices: 49.9 us -> 35.2 us
  Pallas kernels: 38.8 us -> 32.8 us
  starting transfers between devices: 37.3 us -> 32.5 us
  other arithmetic: 8.2 us -> 6.74 us
    ppermute x22 -> x23, waiting for transfers between devices: 47.6 us -> 35.2 us  [move(): return lax.ppermute(array, AXES, pairs)]
    pallas_call x3 -> x4, Pallas kernels: 28.6 us -> 21.1 us  [the longest x3 19.7 us: products(): pl.pallas_call(functools.partial(product_kernel, plan), out_shape=shapes,...]
    ppermute x22 -> x23, starting transfers between devices: 37.2 us -> 32.5 us  [move(): return lax.ppermute(array, AXES, pairs)]
    ppermute x1, waiting for transfers between devices: 2.3 us -> 0.01 us  [local(): other = lax.ppermute(own, 'core', [(0, 1), (1, 0)])]
    unnamed x18 -> x8, local copies, waits for them, and re-layouts: 2.34 us -> 4.55 us
    convert_element_type x0 -> x4, other arithmetic: none -> 2.09 us  [the longest x2 2.01 us: local(): main_2 = main_2 + move(part[d].astype(BF), main_to(1, d)).astype(F32)]
    slice x2 -> x0, local copies, waits for them, and re-layouts: 1.69 us -> none  [local(): part = [sum_p[0:4], sum_p[4:8], sum_m[0:4], sum_m[4:8]]]
    pallas_call x1, Pallas kernels: 8.64 us -> 10.1 us  [scaled_rows(): pl.pallas_call(gather_kernel, out_shape=jax.ShapeDtypeStruct((unknowns, r...]
  transfers between devices with their start and end apart: 23 -> 24, of which waited for: 11 -> 11; matrix products, arithmetic and copies ran while one was open for 7% -> 6% of each run, Pallas kernels for 15% -> 13%
where the time goes in v3:
time: 113 us
  waiting for transfers between devices  35.2 us (31%)
  Pallas kernels  32.8 us (29%)
  starting transfers between devices  32.5 us (29%)
  other arithmetic  6.74 us (6%)
  local copies, waits for them, and re-layouts  5.39 us (5%)
    ppermute x23, waiting for transfers between devices, move(): return lax.ppermute(array, AXES, pairs)  35.2 us
    ppermute x23, starting transfers between devices, move(): return lax.ppermute(array, AXES, pairs)  32.5 us
    pallas_call x3, Pallas kernels, products(): pl.pallas_call(functools.partial(product_kernel, plan), out_shape=shapes,...  19.7 us
    pallas_call x1, Pallas kernels, scaled_rows(): pl.pallas_call(gather_kernel, out_shape=jax.ShapeDtypeStruct((unknowns, r...  10.1 us
    unnamed x8, local copies, waits for them, and re-layouts  4.55 us
  transfers between devices with their start and end apart: 24, of which 11 were waited for; matrix products, arithmetic and copies ran while one was open for 6% of the time, Pallas kernels for 13%

profile of v3, /device:TPU:6, one launch (start us, length us, event | category | flops | bytes accessed | tf_op | source)
XLA Modules:
  0.0 112.9 jit_solution(2144290079990711053)
XLA Ops:
  0.0 10.1 %shard_map.55.rows_ref.refs_0_ = bf16[4096,256]{1,0:T(8,128)(2,1)} custom-call(s32[4096]{0:T(1024)} %map_ref.1, s32[8]{0:T(128)} %counts_ref.1, f32[1,256]{1,0:T(1,128)} %bitcast.21, bf16[256,4096]{1,0:T(8,128)(2,1)} %design_ref.1), custom_call_target="tpu_custom_call" | custom-call | bytes 16777216 | tf_op jit(solution)/shard_map/pallas_call | solution.py:133
  10.2 0.1 collective-permute-start
  10.3 1.6 %copy-done = bf16[4096,256]{1,0:T(8,128)(2,1)S(1)} copy-done((bf16[4096,256]{1,0:T(8,128)(2,1)S(1)}, bf16[4096,256]{1,0:T(8,128)(2,1)}, u32[]{:S(2)}) %copy-start) | copy-done | bytes 2097176
  11.8 1.4 %shard_map.56.refs_2_ = bf16[256,4096]{1,0:T(8,128)(2,1)S(1)} custom-call(bf16[4096,256]{1,0:T(8,128)(2,1)S(1)} %copy-done), custom_call_target="tpu_custom_call" | custom-call | bytes 4194304 | tf_op jit(solution)/shard_map/pallas_call | solution.py:158
  13.3 1.4 %copy-done.2 = bf16[256,4096]{1,0:T(8,128)(2,1)} copy-done((bf16[256,4096]{1,0:T(8,128)(2,1)}, bf16[256,4096]{1,0:T(8,128)(2,1)S(1)}, u32[]{:S(2)}) %copy-start.2) | copy-done | bytes 2097176
  14.7 0.7 dynamic-slice_reduce_fusion.table
  15.4 0.0 collective-permute-done.refs_1_
  15.4 1.6 %copy-done.3 = bf16[256,4096]{1,0:T(8,128)(2,1)S(1)} copy-done((bf16[256,4096]{1,0:T(8,128)(2,1)S(1)}, bf16[256,4096]{1,0:T(8,128)(2,1)}, u32[]{:S(2)}) %copy-start.3) | copy-done | bytes 2097176
  17.0 6.9 %shard_map.57 = (bf16[8,176,256]{2,1,0:T(8,128)(2,1)S(1)}, bf16[8,176,256]{2,1,0:T(8,128)(2,1)S(1)}, bf16[1296,256]{1,0:T(8,128)(2,1)S(1)}, bf16[4096,512]{1,0:T(8,128)(2,1)S(1)}, bf16[512,4096]{1,0:T(8,128)(2,1)S(1)}) custom-call(s32[528]{0:T(1024)S(1)} %dynamic-slice_reduce_fusion.table, bf16[4096,256]{1,0:T(8,128)(2,1)S(1)} %copy-done.1, ...), custom_call_target="tpu_custom_call" | custom-call | bytes 1048576 | tf_op jit(solution)/shard_map/pallas_call | solution.py:254
  23.9 0.4 collective-permute-start.1
  24.4 1.6 %collective-permute-start.5 = (bf16[8,176,256]{2,1,0:T(8,128)(2,1)S(1)}, bf16[8,176,256]{2,1,0:T(8,128)(2,1)S(1)}, u32[]{:S(2)}, u32[]{:S(2)}) collective-permute-start(bf16[8,176,256]{2,1,0:T(8,128)(2,1)S(1)} %get-tuple-element.40), channel_id=1, source_target_pairs={{0,6},{1,97},{2,0},{3,99},{4,2},{5,101},{6,4},{7,103},{8,14},{9,10... | collective-permute-start | bytes 2162696 | tf_op jit(solution)/shard_map/ppermute | solution.py:297
  26.0 2.5 %collective-permute-start.13 = (bf16[1296,256]{1,0:T(8,128)(2,1)S(1)}, bf16[1296,256]{1,0:T(8,128)(2,1)S(1)}, u32[]{:S(2)}, u32[]{:S(2)}) collective-permute-start(bf16[1296,256]{1,0:T(8,128)(2,1)S(1)} %get-tuple-element.46), channel_id=1, source_target_pairs={{0,8},{1,25},{2,10},{3,27},{4,12},{5,29},{6,14},{7,31},{8,16},{9,1... | collective-permute-start | bytes 1990664 | tf_op jit(solution)/shard_map/ppermute | solution.py:297
  28.5 3.4 %shard_map.58 = (bf16[8,176,256]{2,1,0:T(8,128)(2,1)S(1)}, bf16[8,176,256]{2,1,0:T(8,128)(2,1)S(1)}, f32[1296,256]{1,0:T(8,128)S(1)}) custom-call(s32[528]{0:T(1024)S(1)} %dynamic-slice_reduce_fusion.table, bf16[4096,512]{1,0:T(8,128)(2,1)S(1)} %get-tuple-element.31.refs_0_, bf16[512,4096]{1,0:T(8,128)(2,1)S(1)} %get-tuple-element.32.refs_1_), custom_call_target="tpu_custom_call" | custom-call | bytes 1048576 | tf_op jit(solution)/shard_map/pallas_call | solution.py:254
  31.9 2.1 %collective-permute-start.3 = (bf16[8,176,256]{2,1,0:T(8,128)(2,1)S(1)}, bf16[8,176,256]{2,1,0:T(8,128)(2,1)S(1)}, u32[]{:S(2)}, u32[]{:S(2)}) collective-permute-start(bf16[8,176,256]{2,1,0:T(8,128)(2,1)S(1)} %get-tuple-element.36), channel_id=1, source_target_pairs={{0,6},{1,97},{2,0},{3,99},{4,2},{5,101},{6,4},{7,103},{8,14},{9,10... | collective-permute-start | bytes 2162696 | tf_op jit(solution)/shard_map/ppermute | solution.py:297
  34.0 1.4 %collective-permute-start.4 = (bf16[8,176,256]{2,1,0:T(8,128)(2,1)S(1)}, bf16[8,176,256]{2,1,0:T(8,128)(2,1)S(1)}, u32[]{:S(2)}, u32[]{:S(2)}) collective-permute-start(bf16[8,176,256]{2,1,0:T(8,128)(2,1)S(1)} %get-tuple-element.38), channel_id=1, source_target_pairs={{0,2},{1,33},{2,4},{3,35},{4,6},{5,37},{6,0},{7,39},{8,10},{9,41},... | collective-permute-start | bytes 2162696 | tf_op jit(solution)/shard_map/ppermute | solution.py:297
  35.3 9.4 %shard_map.59 = (f32[8,176,256]{2,1,0:T(8,128)S(1)}, f32[8,176,256]{2,1,0:T(8,128)S(1)}, f32[1296,256]{1,0:T(8,128)S(1)}, f32[4,176,256]{2,1,0:T(8,128)S(1)}, f3...) custom-call(s32[528]{0:T(1024)S(1)} %dynamic-slice_reduce_fusion.tab, ...), custom_call_target="tpu_custom_call" | custom-call | bytes 1048576 | tf_op jit(solution)/shard_map/pallas_call | solution.py:254
  44.8 0.0 collective-permute-done.1
  44.8 0.2 add_convert_fusion.1
  45.0 0.5 collective-permute-start.2
  45.5 0.2 add_convert_fusion
  45.8 1.6 %collective-permute-start.6 = (bf16[8,176,256]{2,1,0:T(8,128)(2,1)S(1)}, bf16[8,176,256]{2,1,0:T(8,128)(2,1)S(1)}, u32[]{:S(2)}, u32[]{:S(2)}) collective-permute-start(bf16[8,176,256]{2,1,0:T(8,128)(2,1)S(1)} %add_convert_fusion), channel_id=1, source_target_pairs={{0,6},{1,97},{2,0},{3,99},{4,2},{5,101},{6,4},{7,103},{8,14},{9,10... | collective-permute-start | bytes 2162696 | tf_op jit(solution)/shard_map/ppermute | solution.py:297
  47.4 0.0 collective-permute-done.13
  47.4 0.2 add_convert_fusion.3
  47.6 0.8 collective-permute-start.14
  48.3 0.0 collective-permute-done.3
  48.3 8.0 %collective-permute-done.2 = bf16[8,176,256]{2,1,0:T(8,128)(2,1)S(1)} collective-permute-done((bf16[8,176,256]{2,1,0:T(8,128)(2,1)S(1)}, bf16[8,176,256]{2,1,0:T(8,128)(2,1)S(1)}, u32[]{:S(2)}, u32[]{:S(2)}) %collective-permute-start.2) | collective-permute-done | bytes 720928 | tf_op jit(solution)/shard_map/ppermute | solution.py:297
  56.4 0.9 add_convert_fusion.5
  57.2 1.9 %collective-permute-start.8 = (bf16[4,176,256]{2,1,0:T(8,128)(2,1)}, bf16[4,176,256]{2,1,0:T(8,128)(2,1)}, u32[]{:S(2)}, u32[]{:S(2)}) collective-permute-start(bf16[4,176,256]{2,1,0:T(8,128)(2,1)} %add_convert_fusion.5), channel_id=1, source_target_pairs={{0,32},{1,9},{2,34},{3,11},{4,36},{5,13},{6,38},{7,15},{8,40},{9,1... | collective-permute-start | bytes 1081352 | tf_op jit(solution)/shard_map/ppermute | solution.py:297
  59.1 0.0 collective-permute-done.4
  59.2 0.0 collective-permute-done.6
  59.2 1.2 %add_convert_fusion.6 = (bf16[4,176,256]{2,1,0:T(8,128)(2,1)}, bf16[4,176,256]{2,1,0:T(8,128)(2,1)}) fusion(f32[4,176,256]{2,1,0:T(8,128)S(1)} %get-tuple-element.37, bf16[8,176,256]{2,1,0:T(8,128)(2,1)S(1)} %collective-permute-done.6, bf16[8,176,256]{2,1,0:T(8,128)(2,1)S(1)} %collective-permute-done.4, f32[4,176,256]{2,1,0:T(8,128)S(1)} %get-tuple-element.42), kind=kLoop, calls=%fused_computation.8 | loop fusion | flops 1802240 | bytes 3604480 | tf_op jit(solution)/shard_map/convert_element_type | solution.py:367
  60.3 3.6 %collective-permute-start.7 = (bf16[4,176,256]{2,1,0:T(8,128)(2,1)}, bf16[4,176,256]{2,1,0:T(8,128)(2,1)}, u32[]{:S(2)}, u32[]{:S(2)}) collective-permute-start(bf16[4,176,256]{2,1,0:T(8,128)(2,1)} %get-tuple-element.53), channel_id=1, source_target_pairs={{0,64},{1,17},{2,66},{3,19},{4,68},{5,21},{6,70},{7,23},{8,72},{9,... | collective-permute-start | bytes 1081352 | tf_op jit(solution)/shard_map/ppermute | solution.py:297
  63.9 1.0 collective-permute-start.9
  64.9 1.1 add_convert_fusion.2
  65.9 0.7 collective-permute-start.15
  66.7 0.1 pad_add_fusion.refs_0_
  66.8 0.2 collective-permute-done.8
  67.0 5.3 %collective-permute-done.7 = bf16[4,176,256]{2,1,0:T(8,128)(2,1)} collective-permute-done((bf16[4,176,256]{2,1,0:T(8,128)(2,1)}, bf16[4,176,256]{2,1,0:T(8,128)(2,1)}, u32[]{:S(2)}, u32[]{:S(2)}) %collective-permute-start.7) | collective-permute-done | bytes 360480 | tf_op jit(solution)/shard_map/ppermute | solution.py:297
  72.3 1.7 %collective-permute-done.9 = bf16[4,176,256]{2,1,0:T(8,128)(2,1)} collective-permute-done((bf16[4,176,256]{2,1,0:T(8,128)(2,1)}, bf16[4,176,256]{2,1,0:T(8,128)(2,1)}, u32[]{:S(2)}, u32[]{:S(2)}) %collective-permute-start.9) | collective-permute-done | bytes 360480 | tf_op jit(solution)/shard_map/ppermute | solution.py:297
  74.0 1.4 %convert_add_fusion.1 = f32[4,176,256]{2,1,0:T(8,128)S(1)} fusion(bf16[4,176,256]{2,1,0:T(8,128)(2,1)} %collective-permute-done.9, bf16[4,176,256]{2,1,0:T(8,128)(2,1)} %collective-permute-done.8, bf16[4,176,256]{2,1,0:T(8,128)(2,1)} %collective-permute-done.7, f32[4,176,256]{2,1,0:T(8,128)S(1)} %get-tuple-element.33, ...), kind=kLoop, calls=%fused_computation.5 | loop fusion | flops 1802240 | bytes 3244032 | tf_op jit(solution)/shard_map/add | solution.py:367
  75.4 2.7 %collective-permute-done.15 = bf16[1296,256]{1,0:T(8,128)(2,1)} collective-permute-done((bf16[1296,256]{1,0:T(8,128)(2,1)}, bf16[1296,256]{1,0:T(8,128)(2,1)}, u32[]{:S(2)}, u32[]{:S(2)}) %collective-permute-start.15) | collective-permute-done | bytes 663584 | tf_op jit(solution)/shard_map/ppermute | solution.py:297
  78.1 1.3 %fusion.6 = (bf16[1296,256]{1,0:T(8,128)(2,1)S(1)}, f32[1296,256]{1,0:T(8,128)S(1)}) fusion(f32[1296,256]{1,0:T(8,128)S(1)} %get-tuple-element.43, bf16[1296,256]{1,0:T(8,128)(2,1)} %collective-permute-done.15), kind=kLoop, calls=%fused_computation.38 | loop fusion | flops 995328 | bytes 3981312 | tf_op jit(solution)/shard_map/convert.7
  79.5 1.0 collective-permute-start.16
  80.5 1.9 %collective-permute-start.17 = (bf16[336,256]{1,0:T(8,128)(2,1)S(1)}, bf16[336,256]{1,0:T(8,128)(2,1)S(1)}, u32[]{:S(2)}, u32[]{:S(2)}) collective-permute-start(bf16[336,256]{1,0:T(8,128)(2,1)S(1)} %get-tuple-element.67), channel_id=1, source_target_pairs={{0,2},{1,7},{2,4},{3,1},{4,6},{5,3},{6,0},{7,5},{8,10},{9,15},{10,... | collective-permute-start | bytes 516104 | tf_op jit(solution)/shard_map/ppermute | solution.py:297
  82.4 0.1 collective-permute-start.18
  82.6 0.4 collective-permute-start.10
  83.0 2.0 %collective-permute-start.12 = (f32[176,256]{1,0:T(8,128)S(1)}, f32[176,256]{1,0:T(8,128)S(1)}, u32[]{:S(2)}, u32[]{:S(2)}) collective-permute-start(f32[176,256]{1,0:T(8,128)S(1)} %get-tuple-element.56), channel_id=1, source_target_pairs={{0,24},{1,7},{2,26},{3,1},{4,28},{5,3},{6,30},{7,5},{8,0},{9,15},{... | collective-permute-start | bytes 540680 | tf_op jit(solution)/shard_map/ppermute | solution.py:297
  85.0 3.4 %collective-permute-done.16 = bf16[336,256]{1,0:T(8,128)(2,1)S(1)} collective-permute-done((bf16[336,256]{1,0:T(8,128)(2,1)S(1)}, bf16[336,256]{1,0:T(8,128)(2,1)S(1)}, u32[]{:S(2)}, u32[]{:S(2)}) %collective-permute-start.16) | collective-permute-done | bytes 172064 | tf_op jit(solution)/shard_map/ppermute | solution.py:297
  88.4 0.0 collective-permute-start.11
  88.4 2.6 %collective-permute-done.17 = bf16[336,256]{1,0:T(8,128)(2,1)S(1)} collective-permute-done((bf16[336,256]{1,0:T(8,128)(2,1)S(1)}, bf16[336,256]{1,0:T(8,128)(2,1)S(1)}, u32[]{:S(2)}, u32[]{:S(2)}) %collective-permute-start.17) | collective-permute-done | bytes 172064 | tf_op jit(solution)/shard_map/ppermute | solution.py:297
  91.0 1.1 collective-permute-done.18
  92.1 0.1 slice_add_fusion
  92.3 3.0 %collective-permute-start.19 = (f32[88,256]{1,0:T(8,128)S(1)}, f32[88,256]{1,0:T(8,128)S(1)}, u32[]{:S(2)}, u32[]{:S(2)}) collective-permute-start(f32[88,256]{1,0:T(8,128)S(1)} %get-tuple-element.63), channel_id=1, source_target_pairs={{0,64},{1,65},{2,66},{3,67},{4,68},{5,69},{6,70},{7,71},{8,72},{9,... | collective-permute-start | bytes 270344 | tf_op jit(solution)/shard_map/ppermute | solution.py:297
  95.3 2.0 %collective-permute-start.21 = (f32[88,256]{1,0:T(8,128)S(1)}, f32[88,256]{1,0:T(8,128)S(1)}, u32[]{:S(2)}, u32[]{:S(2)}) collective-permute-start(f32[88,256]{1,0:T(8,128)S(1)} %get-tuple-element.64), channel_id=1, source_target_pairs={{0,96},{1,33},{2,98},{3,35},{4,100},{5,37},{6,102},{7,39},{8,104},... | collective-permute-start | bytes 270344 | tf_op jit(solution)/shard_map/ppermute | solution.py:297
  97.3 0.0 collective-permute-done.10
  97.3 0.1 collective-permute-start.20
  97.3 0.0 collective-permute-done.12
  97.3 0.0 collective-permute-done.11
  97.4 3.5 %collective-permute-start.22 = (bf16[176,256]{1,0:T(8,128)(2,1)S(1)}, bf16[176,256]{1,0:T(8,128)(2,1)S(1)}, u32[]{:S(2)}, u32[]{:S(2)}) collective-permute-start(bf16[176,256]{1,0:T(8,128)(2,1)S(1)} %get-tuple-element.49), channel_id=1, source_target_pairs={{0,8},{1,16},{2,32},{3,48},{4,64},{5,80},{6,96},{7,112},{8,0},{9,2... | collective-permute-start | bytes 270344 | tf_op jit(solution)/shard_map/ppermute | solution.py:297
  100.9 2.1 %collective-permute-done.20 = f32[88,256]{1,0:T(8,128)S(1)} collective-permute-done((f32[88,256]{1,0:T(8,128)S(1)}, f32[88,256]{1,0:T(8,128)S(1)}, u32[]{:S(2)}, u32[]{:S(2)}) %collective-permute-start.20) | collective-permute-done | bytes 90144 | tf_op jit(solution)/shard_map/ppermute | solution.py:297
  103.1 0.3 collective-permute-start.23
  103.4 4.2 %collective-permute-done.22.refs_3_ = bf16[176,256]{1,0:T(8,128)(2,1)S(1)} collective-permute-done((bf16[176,256]{1,0:T(8,128)(2,1)S(1)}, bf16[176,256]{1,0:T(8,128)(2,1)S(1)}, u32[]{:S(2)}, u32[]{:S(2)}) %collective-permute-start.22) | collective-permute-done | bytes 90144 | tf_op jit(solution)/shard_map/ppermute | solution.py:297
  107.6 3.7 %collective-permute-done.23.refs_4_ = bf16[80,256]{1,0:T(8,128)(2,1)S(1)} collective-permute-done((bf16[80,256]{1,0:T(8,128)(2,1)S(1)}, bf16[80,256]{1,0:T(8,128)(2,1)S(1)}, u32[]{:S(2)}, u32[]{:S(2)}) %collective-permute-start.23) | collective-permute-done | bytes 40992 | tf_op jit(solution)/shard_map/ppermute | solution.py:297
  111.4 1.5 %shard_map.60 = f32[256,512]{1,0:T(8,128)} custom-call(s32[2]{0:T(128)S(1)} %pad_add_fusion.refs_0_, f32[176,256]{1,0:T(8,128)S(1)} %get-tuple-element.50.refs_1_, f32[80,256]{1,0:T(8,128)S(1)} %get-tuple-element.48.refs_2_, bf16[176,256]{1,0:T(8,128)(2,1)S(1)} %collective-permute-done.22.refs_3_, bf16[80,256]{1,0:T(8,128)(2,1)S(1)} %collective-permute-done.23.refs_4_, ...), custom_call_target="tpu_custom_call" | custom-call | tf_op jit(solution)/shard_map/pallas_call | solution.py:396
  (24 shorter events, 0.3 us)
Async XLA Ops:
  10.2 5.3 %collective-permute-start = (bf16[4096,256]{1,0:T(8,128)(2,1)}, bf16[4096,256]{1,0:T(8,128)(2,1)}, u32[]{:S(2)}, u32[]{:S(2)}) collective-permute-start(bf16[4096,256]{1,0:T(8,128)(2,1)} %shard_map.55.rows_ref.refs_0_), channel_id=1, source_target_pairs={{0,1},{1,0},{2,3},{3,2},{4,5},{5,4},{6,7},{7,6},{8,9},{9,8},{10,11... | collective-permute-start | bytes 6291464 | tf_op jit(solution)/shard_map/ppermute | solution.py:299
  10.2 1.6 %copy-start = (bf16[4096,256]{1,0:T(8,128)(2,1)S(1)}, bf16[4096,256]{1,0:T(8,128)(2,1)}, u32[]{:S(2)}) copy-start(bf16[4096,256]{1,0:T(8,128)(2,1)} %shard_map.55.rows_ref.refs_0_) | copy-start | bytes 6291460
  11.8 3.6 %copy-start.1 = (bf16[4096,256]{1,0:T(8,128)(2,1)S(1)}, bf16[4096,256]{1,0:T(8,128)(2,1)}, u32[]{:S(2)}) copy-start(bf16[4096,256]{1,0:T(8,128)(2,1)} %shard_map.55.rows_ref.refs_0_) | copy-start | bytes 6291460
  13.3 1.4 %copy-start.2 = (bf16[256,4096]{1,0:T(8,128)(2,1)}, bf16[256,4096]{1,0:T(8,128)(2,1)S(1)}, u32[]{:S(2)}) copy-start(bf16[256,4096]{1,0:T(8,128)(2,1)S(1)} %shard_map.56.refs_2_) | copy-start | bytes 6291460
  15.4 1.6 %copy-start.3 = (bf16[256,4096]{1,0:T(8,128)(2,1)S(1)}, bf16[256,4096]{1,0:T(8,128)(2,1)}, u32[]{:S(2)}) copy-start(bf16[256,4096]{1,0:T(8,128)(2,1)} %copy-done.2) | copy-start | bytes 6291460
  23.9 20.8 %collective-permute-start.1 = (bf16[8,176,256]{2,1,0:T(8,128)(2,1)S(1)}, bf16[8,176,256]{2,1,0:T(8,128)(2,1)S(1)}, u32[]{:S(2)}, u32[]{:S(2)}) collective-permute-start(bf16[8,176,256]{2,1,0:T(8,128)(2,1)S(1)} %get-tuple-element.35), channel_id=1, source_target_pairs={{0,2},{1,33},{2,4},{3,35},{4,6},{5,37},{6,0},{7,39},{8,10},{9,41},... | collective-permute-start | bytes 2162696 | tf_op jit(solution)/shard_map/ppermute | solution.py:297
  24.4 21.2 %collective-permute-start.5 = (bf16[8,176,256]{2,1,0:T(8,128)(2,1)S(1)}, bf16[8,176,256]{2,1,0:T(8,128)(2,1)S(1)}, u32[]{:S(2)}, u32[]{:S(2)}) collective-permute-start(bf16[8,176,256]{2,1,0:T(8,128)(2,1)S(1)} %get-tuple-element.40), channel_id=1, source_target_pairs={{0,6},{1,97},{2,0},{3,99},{4,2},{5,101},{6,4},{7,103},{8,14},{9,10... | collective-permute-start | bytes 2162696 | tf_op jit(solution)/shard_map/ppermute | solution.py:297
  26.0 21.4 %collective-permute-start.13 = (bf16[1296,256]{1,0:T(8,128)(2,1)S(1)}, bf16[1296,256]{1,0:T(8,128)(2,1)S(1)}, u32[]{:S(2)}, u32[]{:S(2)}) collective-permute-start(bf16[1296,256]{1,0:T(8,128)(2,1)S(1)} %get-tuple-element.46), channel_id=1, source_target_pairs={{0,8},{1,25},{2,10},{3,27},{4,12},{5,29},{6,14},{7,31},{8,16},{9,1... | collective-permute-start | bytes 1990664 | tf_op jit(solution)/shard_map/ppermute | solution.py:297
  31.9 16.5 %collective-permute-start.3 = (bf16[8,176,256]{2,1,0:T(8,128)(2,1)S(1)}, bf16[8,176,256]{2,1,0:T(8,128)(2,1)S(1)}, u32[]{:S(2)}, u32[]{:S(2)}) collective-permute-start(bf16[8,176,256]{2,1,0:T(8,128)(2,1)S(1)} %get-tuple-element.36), channel_id=1, source_target_pairs={{0,6},{1,97},{2,0},{3,99},{4,2},{5,101},{6,4},{7,103},{8,14},{9,10... | collective-permute-start | bytes 2162696 | tf_op jit(solution)/shard_map/ppermute | solution.py:297
  34.0 25.2 %collective-permute-start.4 = (bf16[8,176,256]{2,1,0:T(8,128)(2,1)S(1)}, bf16[8,176,256]{2,1,0:T(8,128)(2,1)S(1)}, u32[]{:S(2)}, u32[]{:S(2)}) collective-permute-start(bf16[8,176,256]{2,1,0:T(8,128)(2,1)S(1)} %get-tuple-element.38), channel_id=1, source_target_pairs={{0,2},{1,33},{2,4},{3,35},{4,6},{5,37},{6,0},{7,39},{8,10},{9,41},... | collective-permute-start | bytes 2162696 | tf_op jit(solution)/shard_map/ppermute | solution.py:297
  45.0 11.4 %collective-permute-start.2 = (bf16[8,176,256]{2,1,0:T(8,128)(2,1)S(1)}, bf16[8,176,256]{2,1,0:T(8,128)(2,1)S(1)}, u32[]{:S(2)}, u32[]{:S(2)}) collective-permute-start(bf16[8,176,256]{2,1,0:T(8,128)(2,1)S(1)} %add_convert_fusion.1), channel_id=1, source_target_pairs={{0,2},{1,33},{2,4},{3,35},{4,6},{5,37},{6,0},{7,39},{8,10},{9,41},... | collective-permute-start | bytes 2162696 | tf_op jit(solution)/shard_map/ppermute | solution.py:297
  45.8 13.4 %collective-permute-start.6 = (bf16[8,176,256]{2,1,0:T(8,128)(2,1)S(1)}, bf16[8,176,256]{2,1,0:T(8,128)(2,1)S(1)}, u32[]{:S(2)}, u32[]{:S(2)}) collective-permute-start(bf16[8,176,256]{2,1,0:T(8,128)(2,1)S(1)} %add_convert_fusion), channel_id=1, source_target_pairs={{0,6},{1,97},{2,0},{3,99},{4,2},{5,101},{6,4},{7,103},{8,14},{9,10... | collective-permute-start | bytes 2162696 | tf_op jit(solution)/shard_map/ppermute | solution.py:297
  47.6 17.3 %collective-permute-start.14 = (bf16[1296,256]{1,0:T(8,128)(2,1)S(1)}, bf16[1296,256]{1,0:T(8,128)(2,1)S(1)}, u32[]{:S(2)}, u32[]{:S(2)}) collective-permute-start(bf16[1296,256]{1,0:T(8,128)(2,1)S(1)} %add_convert_fusion.3), channel_id=1, source_target_pairs={{0,8},{1,25},{2,10},{3,27},{4,12},{5,29},{6,14},{7,31},{8,16},{9,1... | collective-permute-start | bytes 1990664 | tf_op jit(solution)/shard_map/ppermute | solution.py:297
  57.2 9.8 %collective-permute-start.8 = (bf16[4,176,256]{2,1,0:T(8,128)(2,1)}, bf16[4,176,256]{2,1,0:T(8,128)(2,1)}, u32[]{:S(2)}, u32[]{:S(2)}) collective-permute-start(bf16[4,176,256]{2,1,0:T(8,128)(2,1)} %add_convert_fusion.5), channel_id=1, source_target_pairs={{0,32},{1,9},{2,34},{3,11},{4,36},{5,13},{6,38},{7,15},{8,40},{9,1... | collective-permute-start | bytes 1081352 | tf_op jit(solution)/shard_map/ppermute | solution.py:297
  60.3 12.0 %collective-permute-start.7 = (bf16[4,176,256]{2,1,0:T(8,128)(2,1)}, bf16[4,176,256]{2,1,0:T(8,128)(2,1)}, u32[]{:S(2)}, u32[]{:S(2)}) collective-permute-start(bf16[4,176,256]{2,1,0:T(8,128)(2,1)} %get-tuple-element.53), channel_id=1, source_target_pairs={{0,64},{1,17},{2,66},{3,19},{4,68},{5,21},{6,70},{7,23},{8,72},{9,... | collective-permute-start | bytes 1081352 | tf_op jit(solution)/shard_map/ppermute | solution.py:297
  63.9 10.1 %collective-permute-start.9 = (bf16[4,176,256]{2,1,0:T(8,128)(2,1)}, bf16[4,176,256]{2,1,0:T(8,128)(2,1)}, u32[]{:S(2)}, u32[]{:S(2)}) collective-permute-start(bf16[4,176,256]{2,1,0:T(8,128)(2,1)} %get-tuple-element.54), channel_id=1, source_target_pairs={{0,96},{1,25},{2,98},{3,27},{4,100},{5,29},{6,102},{7,31},{8,104},... | collective-permute-start | bytes 1081352 | tf_op jit(solution)/shard_map/ppermute | solution.py:297
  65.9 12.2 %collective-permute-start.15 = (bf16[1296,256]{1,0:T(8,128)(2,1)}, bf16[1296,256]{1,0:T(8,128)(2,1)}, u32[]{:S(2)}, u32[]{:S(2)}) collective-permute-start(bf16[1296,256]{1,0:T(8,128)(2,1)} %add_convert_fusion.2), channel_id=1, source_target_pairs={{0,8},{1,25},{2,10},{3,27},{4,12},{5,29},{6,14},{7,31},{8,16},{9,1... | collective-permute-start | bytes 1990664 | tf_op jit(solution)/shard_map/ppermute | solution.py:297
  79.5 8.9 %collective-permute-start.16 = (bf16[336,256]{1,0:T(8,128)(2,1)S(1)}, bf16[336,256]{1,0:T(8,128)(2,1)S(1)}, u32[]{:S(2)}, u32[]{:S(2)}) collective-permute-start(bf16[336,256]{1,0:T(8,128)(2,1)S(1)} %get-tuple-element.66), channel_id=1, source_target_pairs={{0,4},{1,5},{2,6},{3,7},{4,0},{5,1},{6,2},{7,3},{8,12},{9,13},{10,... | collective-permute-start | bytes 516104 | tf_op jit(solution)/shard_map/ppermute | solution.py:297
  80.5 10.5 %collective-permute-start.17 = (bf16[336,256]{1,0:T(8,128)(2,1)S(1)}, bf16[336,256]{1,0:T(8,128)(2,1)S(1)}, u32[]{:S(2)}, u32[]{:S(2)}) collective-permute-start(bf16[336,256]{1,0:T(8,128)(2,1)S(1)} %get-tuple-element.67), channel_id=1, source_target_pairs={{0,2},{1,7},{2,4},{3,1},{4,6},{5,3},{6,0},{7,5},{8,10},{9,15},{10,... | collective-permute-start | bytes 516104 | tf_op jit(solution)/shard_map/ppermute | solution.py:297
  82.4 9.7 %collective-permute-start.18 = (bf16[336,256]{1,0:T(8,128)(2,1)S(1)}, bf16[336,256]{1,0:T(8,128)(2,1)S(1)}, u32[]{:S(2)}, u32[]{:S(2)}) collective-permute-start(bf16[336,256]{1,0:T(8,128)(2,1)S(1)} %concatenate.26), channel_id=1, source_target_pairs={{0,6},{1,3},{2,0},{3,5},{4,2},{5,7},{6,4},{7,1},{8,14},{9,11},{10,... | collective-permute-start | bytes 516104 | tf_op jit(solution)/shard_map/ppermute | solution.py:297
  82.6 14.7 %collective-permute-start.10 = (f32[176,256]{1,0:T(8,128)S(1)}, f32[176,256]{1,0:T(8,128)S(1)}, u32[]{:S(2)}, u32[]{:S(2)}) collective-permute-start(f32[176,256]{1,0:T(8,128)S(1)} %get-tuple-element.55), channel_id=1, source_target_pairs={{0,16},{1,5},{2,18},{3,7},{4,20},{5,1},{6,22},{7,3},{8,24},{9,13},... | collective-permute-start | bytes 540680 | tf_op jit(solution)/shard_map/ppermute | solution.py:297
  83.0 14.3 %collective-permute-start.12 = (f32[176,256]{1,0:T(8,128)S(1)}, f32[176,256]{1,0:T(8,128)S(1)}, u32[]{:S(2)}, u32[]{:S(2)}) collective-permute-start(f32[176,256]{1,0:T(8,128)S(1)} %get-tuple-element.56), channel_id=1, source_target_pairs={{0,24},{1,7},{2,26},{3,1},{4,28},{5,3},{6,30},{7,5},{8,0},{9,15},{... | collective-permute-start | bytes 540680 | tf_op jit(solution)/shard_map/ppermute | solution.py:297
  88.4 9.0 %collective-permute-start.11 = (f32[176,256]{1,0:T(8,128)S(1)}, f32[176,256]{1,0:T(8,128)S(1)}, u32[]{:S(2)}, u32[]{:S(2)}) collective-permute-start(f32[176,256]{1,0:T(8,128)S(1)} %get-tuple-element.57), channel_id=1, source_target_pairs={{0,8},{1,3},{2,10},{3,5},{4,12},{5,7},{6,14},{7,1},{8,16},{9,11},{... | collective-permute-start | bytes 540680 | tf_op jit(solution)/shard_map/ppermute | solution.py:297
  92.3 8.6 %collective-permute-start.19 = (f32[88,256]{1,0:T(8,128)S(1)}, f32[88,256]{1,0:T(8,128)S(1)}, u32[]{:S(2)}, u32[]{:S(2)}) collective-permute-start(f32[88,256]{1,0:T(8,128)S(1)} %get-tuple-element.63), channel_id=1, source_target_pairs={{0,64},{1,65},{2,66},{3,67},{4,68},{5,69},{6,70},{7,71},{8,72},{9,... | collective-permute-start | bytes 270344 | tf_op jit(solution)/shard_map/ppermute | solution.py:297
  95.3 5.6 %collective-permute-start.21 = (f32[88,256]{1,0:T(8,128)S(1)}, f32[88,256]{1,0:T(8,128)S(1)}, u32[]{:S(2)}, u32[]{:S(2)}) collective-permute-start(f32[88,256]{1,0:T(8,128)S(1)} %get-tuple-element.64), channel_id=1, source_target_pairs={{0,96},{1,33},{2,98},{3,35},{4,100},{5,37},{6,102},{7,39},{8,104},... | collective-permute-start | bytes 270344 | tf_op jit(solution)/shard_map/ppermute | solution.py:297
  97.3 5.7 %collective-permute-start.20 = (f32[88,256]{1,0:T(8,128)S(1)}, f32[88,256]{1,0:T(8,128)S(1)}, u32[]{:S(2)}, u32[]{:S(2)}) collective-permute-start(f32[88,256]{1,0:T(8,128)S(1)} %get-tuple-element.65), channel_id=1, source_target_pairs={{0,32},{1,97},{2,34},{3,99},{4,36},{5,101},{6,38},{7,103},{8,40},{... | collective-permute-start | bytes 270344 | tf_op jit(solution)/shard_map/ppermute | solution.py:297
  97.4 10.2 %collective-permute-start.22 = (bf16[176,256]{1,0:T(8,128)(2,1)S(1)}, bf16[176,256]{1,0:T(8,128)(2,1)S(1)}, u32[]{:S(2)}, u32[]{:S(2)}) collective-permute-start(bf16[176,256]{1,0:T(8,128)(2,1)S(1)} %get-tuple-element.49), channel_id=1, source_target_pairs={{0,8},{1,16},{2,32},{3,48},{4,64},{5,80},{6,96},{7,112},{8,0},{9,2... | collective-permute-start | bytes 270344 | tf_op jit(solution)/shard_map/ppermute | solution.py:297
  103.1 8.3 %collective-permute-start.23 = (bf16[80,256]{1,0:T(8,128)(2,1)S(1)}, bf16[80,256]{1,0:T(8,128)(2,1)S(1)}, u32[]{:S(2)}, u32[]{:S(2)}) collective-permute-start(bf16[80,256]{1,0:T(8,128)(2,1)S(1)} %get-tuple-element.47), channel_id=1, source_target_pairs={{0,8},{1,16},{2,32},{3,48},{4,64},{5,80},{6,96},{7,112},{8,0},{9,2... | collective-permute-start | bytes 122888 | tf_op jit(solution)/shard_map/ppermute | solution.py:297

commit v4 on v3

v4 whole, which is shorter than its diff:
```python
import functools

import jax
import jax.numpy as jnp
import numpy as np
from jax import lax
from jax.experimental import pallas as pl
from jax.experimental.pallas import tpu as pltpu
from jax.sharding import Mesh, PartitionSpec as P

ARC_ROWS = 32
AXES = ("z", "y", "x", "core")
BLK = 256
MAIN = 176
REST = BLK - MAIN
GRANT_FIRST = 24
EXTRA = 16
BF = jnp.bfloat16
F32 = jnp.float32


def linear(z, y, x, q):
    return ((z % 4 * 4 + y % 4) * 4 + x % 4) * 2 + q


def shift_pairs(order0, order1, sign1, stage, step):
    pairs = []
    for z in range(4):
        for y in range(4):
            for x in range(4):
                for q in range(2):
                    axis = (order0, order1)[q][stage]
                    by = step * (1, sign1)[q]
                    to = {"z": z, "y": y, "x": x}
                    to[axis] += by
                    pairs.append((linear(z, y, x, q), linear(to["z"], to["y"], to["x"], q)))
    return pairs


def mirror_pairs():
    pairs = []
    for z in range(4):
        for y in range(4):
            for x in range(4):
                for q in range(2):
                    r, c = 4 * z + y, 2 * x + q
                    i, h = r // 2, r % 2
                    if i < c:
                        to_r, to_c = 2 * c + h, i
                    elif i > c:
                        to_r, to_c = 2 * c + 1 - h, i
                    else:
                        to_r, to_c = 2 * i + 1 - h, i
                    to = linear(to_r // 4, to_r % 4, to_c // 2, to_c % 2)
                    pairs.append((linear(z, y, x, q), to))
    return pairs


MAIN_ORDER = (("x", "z", "y"), ("z", "y", "x"), 1)
REST_ORDER = (("y", "x", "z"), ("y", "x", "z"), -1)


def block_table(order, offsets):
    order0, order1, sign1 = order
    rows = []
    for device in range(128):
        place = {"z": device // 32, "y": device // 8 % 4, "x": device // 2 % 4}
        core = device % 2
        for d in offsets:
            at = dict(place)
            for name, by in zip((order0, order1)[core], d):
                at[name] = (place[name] + by * (1, sign1)[core]) % 4
            r, c = 4 * at["z"] + at["y"], 2 * at["x"] + core
            i, h = r // 2, r % 2
            s = h if i <= c else 1 - h
            rows += [r, 2 * c + s, 2 * c + 1 - s, int(i == c)]
    return np.asarray(rows, np.int32).reshape(128, -1)


def cross_table():
    rows = []
    for device in range(128):
        x, core = device // 2 % 4, device % 2
        for d in range(4):
            first = 2 * (2 * ((x + d * (1, REST_ORDER[2])[core]) % 4) + core)
            rows += [first, first + 1, 0, 0]
    return np.asarray(rows, np.int32).reshape(128, -1)


def pick_rows(map_ref, first, columns, picked, out_ref):
    width, half, unroll = out_ref.shape[1], out_ref.shape[1] // 2, 32

    @pl.loop(0, out_ref.shape[0] // unroll)
    def _(g):
        rows = [columns[pl.ds(2 * map_ref[first + g * unroll + u], 2), :] for u in range(unroll)]
        for u in range(unroll):
            picked[pl.ds(2 * (g * unroll + u), 2), :] = rows[u]

    @pl.loop(0, out_ref.shape[0] // width)
    def _(t):
        at = pl.multiple_of(t * width, width)
        for h in range(2):
            out_ref[pl.ds(at, width), pl.ds(h * half, half)] = picked[
                pl.ds(2 * at + h, width, 2), :
            ].astype(BF)


def first_pick_kernel(map_ref, counts_ref, weight_ref, design_ref, columns, out_ref, held, picked, sems):
    width, half = held.shape[0], held.shape[0] // 2
    tiles, loads = held.shape[1] // width, sems.shape[0]
    copies = []
    for n in range(loads):
        part = pl.ds(n * (held.shape[1] // loads), held.shape[1] // loads)
        copies.append(pltpu.make_async_copy(design_ref.at[:, part], held.at[:, part], sems.at[n]))
        copies[-1].start()

    slot = lax.broadcasted_iota(jnp.int32, (1, width), 1)
    count = jnp.zeros((1, width), jnp.int32)
    for arc in range(width // ARC_ROWS):
        count = jnp.where(slot // ARC_ROWS == arc, counts_ref[arc], count)
    weight = weight_ref[...]
    scale = jnp.sqrt(jnp.where(slot % ARC_ROWS < count, weight, jnp.zeros_like(weight)))

    for n in range(loads):
        copies[n].wait()

        @pl.loop(n * (tiles // loads), (n + 1) * (tiles // loads))
        def _(t):
            at = pl.multiple_of(t * width, width)
            wide = (held[:, pl.ds(at, width)].T.astype(F32) * scale).astype(BF).astype(F32)
            for h in range(2):
                columns[pl.ds(2 * at + h, width, 2), :] = wide[:, h * half : (h + 1) * half]

    pick_rows(map_ref, 0, columns, picked, out_ref)


def second_pick_kernel(map_ref, columns, out_ref, picked):
    pick_rows(map_ref, out_ref.shape[0], columns, picked, out_ref)


def cost(size):
    return pl.CostEstimate(flops=0, bytes_accessed=size << 20, transcendentals=0)


def grant(size):
    return pltpu.CompilerParams(vmem_limit_bytes=size * 1024 * 1024)


def scaled_rows(column_map, counts, weight, design):
    rows, unknowns = design.shape
    vmem, smem = pl.BlockSpec(memory_space=pltpu.VMEM), pl.BlockSpec(memory_space=pltpu.SMEM)
    part = jax.ShapeDtypeStruct((unknowns // 2, rows), BF)
    picked = pltpu.VMEM((unknowns, rows // 2), F32)
    columns, low = pl.pallas_call(
        first_pick_kernel,
        out_shape=[jax.ShapeDtypeStruct((2 * unknowns, rows // 2), F32), part],
        in_specs=[smem, smem, vmem, pl.BlockSpec(memory_space=pl.ANY)],
        out_specs=[vmem, vmem],
        scratch_shapes=[pltpu.VMEM((rows, unknowns), BF), picked, pltpu.SemaphoreType.DMA((4,))],
        compiler_params=grant(GRANT_FIRST),
        cost_estimate=cost(8),
    )(column_map, counts, weight[None, :], design)
    high = pl.pallas_call(
        second_pick_kernel,
        out_shape=part,
        in_specs=[smem, vmem],
        out_specs=vmem,
        scratch_shapes=[picked],
        compiler_params=grant(16),
        cost_estimate=cost(8),
    )(column_map, columns)
    return low, high


def turn(from_ref, to_ref, row, column):
    deep = from_ref.shape[1]

    @pl.loop(0, from_ref.shape[0] // BLK)
    def _(t):
        at = pl.multiple_of(t * BLK, BLK)
        to_ref[pl.ds(row, deep), pl.ds(column + at, BLK)] = from_ref[pl.ds(at, BLK), :].T


def turn_kernel(own_low, own_high, other_low, own_out, low_out):
    turn(own_low, own_out, 0, 0)
    turn(own_high, own_out, 0, own_low.shape[0])
    turn(other_low, low_out, 0, 0)


def product_kernel(plan, opening, cross_made, cross_used, table, *refs):
    if opening:
        own_low, own_high, other_low, other_high, own_turned, low_turned, *outs, sems = refs
        *outs, held, turned = outs
        terms, lines = [], None
        half, deep = own_low.shape
        pieces = [
            (own_low, held.at[pl.ds(0, half), pl.ds(0, deep)]),
            (own_high, held.at[pl.ds(half, half), pl.ds(0, deep)]),
            (other_low, held.at[pl.ds(0, half), pl.ds(deep, deep)]),
            (other_high, held.at[pl.ds(half, half), pl.ds(deep, deep)]),
            (own_turned, turned.at[pl.ds(0, deep), :]),
            (low_turned, turned.at[pl.ds(deep, deep), pl.ds(0, half)]),
        ]
        copies = [pltpu.make_async_copy(a, b, sems.at[n]) for n, (a, b) in enumerate(pieces)]
        for copy in copies:
            copy.start()
        turn(other_high, turned, deep, half)
        for copy in copies:
            copy.wait()
    else:
        held, turned, *outs = refs
        lines = None
        if cross_used:
            lines, *outs = outs
            lines = lines[...]
        count = len(outs) - len(plan) - int(cross_made)
        terms, outs = outs[:count], outs[count:]

    def dot(rows_at, rows, cols_at):
        return jnp.dot(
            held[pl.ds(rows_at, rows), :], turned[:, pl.ds(cols_at, BLK)], preferred_element_type=F32
        )

    i = lax.broadcasted_iota(jnp.int32, (BLK, BLK), 0)
    j = lax.broadcasted_iota(jnp.int32, (BLK, BLK), 1)
    if cross_made:
        *outs, cross_out = outs
        made = []
        for e in range(4):
            at = 4 * e
            cross = dot(pl.multiple_of(table[at] * BLK, BLK), BLK, pl.multiple_of(table[at + 1] * BLK, BLK))
            made.append(jnp.sum(jnp.where(i == j, cross, 0.0), axis=0, keepdims=True))
        lines = jnp.concatenate(made + [jnp.zeros((EXTRA - 4, BLK), F32)], axis=0)
        cross_out[...] = lines

    for out, (first, count, row0, rows, ring, added) in zip(outs, plan):

        def plus(o, value, rows=rows, ring=ring, added=added):
            for n, at in added:
                if ring:
                    term = terms[n][pl.ds(pl.multiple_of((at + o) * rows, 16), rows), :]
                else:
                    term = terms[n][at + o]
                value = value + term.astype(F32)
            return value

        def put(o, value, out=out, rows=rows, ring=ring):
            if ring:
                out[pl.ds(pl.multiple_of(o * rows, 16), rows), :] = value
            else:
                out[o] = value

        batch = 8 if count % 8 == 0 else 4

        @pl.loop(0, count // batch)
        def _(g, batch=batch, first=first, row0=row0, rows=rows, put=put, plus=plus, out=out):
            starts, values = [], []
            for u in range(batch):
                at = 4 * (first + g * batch + u)
                rows_at = pl.multiple_of(table[at] * BLK + row0, 16)
                starts.append(rows_at)
                value = dot(rows_at, rows, pl.multiple_of(table[at + 1] * BLK, BLK))
                values.append(plus(g * batch + u, value).astype(out.dtype))
            for u in range(batch):
                put(g * batch + u, values[u])
            for u in range(batch):
                at = 4 * (first + g * batch + u)

                @pl.when(table[at + 3] == 1)
                def _(u=u, at=at):
                    cols_at = pl.multiple_of(table[at + 1] * BLK, BLK)
                    mixed_at = pl.multiple_of(table[at + 2] * BLK, BLK)
                    value = dot(starts[u], rows, cols_at)
                    mixed = dot(starts[u], rows, mixed_at)
                    low = i[:rows] + row0 >= j[:rows]
                    value = plus(g * batch + u, jnp.where(low, value, mixed))
                    put(g * batch + u, value.astype(out.dtype))

        if ring:
            total = lines
            for n, _ in added:
                total = total + terms[n][pl.ds(16 * REST, EXTRA), :].astype(F32)
            out[pl.ds(count * rows, EXTRA), :] = total.astype(out.dtype)


def products(operands, table, plan, kinds, cross=None, cross_made=False, terms=(), weight=1):
    shapes = []
    for (_, count, _, rows, ring, _), kind in zip(plan, kinds):
        shape = (count * rows + EXTRA, BLK) if ring else (count, rows, BLK)
        shapes.append(jax.ShapeDtypeStruct(shape, kind))
    if cross_made:
        shapes.append(jax.ShapeDtypeStruct((EXTRA, BLK), F32))
    vmem = pl.BlockSpec(memory_space=pltpu.VMEM)
    opening = len(operands) == 6
    if opening:
        half, deep = operands[0].shape
        shapes += [jax.ShapeDtypeStruct((2 * half, 2 * deep), BF), jax.ShapeDtypeStruct((2 * deep, 2 * half), BF)]
    extra = () if cross is None else (cross,)
    return pl.pallas_call(
        functools.partial(product_kernel, plan, opening, cross_made, cross is not None),
        out_shape=shapes,
        in_specs=[pl.BlockSpec(memory_space=pltpu.SMEM)] + [vmem] * (len(operands) + len(extra) + len(terms)),
        out_specs=[vmem] * len(shapes),
        scratch_shapes=[pltpu.SemaphoreType.DMA((6,))] if opening else [],
        compiler_params=grant(24),
        cost_estimate=cost(weight),
    )(table, *operands, *extra, *terms)


def call_sum(kernel, shapes, *operands):
    vmem = pl.BlockSpec(memory_space=pltpu.VMEM)
    return pl.pallas_call(
        kernel,
        out_shape=[jax.ShapeDtypeStruct(shape, kind) for shape, kind in shapes],
        in_specs=[vmem] * len(operands),
        out_specs=[vmem] * len(shapes),
        compiler_params=grant(12),
        cost_estimate=cost(1),
    )(*operands)


def main_sum_kernel(own, second, first, third, *outs):
    for d, out in enumerate(outs):
        total = own[d]
        for ref in (second, first, third):
            total = total + ref[d].astype(F32)
        out[...] = total


def rest_sum_kernel(own, second, first, third, *outs):
    quarter = own.shape[0] - EXTRA
    cross = own[pl.ds(quarter, EXTRA), :][0:1]
    for d, ref in ((2, second), (1, first), (3, third)):
        cross = cross + ref[pl.ds(quarter, EXTRA), :].astype(F32)[d : d + 1]
    cross = jnp.broadcast_to(cross, (8, BLK))
    for d, out in enumerate(outs):
        part = pl.ds(d * REST, REST)
        total = own[part, :]
        for ref in (second, first, third):
            total = total + ref[part, :].astype(F32)
        out[pl.ds(0, REST), :] = total
        out[pl.ds(REST, 8), :] = cross


def last_sum_kernel(own, second, first, third, out, sent):
    total = own[...] + second[...] + first[...] + third[...]
    out[...] = total
    sent[...] = total[: sent.shape[0]].astype(sent.dtype)


def finish_kernel(state, scale, main_ref, rest_ref, got_main_ref, got_rest_ref, out_ref):
    s, fold = state[0], state[1] == 1
    here = jnp.concatenate([main_ref[...], rest_ref[0:REST, :]], axis=0)
    got = jnp.concatenate([got_main_ref[...].astype(F32), got_rest_ref[...].astype(F32)], axis=0).T
    mine = here.T
    i = lax.broadcasted_iota(jnp.int32, (BLK, BLK), 0)
    j = lax.broadcasted_iota(jnp.int32, (BLK, BLK), 1)
    on = jnp.logical_and(fold, i == j)
    low = jnp.logical_or(jnp.logical_not(fold), i >= j)
    first = jnp.where(low, here, mine) * scale
    second = jnp.where(on, rest_ref[REST : REST + 1, :], jnp.where(low, got, here)) * scale

    @pl.when(s == 0)
    def _():
        out_ref[:, 0:BLK] = first
        out_ref[:, BLK : 2 * BLK] = second

    @pl.when(s == 1)
    def _():
        out_ref[:, BLK : 2 * BLK] = first
        out_ref[:, 0:BLK] = second


def local(design, weight, counts, column_map):
    rows_here = design.shape[0]
    core = lax.axis_index("core")
    place = {name: lax.axis_index(name) for name in ("z", "y", "x")}
    total_rows = rows_here * 128

    own_low, own_high = scaled_rows(column_map, counts, weight, design)

    def move(array, pairs):
        return lax.ppermute(array, AXES, pairs)

    M, R = MAIN_ORDER, REST_ORDER

    def main_to(stage, step):
        return shift_pairs(*M, stage, step)

    def rest_to(stage, step):
        return shift_pairs(*R, stage, step)

    swap = [(0, 1), (1, 0)]
    other_low = lax.ppermute(own_low, "core", swap)
    other_high = lax.ppermute(own_high, "core", swap)
    half = own_low.shape
    own_turned, low_turned = pl.pallas_call(
        turn_kernel,
        out_shape=[
            jax.ShapeDtypeStruct((half[1], 2 * half[0]), BF),
            jax.ShapeDtypeStruct((half[1], half[0]), BF),
        ],
        in_specs=[pl.BlockSpec(memory_space=pltpu.VMEM)] * 3,
        out_specs=[pl.BlockSpec(memory_space=pltpu.VMEM)] * 2,
        compiler_params=grant(12),
        cost_estimate=cost(1),
    )(own_low, own_high, other_low)

    plus = [(a, b) for a in (0, 1) for b in range(4)]
    minus = [(a, b) for a in (2, 3) for b in range(4)]
    every = plus + minus
    tables = [cross_table()]

    def blocks(order, d, rest, *added):
        first = sum(t.shape[1] for t in tables) // 4
        tables.append(block_table(order, [(d,) + p for p in rest]))
        row0, rows = (0, MAIN) if order is M else (MAIN, REST)
        return first, len(rest), row0, rows, order is R, added

    plan_1 = [blocks(M, 2, plus), blocks(M, 2, minus)]
    plan_1r = [blocks(R, 3, every)]
    plan_2 = [blocks(M, 1, minus), blocks(M, 3, plus)]
    plan_2r = [blocks(R, 2, every, (0, 0))]
    plan_3 = [blocks(M, 1, plus, (0, 0)), blocks(M, 3, minus, (1, 0))]
    plan_3r = [blocks(R, 1, every, (0, 0))]
    plan_4 = [
        blocks(M, 0, every[4 * d : 4 * d + 4], (2 * (d // 2), 4 * (d % 2)), (2 * (d // 2) + 1, 4 * (d % 2)))
        for d in range(4)
    ]
    plan_4r = [blocks(R, 0, every[4 * d : 4 * d + 4], (0, 4 * d)) for d in range(4)]
    device = ((place["z"] * 4 + place["y"]) * 4 + place["x"]) * 2 + core
    table = lax.dynamic_index_in_dim(
        jnp.asarray(np.concatenate(tables, axis=1)), device, 0, keepdims=False
    )

    pieces = (own_low, own_high, other_low, other_high, own_turned, low_turned)
    ring, cross, *both = products(pieces, table, plan_1r, (BF,), cross_made=True)
    got_r = move(ring, rest_to(0, 1))
    first_p, first_m = products(both, table, plan_1, (BF, BF))
    got_1p = move(first_p, main_to(0, 1))
    got_1m = move(first_m, main_to(0, -1))
    both, first_p = lax.optimization_barrier((both, first_p))
    side_p, side_m = products(both, table, plan_2, (BF, BF))
    got_2p = move(side_p, main_to(0, 1))
    got_2m = move(side_m, main_to(0, -1))
    both, side_p = lax.optimization_barrier((both, side_p))
    (ring,) = products(both, table, plan_2r, (BF,), cross, terms=(got_r,))
    got_r = move(ring, rest_to(0, 1))
    both, ring = lax.optimization_barrier((both, ring))
    relay_p, relay_m = products(both, table, plan_3, (BF, BF), terms=(got_1p, got_1m))
    got_3p = move(relay_p, main_to(0, 1))
    got_3m = move(relay_m, main_to(0, -1))
    both, relay_p, got_2p, got_2m = lax.optimization_barrier((both, relay_p, got_2p, got_2m))
    (ring,) = products(both, table, plan_3r, (BF,), cross, terms=(got_r,), weight=60)
    got_r = move(ring, rest_to(0, 1))
    both, ring = lax.optimization_barrier((both, ring))
    part = products(both, table, plan_4, (F32, BF, BF, BF), terms=(got_3p, got_2m, got_2p, got_3m))
    rest = products(both, table, plan_4r, (F32, BF, BF, BF), cross, terms=(got_r,))

    got = [move(part[d], main_to(1, d)) for d in (2, 1, 3)]
    got_r = [move(rest[d], rest_to(1, d)) for d in (2, 1, 3)]
    part = call_sum(main_sum_kernel, [((MAIN, BLK), F32)] * 4, part[0], *got)
    rest = call_sum(rest_sum_kernel, [((REST + 8, BLK), F32)] * 4, rest[0], *got_r)

    got = [move(part[d], main_to(2, d)) for d in (2, 1, 3)]
    got_r = [move(rest[d], rest_to(2, d)) for d in (2, 1, 3)]
    main_3, main_sent = call_sum(last_sum_kernel, [((MAIN, BLK), F32), ((MAIN, BLK), BF)], part[0], *got)
    rest_3, rest_sent = call_sum(last_sum_kernel, [((REST + 8, BLK), F32), ((REST, BLK), BF)], rest[0], *got_r)
    got_main = move(main_sent, mirror_pairs())
    got_rest = move(rest_sent, mirror_pairs())

    r, c = 4 * place["z"] + place["y"], 2 * place["x"] + core
    i, h = r // 2, r % 2
    s = jnp.where(i <= c, h, 1 - h)
    state = jnp.stack([s, (i == c).astype(jnp.int32)]).astype(jnp.int32)
    vmem = pl.BlockSpec(memory_space=pltpu.VMEM)
    return pl.pallas_call(
        lambda *refs: finish_kernel(refs[0], 1.0 / total_rows, *refs[1:]),
        out_shape=jax.ShapeDtypeStruct((BLK, 2 * BLK), F32),
        in_specs=[pl.BlockSpec(memory_space=pltpu.SMEM)] + [vmem] * 4,
        out_specs=vmem,
        compiler_params=pltpu.CompilerParams(vmem_limit_bytes=16 * 1024 * 1024),
    )(state, main_3, rest_3, got_main, got_rest)


def solution(mesh):
    fine = Mesh(mesh.devices.reshape(4, 4, 4, 2), AXES)
    return jax.shard_map(
        local,
        mesh=fine,
        in_specs=(P(AXES, None), P(AXES), P(AXES), P()),
        out_specs=P(("z", "y"), ("x", "core")),
        check_vma=False,
    )
```

time: 113 us -> 105 us (0.929)
  waiting for transfers between devices: 35.2 us -> 21.4 us
  starting transfers between devices: 32.5 us -> 44.3 us
  other arithmetic: 6.74 us -> 0.07 us
  Pallas kernels: 32.8 us -> 34.1 us
    ppermute x23, waiting for transfers between devices: 35.2 us -> 21.4 us  [move(): return lax.ppermute(array, AXES, pairs)]
    ppermute x23, starting transfers between devices: 32.5 us -> 43.7 us  [move(): return lax.ppermute(array, AXES, pairs)]
    convert_element_type x11 -> x0, other arithmetic: 3.83 us -> none  [the longest x2 2.01 us: local(): main_2 = main_2 + move(part[d].astype(BF), main_to(1, d)).astype(F32)]
    add x4 -> x0, other arithmetic: 1.54 us -> none  [the longest x1 1.44 us: local(): main_2 = main_2 + move(part[d].astype(BF), main_to(1, d)).astype(F32)]
    pallas_call x5 -> x15, Pallas kernels: 31.3 us -> 32.6 us  [the longest x8 21.5 us: products(): pl.pallas_call(functools.partial(product_kernel, plan, opening, cross_mad...]
    another operation x1 -> x0, other arithmetic: 1.25 us -> none
  transfers between devices with their start and end apart: 24 -> 25, of which waited for: 11 -> 11; matrix products, arithmetic and copies ran while one was open for 6% -> 1% of each run, Pallas kernels for 13% -> 22%
where the time goes in v4:
time: 105 us; the launch traced here: 104 us
  starting transfers between devices  44.3 us (42%)
  Pallas kernels  34.1 us (32%)
  waiting for transfers between devices  21.4 us (20%)
  local copies, waits for them, and re-layouts  4.38 us (4%)
    ppermute x23, starting transfers between devices, move(): return lax.ppermute(array, AXES, pairs)  43.7 us
    pallas_call x8, Pallas kernels, products(): pl.pallas_call(functools.partial(product_kernel, plan, opening, cross_mad...  21.5 us
    ppermute x23, waiting for transfers between devices, move(): return lax.ppermute(array, AXES, pairs)  21.4 us
    pallas_call x1, Pallas kernels, scaled_rows(): pl.pallas_call(first_pick_kernel, out_shape=[jax.ShapeDtypeStruct((2 * un...  5.13 us
    unnamed x8, local copies, waits for them, and re-layouts  3.64 us
    pallas_call x1, Pallas kernels, scaled_rows(): pl.pallas_call(second_pick_kernel, out_shape=part, in_specs=[smem, vmem],...  3.44 us
    pallas_call x1, Pallas kernels, local(): pl.pallas_call(turn_kernel, out_shape=[jax.ShapeDtypeStruct((half[1], 2 *...  2.16 us
  transfers between devices with their start and end apart: 25, of which 11 were waited for; matrix products, arithmetic and copies ran while one was open for 1% of the time, Pallas kernels for 22%

profile of v4, /device:TPU:6, one launch (start us, length us, event | category | flops | bytes accessed | tf_op | source)
XLA Modules:
  0.0 104.5 jit_solution(8155336101219863814)
XLA Ops:
  0.0 1.6 %copy-done = bf16[256,4096]{1,0:T(8,128)(2,1)S(1)} copy-done((bf16[256,4096]{1,0:T(8,128)(2,1)S(1)}, bf16[256,4096]{1,0:T(8,128)(2,1)}, u32[]{:S(2)}) %copy-start) | copy-done | bytes 2097176
  1.6 0.7 copy-done.1
  2.3 0.7 copy-done.2
  3.0 0.7 copy-done.3
  3.6 5.1 %shard_map.55 = (f32[8192,128]{1,0:T(8,128)S(1)}, bf16[2048,256]{1,0:T(8,128)(2,1)S(1)}) custom-call(s32[4096]{0:T(1024)S(1)} %copy-done.1, s32[8]{0:T(128)S(1)} %copy-done.3, f32[1,256]{1,0:T(1,128)S(1)} %bitcast.3, bf16[256,4096]{1,0:T(8,128)(2,1)S(1)} %copy-done), custom_call_target="tpu_custom_call" | custom-call | bytes 8388608 | tf_op jit(solution)/shard_map/pallas_call | solution.py:154
  8.8 0.1 collective-permute-start
  8.9 3.4 %shard_map.56.own_high.refs_1_ = bf16[2048,256]{1,0:T(8,128)(2,1)S(1)} custom-call(s32[4096]{0:T(1024)S(1)} %copy-done.1, f32[8192,128]{1,0:T(8,128)S(1)} %get-tuple-element.52.columns), custom_call_target="tpu_custom_call" | custom-call | bytes 8388608 | tf_op jit(solution)/shard_map/pallas_call | solution.py:163
  12.3 0.6 collective-permute-start.1
  12.9 0.7 dynamic-slice_reduce_fusion.table
  13.6 0.0 collective-permute-done.other_low.refs_2_
  13.7 2.2 %shard_map.57 = (bf16[256,4096]{1,0:T(8,128)(2,1)S(1)}, bf16[256,2048]{1,0:T(8,128)(2,1)S(1)}) custom-call(bf16[2048,256]{1,0:T(8,128)(2,1)S(1)} %get-tuple-element.51.own_low.refs_0_, bf16[2048,256]{1,0:T(8,128)(2,1)S(1)} %shard_map.56.own_high.refs_1_, bf16[2048,256]{1,0:T(8,128)(2,1)S(1)} %collective-permute-done.other_low.refs_2_), custom_call_target="tpu_custom_call" | custom-call | bytes 1048576 | tf_op jit(solution)/shard_map/pallas_call | solution.py:397
  15.8 4.3 %shard_map.58 = (bf16[1296,256]{1,0:T(8,128)(2,1)S(1)}, f32[16,256]{1,0:T(8,128)S(1)}, bf16[4096,512]{1,0:T(8,128)(2,1)S(1)}, bf16[512,4096]{1,0:T(8,128)(2,1)S(1)}) custom-call(s32[528]{0:T(1024)S(1)} %dynamic-slice_reduce_fusion.table, bf16[2048,256]{1,0:T(8,128)(2,1)S(1)} %get-tuple-element.51.own_low.refs_0_, ...), custom_call_target="tpu_custom_call" | custom-call | bytes 1048576 | tf_op jit(solution)/shard_map/pallas_call | solution.py:299
  20.1 2.5 %collective-permute-start.2 = (bf16[1296,256]{1,0:T(8,128)(2,1)S(1)}, bf16[1296,256]{1,0:T(8,128)(2,1)S(1)}, u32[]{:S(2)}, u32[]{:S(2)}) collective-permute-start(bf16[1296,256]{1,0:T(8,128)(2,1)S(1)} %get-tuple-element.64), channel_id=1, source_target_pairs={{0,8},{1,25},{2,10},{3,27},{4,12},{5,29},{6,14},{7,31},{8,16},{9,1... | collective-permute-start | bytes 1990664 | tf_op jit(solution)/shard_map/ppermute | solution.py:383
  22.6 2.4 %shard_map.59 = (bf16[8,176,256]{2,1,0:T(8,128)(2,1)S(1)}, bf16[8,176,256]{2,1,0:T(8,128)(2,1)S(1)}) custom-call(s32[528]{0:T(1024)S(1)} %dynamic-slice_reduce_fusion.table, bf16[4096,512]{1,0:T(8,128)(2,1)S(1)} %get-tuple-element.72.refs_0_, bf16[512,4096]{1,0:T(8,128)(2,1)S(1)} %get-tuple-element.73.refs_1_), custom_call_target="tpu_custom_call" | custom-call | bytes 1048576 | tf_op jit(solution)/shard_map/pallas_call | solution.py:299
  25.0 0.9 collective-permute-start.4
  25.9 2.4 %collective-permute-start.3 = (bf16[8,176,256]{2,1,0:T(8,128)(2,1)S(1)}, bf16[8,176,256]{2,1,0:T(8,128)(2,1)S(1)}, u32[]{:S(2)}, u32[]{:S(2)}) collective-permute-start(bf16[8,176,256]{2,1,0:T(8,128)(2,1)S(1)} %get-tuple-element.57), channel_id=1, source_target_pairs={{0,2},{1,33},{2,4},{3,35},{4,6},{5,37},{6,0},{7,39},{8,10},{9,41},... | collective-permute-start | bytes 2162696 | tf_op jit(solution)/shard_map/ppermute | solution.py:383
  28.3 1.9 %shard_map.60 = (bf16[8,176,256]{2,1,0:T(8,128)(2,1)S(1)}, bf16[8,176,256]{2,1,0:T(8,128)(2,1)S(1)}) custom-call(s32[528]{0:T(1024)S(1)} %dynamic-slice_reduce_fusion.table, bf16[4096,512]{1,0:T(8,128)(2,1)S(1)} %get-tuple-element.72.refs_0_, bf16[512,4096]{1,0:T(8,128)(2,1)S(1)} %get-tuple-element.73.refs_1_), custom_call_target="tpu_custom_call" | custom-call | bytes 1048576 | tf_op jit(solution)/shard_map/pallas_call | solution.py:299
  30.2 0.7 collective-permute-start.6
  30.9 2.6 %collective-permute-start.5 = (bf16[8,176,256]{2,1,0:T(8,128)(2,1)S(1)}, bf16[8,176,256]{2,1,0:T(8,128)(2,1)S(1)}, u32[]{:S(2)}, u32[]{:S(2)}) collective-permute-start(bf16[8,176,256]{2,1,0:T(8,128)(2,1)S(1)} %get-tuple-element.60), channel_id=1, source_target_pairs={{0,2},{1,33},{2,4},{3,35},{4,6},{5,37},{6,0},{7,39},{8,10},{9,41},... | collective-permute-start | bytes 2162696 | tf_op jit(solution)/shard_map/ppermute | solution.py:383
  33.5 0.0 collective-permute-done.2.refs_3_
  33.5 1.8 %shard_map.61 = bf16[1296,256]{1,0:T(8,128)(2,1)S(1)} custom-call(s32[528]{0:T(1024)S(1)} %dynamic-slice_reduce_fusion.table, bf16[4096,512]{1,0:T(8,128)(2,1)S(1)} %get-tuple-element.72.refs_0_, bf16[512,4096]{1,0:T(8,128)(2,1)S(1)} %get-tuple-element.73.refs_1_, f32[16,256]{1,0:T(8,128)S(1)} %get-tuple-element.63.refs_2_, ...), custom_call_target="tpu_custom_call" | custom-call | bytes 1048576 | tf_op jit(solution)/shard_map/pallas_call | solution.py:299
  35.3 1.6 %collective-permute-start.7 = (bf16[1296,256]{1,0:T(8,128)(2,1)S(1)}, bf16[1296,256]{1,0:T(8,128)(2,1)S(1)}, u32[]{:S(2)}, u32[]{:S(2)}) collective-permute-start(bf16[1296,256]{1,0:T(8,128)(2,1)S(1)} %shard_map.61), channel_id=1, source_target_pairs={{0,8},{1,25},{2,10},{3,27},{4,12},{5,29},{6,14},{7,31},{8,16},{9,1... | collective-permute-start | bytes 1990664 | tf_op jit(solution)/shard_map/ppermute | solution.py:383
  36.9 0.6 collective-permute-done.4.refs_3_
  37.6 0.0 collective-permute-done.3.refs_2_
  37.6 2.9 %shard_map.62 = (bf16[8,176,256]{2,1,0:T(8,128)(2,1)S(1)}, bf16[8,176,256]{2,1,0:T(8,128)(2,1)S(1)}) custom-call(s32[528]{0:T(1024)S(1)} %dynamic-slice_reduce_fusion.table, bf16[4096,512]{1,0:T(8,128)(2,1)S(1)} %get-tuple-element.72.refs_0_, bf16[512,4096]{1,0:T(8,128)(2,1)S(1)} %get-tuple-element.73.refs_1_, ...), custom_call_target="tpu_custom_call" | custom-call | bytes 1048576 | tf_op jit(solution)/shard_map/pallas_call | solution.py:299
  40.5 0.1 collective-permute-start.9
  40.6 3.3 %collective-permute-start.8 = (bf16[8,176,256]{2,1,0:T(8,128)(2,1)S(1)}, bf16[8,176,256]{2,1,0:T(8,128)(2,1)S(1)}, u32[]{:S(2)}, u32[]{:S(2)}) collective-permute-start(bf16[8,176,256]{2,1,0:T(8,128)(2,1)S(1)} %get-tuple-element.68), channel_id=1, source_target_pairs={{0,2},{1,33},{2,4},{3,35},{4,6},{5,37},{6,0},{7,39},{8,10},{9,41},... | collective-permute-start | bytes 2162696 | tf_op jit(solution)/shard_map/ppermute | solution.py:383
  43.9 1.4 %collective-permute-done.6.refs_3_ = bf16[8,176,256]{2,1,0:T(8,128)(2,1)S(1)} collective-permute-done((bf16[8,176,256]{2,1,0:T(8,128)(2,1)S(1)}, bf16[8,176,256]{2,1,0:T(8,128)(2,1)S(1)}, u32[]{:S(2)}, u32[]{:S(2)}) %collective-permute-start.6) | collective-permute-done | bytes 720928 | tf_op jit(solution)/shard_map/ppermute | solution.py:383
  45.3 1.9 %collective-permute-done.7.refs_3_ = bf16[1296,256]{1,0:T(8,128)(2,1)S(1)} collective-permute-done((bf16[1296,256]{1,0:T(8,128)(2,1)S(1)}, bf16[1296,256]{1,0:T(8,128)(2,1)S(1)}, u32[]{:S(2)}, u32[]{:S(2)}) %collective-permute-start.7) | collective-permute-done | bytes 663584 | tf_op jit(solution)/shard_map/ppermute | solution.py:383
  47.3 2.7 %shard_map.63 = bf16[1296,256]{1,0:T(8,128)(2,1)S(1)} custom-call(s32[528]{0:T(1024)S(1)} %dynamic-slice_reduce_fusion.table, bf16[4096,512]{1,0:T(8,128)(2,1)S(1)} %get-tuple-element.72.refs_0_, bf16[512,4096]{1,0:T(8,128)(2,1)S(1)} %get-tuple-element.73.refs_1_, f32[16,256]{1,0:T(8,128)S(1)} %get-tuple-element.63.refs_2_, ...), custom_call_target="tpu_custom_call" | custom-call | bytes 62914560 | tf_op jit(solution)/shard_map/pallas_call | solution.py:299
  49.9 0.1 collective-permute-start.16
  50.0 3.1 %collective-permute-done.9.refs_5_ = bf16[8,176,256]{2,1,0:T(8,128)(2,1)S(1)} collective-permute-done((bf16[8,176,256]{2,1,0:T(8,128)(2,1)S(1)}, bf16[8,176,256]{2,1,0:T(8,128)(2,1)S(1)}, u32[]{:S(2)}, u32[]{:S(2)}) %collective-permute-start.9) | collective-permute-done | bytes 720928 | tf_op jit(solution)/shard_map/ppermute | solution.py:383
  53.1 0.0 collective-permute-done.8.refs_2_
  53.1 2.7 %shard_map.64 = (f32[4,176,256]{2,1,0:T(8,128)S(1)}, bf16[4,176,256]{2,1,0:T(8,128)(2,1)S(1)}, bf16[4,176,256]{2,1,0:T(8,128)(2,1)S(1)}, bf16[4,176,256]{2,1,0:T(8,128)(2,1)S(1)}) custom-call(s32[528]{0:T(1024)S(1)} %dynamic-slice_reduce_fusion.table, bf16[4096,512]{1,0:T(8,128)(2,1)S(1)} %get-tuple-element.72.refs_0_, ...), custom_call_target="tpu_custom_call" | custom-call | bytes 1048576 | tf_op jit(solution)/shard_map/pallas_call | solution.py:299
  55.9 3.9 %collective-permute-start.10 = (bf16[4,176,256]{2,1,0:T(8,128)(2,1)S(1)}, bf16[4,176,256]{2,1,0:T(8,128)(2,1)S(1)}, u32[]{:S(2)}, u32[]{:S(2)}) collective-permute-start(bf16[4,176,256]{2,1,0:T(8,128)(2,1)S(1)} %get-tuple-element.78), channel_id=1, source_target_pairs={{0,64},{1,17},{2,66},{3,19},{4,68},{5,21},{6,70},{7,23},{8,72},{9,... | collective-permute-start | bytes 1081352 | tf_op jit(solution)/shard_map/ppermute | solution.py:383
  59.7 1.1 %collective-permute-start.11 = (bf16[4,176,256]{2,1,0:T(8,128)(2,1)S(1)}, bf16[4,176,256]{2,1,0:T(8,128)(2,1)S(1)}, u32[]{:S(2)}, u32[]{:S(2)}) collective-permute-start(bf16[4,176,256]{2,1,0:T(8,128)(2,1)S(1)} %get-tuple-element.79), channel_id=1, source_target_pairs={{0,32},{1,9},{2,34},{3,11},{4,36},{5,13},{6,38},{7,15},{8,40},{9,1... | collective-permute-start | bytes 1081352 | tf_op jit(solution)/shard_map/ppermute | solution.py:383
  60.8 2.2 %collective-permute-start.12 = (bf16[4,176,256]{2,1,0:T(8,128)(2,1)S(1)}, bf16[4,176,256]{2,1,0:T(8,128)(2,1)S(1)}, u32[]{:S(2)}, u32[]{:S(2)}) collective-permute-start(bf16[4,176,256]{2,1,0:T(8,128)(2,1)S(1)} %get-tuple-element.80), channel_id=1, source_target_pairs={{0,96},{1,25},{2,98},{3,27},{4,100},{5,29},{6,102},{7,31},{8,104},... | collective-permute-start | bytes 1081352 | tf_op jit(solution)/shard_map/ppermute | solution.py:383
  63.0 0.0 collective-permute-done.16.refs_3_
  63.0 2.9 %shard_map.67 = (f32[336,256]{1,0:T(8,128)S(1)}, bf16[336,256]{1,0:T(8,128)(2,1)S(1)}, bf16[336,256]{1,0:T(8,128)(2,1)S(1)}, bf16[336,256]{1,0:T(8,128)(2,1)S(1)}) custom-call(s32[528]{0:T(1024)S(1)} %dynamic-slice_reduce_fusion.table, bf16[4096,512]{1,0:T(8,128)(2,1)S(1)} %get-tuple-element.72.refs_0_, bf16[512,4096]{1,0:T(8,128)(2,1)S(1)} %get-tuple-element.73.refs_1_, ...), custom_call_target="tpu_custom_call" | custom-call | bytes 1048576 | tf_op jit(solution)/shard_map/pallas_call | solution.py:299
  65.8 2.6 %collective-permute-start.17 = (bf16[336,256]{1,0:T(8,128)(2,1)S(1)}, bf16[336,256]{1,0:T(8,128)(2,1)S(1)}, u32[]{:S(2)}, u32[]{:S(2)}) collective-permute-start(bf16[336,256]{1,0:T(8,128)(2,1)S(1)} %get-tuple-element.87), channel_id=1, source_target_pairs={{0,4},{1,5},{2,6},{3,7},{4,0},{5,1},{6,2},{7,3},{8,12},{9,13},{10,... | collective-permute-start | bytes 516104 | tf_op jit(solution)/shard_map/ppermute | solution.py:383
  68.4 0.6 collective-permute-done.11.first
  69.0 1.1 %collective-permute-done.12.third = bf16[4,176,256]{2,1,0:T(8,128)(2,1)S(1)} collective-permute-done((bf16[4,176,256]{2,1,0:T(8,128)(2,1)S(1)}, bf16[4,176,256]{2,1,0:T(8,128)(2,1)S(1)}, u32[]{:S(2)}, u32[]{:S(2)}) %collective-permute-start.12) | collective-permute-done | bytes 360480 | tf_op jit(solution)/shard_map/ppermute | solution.py:383
  70.1 0.1 shard_map.65
  70.2 2.2 %collective-permute-start.13 = (f32[176,256]{1,0:T(8,128)S(1)}, f32[176,256]{1,0:T(8,128)S(1)}, u32[]{:S(2)}, u32[]{:S(2)}) collective-permute-start(f32[176,256]{1,0:T(8,128)S(1)} %get-tuple-element.82), channel_id=1, source_target_pairs={{0,16},{1,5},{2,18},{3,7},{4,20},{5,1},{6,22},{7,3},{8,24},{9,13},... | collective-permute-start | bytes 540680 | tf_op jit(solution)/shard_map/ppermute | solution.py:383
  72.4 3.2 %collective-permute-start.18 = (bf16[336,256]{1,0:T(8,128)(2,1)S(1)}, bf16[336,256]{1,0:T(8,128)(2,1)S(1)}, u32[]{:S(2)}, u32[]{:S(2)}) collective-permute-start(bf16[336,256]{1,0:T(8,128)(2,1)S(1)} %get-tuple-element.88), channel_id=1, source_target_pairs={{0,2},{1,7},{2,4},{3,1},{4,6},{5,3},{6,0},{7,5},{8,10},{9,15},{10,... | collective-permute-start | bytes 516104 | tf_op jit(solution)/shard_map/ppermute | solution.py:383
  75.6 0.0 collective-permute-start.19
  75.6 0.0 collective-permute-start.14
  75.6 3.2 %collective-permute-start.15 = (f32[176,256]{1,0:T(8,128)S(1)}, f32[176,256]{1,0:T(8,128)S(1)}, u32[]{:S(2)}, u32[]{:S(2)}) collective-permute-start(f32[176,256]{1,0:T(8,128)S(1)} %get-tuple-element.84), channel_id=1, source_target_pairs={{0,24},{1,7},{2,26},{3,1},{4,28},{5,3},{6,30},{7,5},{8,0},{9,15},{... | collective-permute-start | bytes 540680 | tf_op jit(solution)/shard_map/ppermute | solution.py:383
  78.8 1.6 %collective-permute-done.18.first = bf16[336,256]{1,0:T(8,128)(2,1)S(1)} collective-permute-done((bf16[336,256]{1,0:T(8,128)(2,1)S(1)}, bf16[336,256]{1,0:T(8,128)(2,1)S(1)}, u32[]{:S(2)}, u32[]{:S(2)}) %collective-permute-start.18) | collective-permute-done | bytes 172064 | tf_op jit(solution)/shard_map/ppermute | solution.py:383
  80.4 2.7 %collective-permute-done.19.third = bf16[336,256]{1,0:T(8,128)(2,1)S(1)} collective-permute-done((bf16[336,256]{1,0:T(8,128)(2,1)S(1)}, bf16[336,256]{1,0:T(8,128)(2,1)S(1)}, u32[]{:S(2)}, u32[]{:S(2)}) %collective-permute-start.19) | collective-permute-done | bytes 172064 | tf_op jit(solution)/shard_map/ppermute | solution.py:383
  83.1 0.1 shard_map.68
  83.2 4.8 %collective-permute-start.20 = (f32[88,256]{1,0:T(8,128)S(1)}, f32[88,256]{1,0:T(8,128)S(1)}, u32[]{:S(2)}, u32[]{:S(2)}) collective-permute-start(f32[88,256]{1,0:T(8,128)S(1)} %get-tuple-element.91), channel_id=1, source_target_pairs={{0,64},{1,65},{2,66},{3,67},{4,68},{5,69},{6,70},{7,71},{8,72},{9,... | collective-permute-start | bytes 270344 | tf_op jit(solution)/shard_map/ppermute | solution.py:383
  88.0 3.2 %collective-permute-start.22 = (f32[88,256]{1,0:T(8,128)S(1)}, f32[88,256]{1,0:T(8,128)S(1)}, u32[]{:S(2)}, u32[]{:S(2)}) collective-permute-start(f32[88,256]{1,0:T(8,128)S(1)} %get-tuple-element.93), channel_id=1, source_target_pairs={{0,96},{1,33},{2,98},{3,35},{4,100},{5,37},{6,102},{7,39},{8,104},... | collective-permute-start | bytes 270344 | tf_op jit(solution)/shard_map/ppermute | solution.py:383
  91.3 0.0 collective-permute-done.14.first
  91.3 0.0 collective-permute-done.15.third
  91.3 0.3 collective-permute-start.23
  91.7 0.0 collective-permute-done.20.second
  91.7 2.9 %collective-permute-done.21.first = f32[88,256]{1,0:T(8,128)S(1)} collective-permute-done((f32[88,256]{1,0:T(8,128)S(1)}, f32[88,256]{1,0:T(8,128)S(1)}, u32[]{:S(2)}, u32[]{:S(2)}) %collective-permute-start.21) | collective-permute-done | bytes 90144 | tf_op jit(solution)/shard_map/ppermute | solution.py:383
  94.6 0.0 collective-permute-done.22.third
  94.6 2.8 %collective-permute-start.24 = (bf16[80,256]{1,0:T(8,128)(2,1)S(1)}, bf16[80,256]{1,0:T(8,128)(2,1)S(1)}, u32[]{:S(2)}, u32[]{:S(2)}) collective-permute-start(bf16[80,256]{1,0:T(8,128)(2,1)S(1)} %get-tuple-element.96), channel_id=1, source_target_pairs={{0,8},{1,16},{2,32},{3,48},{4,64},{5,80},{6,96},{7,112},{8,0},{9,2... | collective-permute-start | bytes 122888 | tf_op jit(solution)/shard_map/ppermute | solution.py:383
  97.4 0.1 pad_add_fusion.refs_0_
  97.5 3.0 %collective-permute-done.23.refs_3_ = bf16[176,256]{1,0:T(8,128)(2,1)S(1)} collective-permute-done((bf16[176,256]{1,0:T(8,128)(2,1)S(1)}, bf16[176,256]{1,0:T(8,128)(2,1)S(1)}, u32[]{:S(2)}, u32[]{:S(2)}) %collective-permute-start.23) | collective-permute-done | bytes 90144 | tf_op jit(solution)/shard_map/ppermute | solution.py:383
  100.5 2.5 %collective-permute-done.24.refs_4_ = bf16[80,256]{1,0:T(8,128)(2,1)S(1)} collective-permute-done((bf16[80,256]{1,0:T(8,128)(2,1)S(1)}, bf16[80,256]{1,0:T(8,128)(2,1)S(1)}, u32[]{:S(2)}, u32[]{:S(2)}) %collective-permute-start.24) | collective-permute-done | bytes 40992 | tf_op jit(solution)/shard_map/ppermute | solution.py:383
  102.9 1.5 %shard_map.70 = f32[256,512]{1,0:T(8,128)} custom-call(s32[2]{0:T(128)S(1)} %pad_add_fusion.refs_0_, f32[176,256]{1,0:T(8,128)S(1)} %get-tuple-element.85.refs_1_, f32[88,256]{1,0:T(8,128)S(1)} %get-tuple-element.94.refs_2_, bf16[176,256]{1,0:T(8,128)(2,1)S(1)} %collective-permute-done.23.refs_3_, bf16[80,256]{1,0:T(8,128)(2,1)S(1)} %collective-permute-done.24.refs_4_), custom_call_target="tpu_custom_call" | custom-call | tf_op jit(solution)/shard_map/pallas_call | solution.py:477
  (12 shorter events, 0.1 us)
Async XLA Ops:
  0.0 1.6 %copy-start = (bf16[256,4096]{1,0:T(8,128)(2,1)S(1)}, bf16[256,4096]{1,0:T(8,128)(2,1)}, u32[]{:S(2)}) copy-start(bf16[256,4096]{1,0:T(8,128)(2,1)} %design_ref.1) | copy-start | bytes 6291460
  1.6 0.7 copy-start.1
  2.3 0.7 copy-start.2
  3.0 0.7 copy-start.3
  8.8 4.9 %collective-permute-start = (bf16[2048,256]{1,0:T(8,128)(2,1)S(1)}, bf16[2048,256]{1,0:T(8,128)(2,1)S(1)}, u32[]{:S(2)}, u32[]{:S(2)}) collective-permute-start(bf16[2048,256]{1,0:T(8,128)(2,1)S(1)} %get-tuple-element.51.own_low.refs_0_), channel_id=1, source_target_pairs={{0,1},{1,0},{2,3},{3,2},{4,5},{5,4},{6,7},{7,6},{8,9},{9,8},{10,11... | collective-permute-start | bytes 3145736 | tf_op jit(solution)/shard_map/ppermute | solution.py:394
  12.3 3.5 %collective-permute-start.1 = (bf16[2048,256]{1,0:T(8,128)(2,1)S(1)}, bf16[2048,256]{1,0:T(8,128)(2,1)}, u32[]{:S(2)}, u32[]{:S(2)}) collective-permute-start(bf16[2048,256]{1,0:T(8,128)(2,1)S(1)} %shard_map.56.own_high.refs_1_), channel_id=1, source_target_pairs={{0,1},{1,0},{2,3},{3,2},{4,5},{5,4},{6,7},{7,6},{8,9},{9,8},{10,11... | collective-permute-start | bytes 3145736 | tf_op jit(solution)/shard_map/ppermute | solution.py:395
  20.1 13.4 %collective-permute-start.2 = (bf16[1296,256]{1,0:T(8,128)(2,1)S(1)}, bf16[1296,256]{1,0:T(8,128)(2,1)S(1)}, u32[]{:S(2)}, u32[]{:S(2)}) collective-permute-start(bf16[1296,256]{1,0:T(8,128)(2,1)S(1)} %get-tuple-element.64), channel_id=1, source_target_pairs={{0,8},{1,25},{2,10},{3,27},{4,12},{5,29},{6,14},{7,31},{8,16},{9,1... | collective-permute-start | bytes 1990664 | tf_op jit(solution)/shard_map/ppermute | solution.py:383
  25.0 12.6 %collective-permute-start.4 = (bf16[8,176,256]{2,1,0:T(8,128)(2,1)S(1)}, bf16[8,176,256]{2,1,0:T(8,128)(2,1)S(1)}, u32[]{:S(2)}, u32[]{:S(2)}) collective-permute-start(bf16[8,176,256]{2,1,0:T(8,128)(2,1)S(1)} %get-tuple-element.67), channel_id=1, source_target_pairs={{0,6},{1,97},{2,0},{3,99},{4,2},{5,101},{6,4},{7,103},{8,14},{9,10... | collective-permute-start | bytes 2162696 | tf_op jit(solution)/shard_map/ppermute | solution.py:383
  25.9 11.7 %collective-permute-start.3 = (bf16[8,176,256]{2,1,0:T(8,128)(2,1)S(1)}, bf16[8,176,256]{2,1,0:T(8,128)(2,1)S(1)}, u32[]{:S(2)}, u32[]{:S(2)}) collective-permute-start(bf16[8,176,256]{2,1,0:T(8,128)(2,1)S(1)} %get-tuple-element.57), channel_id=1, source_target_pairs={{0,2},{1,33},{2,4},{3,35},{4,6},{5,37},{6,0},{7,39},{8,10},{9,41},... | collective-permute-start | bytes 2162696 | tf_op jit(solution)/shard_map/ppermute | solution.py:383
  30.2 15.1 %collective-permute-start.6 = (bf16[8,176,256]{2,1,0:T(8,128)(2,1)S(1)}, bf16[8,176,256]{2,1,0:T(8,128)(2,1)S(1)}, u32[]{:S(2)}, u32[]{:S(2)}) collective-permute-start(bf16[8,176,256]{2,1,0:T(8,128)(2,1)S(1)} %get-tuple-element.69), channel_id=1, source_target_pairs={{0,6},{1,97},{2,0},{3,99},{4,2},{5,101},{6,4},{7,103},{8,14},{9,10... | collective-permute-start | bytes 2162696 | tf_op jit(solution)/shard_map/ppermute | solution.py:383
  30.9 14.4 %collective-permute-start.5 = (bf16[8,176,256]{2,1,0:T(8,128)(2,1)S(1)}, bf16[8,176,256]{2,1,0:T(8,128)(2,1)S(1)}, u32[]{:S(2)}, u32[]{:S(2)}) collective-permute-start(bf16[8,176,256]{2,1,0:T(8,128)(2,1)S(1)} %get-tuple-element.60), channel_id=1, source_target_pairs={{0,2},{1,33},{2,4},{3,35},{4,6},{5,37},{6,0},{7,39},{8,10},{9,41},... | collective-permute-start | bytes 2162696 | tf_op jit(solution)/shard_map/ppermute | solution.py:383
  35.3 12.0 %collective-permute-start.7 = (bf16[1296,256]{1,0:T(8,128)(2,1)S(1)}, bf16[1296,256]{1,0:T(8,128)(2,1)S(1)}, u32[]{:S(2)}, u32[]{:S(2)}) collective-permute-start(bf16[1296,256]{1,0:T(8,128)(2,1)S(1)} %shard_map.61), channel_id=1, source_target_pairs={{0,8},{1,25},{2,10},{3,27},{4,12},{5,29},{6,14},{7,31},{8,16},{9,1... | collective-permute-start | bytes 1990664 | tf_op jit(solution)/shard_map/ppermute | solution.py:383
  40.5 12.6 %collective-permute-start.9 = (bf16[8,176,256]{2,1,0:T(8,128)(2,1)S(1)}, bf16[8,176,256]{2,1,0:T(8,128)(2,1)S(1)}, u32[]{:S(2)}, u32[]{:S(2)}) collective-permute-start(bf16[8,176,256]{2,1,0:T(8,128)(2,1)S(1)} %get-tuple-element.76), channel_id=1, source_target_pairs={{0,6},{1,97},{2,0},{3,99},{4,2},{5,101},{6,4},{7,103},{8,14},{9,10... | collective-permute-start | bytes 2162696 | tf_op jit(solution)/shard_map/ppermute | solution.py:383
  40.6 12.5 %collective-permute-start.8 = (bf16[8,176,256]{2,1,0:T(8,128)(2,1)S(1)}, bf16[8,176,256]{2,1,0:T(8,128)(2,1)S(1)}, u32[]{:S(2)}, u32[]{:S(2)}) collective-permute-start(bf16[8,176,256]{2,1,0:T(8,128)(2,1)S(1)} %get-tuple-element.68), channel_id=1, source_target_pairs={{0,2},{1,33},{2,4},{3,35},{4,6},{5,37},{6,0},{7,39},{8,10},{9,41},... | collective-permute-start | bytes 2162696 | tf_op jit(solution)/shard_map/ppermute | solution.py:383
  49.9 13.0 %collective-permute-start.16 = (bf16[1296,256]{1,0:T(8,128)(2,1)S(1)}, bf16[1296,256]{1,0:T(8,128)(2,1)S(1)}, u32[]{:S(2)}, u32[]{:S(2)}) collective-permute-start(bf16[1296,256]{1,0:T(8,128)(2,1)S(1)} %shard_map.63), channel_id=1, source_target_pairs={{0,8},{1,25},{2,10},{3,27},{4,12},{5,29},{6,14},{7,31},{8,16},{9,1... | collective-permute-start | bytes 1990664 | tf_op jit(solution)/shard_map/ppermute | solution.py:383
  55.9 12.5 %collective-permute-start.10 = (bf16[4,176,256]{2,1,0:T(8,128)(2,1)S(1)}, bf16[4,176,256]{2,1,0:T(8,128)(2,1)S(1)}, u32[]{:S(2)}, u32[]{:S(2)}) collective-permute-start(bf16[4,176,256]{2,1,0:T(8,128)(2,1)S(1)} %get-tuple-element.78), channel_id=1, source_target_pairs={{0,64},{1,17},{2,66},{3,19},{4,68},{5,21},{6,70},{7,23},{8,72},{9,... | collective-permute-start | bytes 1081352 | tf_op jit(solution)/shard_map/ppermute | solution.py:383
  59.7 9.3 %collective-permute-start.11 = (bf16[4,176,256]{2,1,0:T(8,128)(2,1)S(1)}, bf16[4,176,256]{2,1,0:T(8,128)(2,1)S(1)}, u32[]{:S(2)}, u32[]{:S(2)}) collective-permute-start(bf16[4,176,256]{2,1,0:T(8,128)(2,1)S(1)} %get-tuple-element.79), channel_id=1, source_target_pairs={{0,32},{1,9},{2,34},{3,11},{4,36},{5,13},{6,38},{7,15},{8,40},{9,1... | collective-permute-start | bytes 1081352 | tf_op jit(solution)/shard_map/ppermute | solution.py:383
  60.8 9.3 %collective-permute-start.12 = (bf16[4,176,256]{2,1,0:T(8,128)(2,1)S(1)}, bf16[4,176,256]{2,1,0:T(8,128)(2,1)S(1)}, u32[]{:S(2)}, u32[]{:S(2)}) collective-permute-start(bf16[4,176,256]{2,1,0:T(8,128)(2,1)S(1)} %get-tuple-element.80), channel_id=1, source_target_pairs={{0,96},{1,25},{2,98},{3,27},{4,100},{5,29},{6,102},{7,31},{8,104},... | collective-permute-start | bytes 1081352 | tf_op jit(solution)/shard_map/ppermute | solution.py:383
  65.8 9.8 %collective-permute-start.17 = (bf16[336,256]{1,0:T(8,128)(2,1)S(1)}, bf16[336,256]{1,0:T(8,128)(2,1)S(1)}, u32[]{:S(2)}, u32[]{:S(2)}) collective-permute-start(bf16[336,256]{1,0:T(8,128)(2,1)S(1)} %get-tuple-element.87), channel_id=1, source_target_pairs={{0,4},{1,5},{2,6},{3,7},{4,0},{5,1},{6,2},{7,3},{8,12},{9,13},{10,... | collective-permute-start | bytes 516104 | tf_op jit(solution)/shard_map/ppermute | solution.py:383
  70.2 17.8 %collective-permute-start.13 = (f32[176,256]{1,0:T(8,128)S(1)}, f32[176,256]{1,0:T(8,128)S(1)}, u32[]{:S(2)}, u32[]{:S(2)}) collective-permute-start(f32[176,256]{1,0:T(8,128)S(1)} %get-tuple-element.82), channel_id=1, source_target_pairs={{0,16},{1,5},{2,18},{3,7},{4,20},{5,1},{6,22},{7,3},{8,24},{9,13},... | collective-permute-start | bytes 540680 | tf_op jit(solution)/shard_map/ppermute | solution.py:383
  72.4 8.0 %collective-permute-start.18 = (bf16[336,256]{1,0:T(8,128)(2,1)S(1)}, bf16[336,256]{1,0:T(8,128)(2,1)S(1)}, u32[]{:S(2)}, u32[]{:S(2)}) collective-permute-start(bf16[336,256]{1,0:T(8,128)(2,1)S(1)} %get-tuple-element.88), channel_id=1, source_target_pairs={{0,2},{1,7},{2,4},{3,1},{4,6},{5,3},{6,0},{7,5},{8,10},{9,15},{10,... | collective-permute-start | bytes 516104 | tf_op jit(solution)/shard_map/ppermute | solution.py:383
  75.6 7.5 %collective-permute-start.19 = (bf16[336,256]{1,0:T(8,128)(2,1)S(1)}, bf16[336,256]{1,0:T(8,128)(2,1)S(1)}, u32[]{:S(2)}, u32[]{:S(2)}) collective-permute-start(bf16[336,256]{1,0:T(8,128)(2,1)S(1)} %get-tuple-element.89), channel_id=1, source_target_pairs={{0,6},{1,3},{2,0},{3,5},{4,2},{5,7},{6,4},{7,1},{8,14},{9,11},{10,... | collective-permute-start | bytes 516104 | tf_op jit(solution)/shard_map/ppermute | solution.py:383
  75.6 15.7 %collective-permute-start.14 = (f32[176,256]{1,0:T(8,128)S(1)}, f32[176,256]{1,0:T(8,128)S(1)}, u32[]{:S(2)}, u32[]{:S(2)}) collective-permute-start(f32[176,256]{1,0:T(8,128)S(1)} %get-tuple-element.83), channel_id=1, source_target_pairs={{0,8},{1,3},{2,10},{3,5},{4,12},{5,7},{6,14},{7,1},{8,16},{9,11},{... | collective-permute-start | bytes 540680 | tf_op jit(solution)/shard_map/ppermute | solution.py:383
  75.6 15.7 %collective-permute-start.15 = (f32[176,256]{1,0:T(8,128)S(1)}, f32[176,256]{1,0:T(8,128)S(1)}, u32[]{:S(2)}, u32[]{:S(2)}) collective-permute-start(f32[176,256]{1,0:T(8,128)S(1)} %get-tuple-element.84), channel_id=1, source_target_pairs={{0,24},{1,7},{2,26},{3,1},{4,28},{5,3},{6,30},{7,5},{8,0},{9,15},{... | collective-permute-start | bytes 540680 | tf_op jit(solution)/shard_map/ppermute | solution.py:383
  83.2 8.5 %collective-permute-start.20 = (f32[88,256]{1,0:T(8,128)S(1)}, f32[88,256]{1,0:T(8,128)S(1)}, u32[]{:S(2)}, u32[]{:S(2)}) collective-permute-start(f32[88,256]{1,0:T(8,128)S(1)} %get-tuple-element.91), channel_id=1, source_target_pairs={{0,64},{1,65},{2,66},{3,67},{4,68},{5,69},{6,70},{7,71},{8,72},{9,... | collective-permute-start | bytes 270344 | tf_op jit(solution)/shard_map/ppermute | solution.py:383
  88.0 6.5 %collective-permute-start.21 = (f32[88,256]{1,0:T(8,128)S(1)}, f32[88,256]{1,0:T(8,128)S(1)}, u32[]{:S(2)}, u32[]{:S(2)}) collective-permute-start(f32[88,256]{1,0:T(8,128)S(1)} %get-tuple-element.92), channel_id=1, source_target_pairs={{0,32},{1,97},{2,34},{3,99},{4,36},{5,101},{6,38},{7,103},{8,40},{... | collective-permute-start | bytes 270344 | tf_op jit(solution)/shard_map/ppermute | solution.py:383
  88.0 6.5 %collective-permute-start.22 = (f32[88,256]{1,0:T(8,128)S(1)}, f32[88,256]{1,0:T(8,128)S(1)}, u32[]{:S(2)}, u32[]{:S(2)}) collective-permute-start(f32[88,256]{1,0:T(8,128)S(1)} %get-tuple-element.93), channel_id=1, source_target_pairs={{0,96},{1,33},{2,98},{3,35},{4,100},{5,37},{6,102},{7,39},{8,104},... | collective-permute-start | bytes 270344 | tf_op jit(solution)/shard_map/ppermute | solution.py:383
  91.3 9.1 %collective-permute-start.23 = (bf16[176,256]{1,0:T(8,128)(2,1)S(1)}, bf16[176,256]{1,0:T(8,128)(2,1)S(1)}, u32[]{:S(2)}, u32[]{:S(2)}) collective-permute-start(bf16[176,256]{1,0:T(8,128)(2,1)S(1)} %get-tuple-element.95), channel_id=1, source_target_pairs={{0,8},{1,16},{2,32},{3,48},{4,64},{5,80},{6,96},{7,112},{8,0},{9,2... | collective-permute-start | bytes 270344 | tf_op jit(solution)/shard_map/ppermute | solution.py:383
  94.6 8.3 %collective-permute-start.24 = (bf16[80,256]{1,0:T(8,128)(2,1)S(1)}, bf16[80,256]{1,0:T(8,128)(2,1)S(1)}, u32[]{:S(2)}, u32[]{:S(2)}) collective-permute-start(bf16[80,256]{1,0:T(8,128)(2,1)S(1)} %get-tuple-element.96), channel_id=1, source_target_pairs={{0,8},{1,16},{2,32},{3,48},{4,64},{5,80},{6,96},{7,112},{8,0},{9,2... | collective-permute-start | bytes 122888 | tf_op jit(solution)/shard_map/ppermute | solution.py:383

commit v5 on v4

--- a/solution.py
+++ b/solution.py
@@ -14,6 +14,7 @@
 MAIN = 176
 REST = BLK - MAIN
 GRANT_FIRST = 24
+WEIGHT = 20
 EXTRA = 16
 BF = jnp.bfloat16
 F32 = jnp.float32
@@ -319,6 +320,30 @@
     )(*operands)
 
 
+def add_kernel(own, got, out):
+    out[...] = (own[...] + got[...].astype(F32)).astype(out.dtype)
+
+
+def home_kernel(*refs):
+    homes, (got_3p, got_2m, got_2p, got_3m), outs = refs[:4], refs[4:8], refs[8:]
+    for d, (home, out) in enumerate(zip(homes, outs)):
+        one, two = (got_3p, got_2m) if d < 2 else (got_2p, got_3m)
+        half = pl.ds(4 * (d % 2), 4)
+        out[...] = (home[...] + one[half].astype(F32) + two[half].astype(F32)).astype(out.dtype)
+
+
+def home_rest_kernel(*refs):
+    homes, got, outs = refs[:4], refs[4], refs[5:]
+    quarter = homes[0].shape[0] - EXTRA
+    for d, (home, out) in enumerate(zip(homes, outs)):
+        out[pl.ds(0, quarter), :] = (
+            home[pl.ds(0, quarter), :] + got[pl.ds(d * quarter, quarter), :].astype(F32)
+        ).astype(out.dtype)
+        out[pl.ds(quarter, EXTRA), :] = (
+            home[pl.ds(quarter, EXTRA), :] + got[pl.ds(4 * quarter, EXTRA), :].astype(F32)
+        ).astype(out.dtype)
+
+
 def main_sum_kernel(own, second, first, third, *outs):
     for d, out in enumerate(outs):
         total = own[d]
@@ -349,26 +374,23 @@
 
 
 def finish_kernel(state, scale, main_ref, rest_ref, got_main_ref, got_rest_ref, out_ref):
-    s, fold = state[0], state[1] == 1
-    here = jnp.concatenate([main_ref[...], rest_ref[0:REST, :]], axis=0)
-    got = jnp.concatenate([got_main_ref[...].astype(F32), got_rest_ref[...].astype(F32)], axis=0).T
-    mine = here.T
-    i = lax.broadcasted_iota(jnp.int32, (BLK, BLK), 0)
-    j = lax.broadcasted_iota(jnp.int32, (BLK, BLK), 1)
-    on = jnp.logical_and(fold, i == j)
-    low = jnp.logical_or(jnp.logical_not(fold), i >= j)
-    first = jnp.where(low, here, mine) * scale
-    second = jnp.where(on, rest_ref[REST : REST + 1, :], jnp.where(low, got, here)) * scale
-
-    @pl.when(s == 0)
+    s, fold = state[0], state[1]
+    here = jnp.concatenate([main_ref[...], rest_ref[0:REST, :]], axis=0) * scale
+    got = jnp.concatenate([got_main_ref[...], got_rest_ref[...]], axis=0).T.astype(F32) * scale
+    first_at, second_at = pl.multiple_of(s * BLK, BLK), pl.multiple_of((1 - s) * BLK, BLK)
+
+    @pl.when(fold == 0)
     def _():
-        out_ref[:, 0:BLK] = first
-        out_ref[:, BLK : 2 * BLK] = second
-
-    @pl.when(s == 1)
+        out_ref[:, pl.ds(first_at, BLK)] = here
+        out_ref[:, pl.ds(second_at, BLK)] = got
+
+    @pl.when(fold == 1)
     def _():
-        out_ref[:, BLK : 2 * BLK] = first
-        out_ref[:, 0:BLK] = second
+        i = lax.broadcasted_iota(jnp.int32, (BLK, BLK), 0)
+        j = lax.broadcasted_iota(jnp.int32, (BLK, BLK), 1)
+        cross = rest_ref[REST : REST + 1, :] * scale
+        out_ref[:, pl.ds(first_at, BLK)] = jnp.where(i >= j, here, here.T)
+        out_ref[:, pl.ds(second_at, BLK)] = jnp.where(i == j, cross, jnp.where(i > j, got, here))
 
 
 def local(design, weight, counts, column_map):
@@ -422,12 +444,12 @@
     plan_2 = [blocks(M, 1, minus), blocks(M, 3, plus)]
     plan_2r = [blocks(R, 2, every, (0, 0))]
     plan_3 = [blocks(M, 1, plus, (0, 0)), blocks(M, 3, minus, (1, 0))]
-    plan_3r = [blocks(R, 1, every, (0, 0))]
+    plan_3r = [blocks(R, 1, every)]
     plan_4 = [
-        blocks(M, 0, every[4 * d : 4 * d + 4], (2 * (d // 2), 4 * (d % 2)), (2 * (d // 2) + 1, 4 * (d % 2)))
+        blocks(M, 0, every[4 * d : 4 * d + 4])
         for d in range(4)
     ]
-    plan_4r = [blocks(R, 0, every[4 * d : 4 * d + 4], (0, 4 * d)) for d in range(4)]
+    plan_4r = [blocks(R, 0, every[4 * d : 4 * d + 4]) for d in range(4)]
     device = ((place["z"] * 4 + place["y"]) * 4 + place["x"]) * 2 + core
     table = lax.dynamic_index_in_dim(
         jnp.asarray(np.concatenate(tables, axis=1)), device, 0, keepdims=False
@@ -451,11 +473,17 @@
     got_3p = move(relay_p, main_to(0, 1))
     got_3m = move(relay_m, main_to(0, -1))
     both, relay_p, got_2p, got_2m = lax.optimization_barrier((both, relay_p, got_2p, got_2m))
-    (ring,) = products(both, table, plan_3r, (BF,), cross, terms=(got_r,), weight=60)
+    (line,) = products(both, table, plan_3r, (F32,), cross, weight=WEIGHT)
+    (ring,) = call_sum(add_kernel, [(line.shape, BF)], line, got_r)
     got_r = move(ring, rest_to(0, 1))
     both, ring = lax.optimization_barrier((both, ring))
-    part = products(both, table, plan_4, (F32, BF, BF, BF), terms=(got_3p, got_2m, got_2p, got_3m))
-    rest = products(both, table, plan_4r, (F32, BF, BF, BF), cross, terms=(got_r,))
+    home = products(both, table, plan_4, (F32,) * 4, weight=WEIGHT)
+    both, home = lax.optimization_barrier((both, home))
+    line = products(both, table, plan_4r, (F32,) * 4, cross, weight=WEIGHT)
+    part = call_sum(
+        home_kernel, [(h.shape, F32 if d == 0 else BF) for d, h in enumerate(home)], *home, got_3p, got_2m, got_2p, got_3m
+    )
+    rest = call_sum(home_rest_kernel, [(h.shape, F32 if d == 0 else BF) for d, h in enumerate(line)], *line, got_r)
 
     got = [move(part[d], main_to(1, d)) for d in (2, 1, 3)]
     got_r = [move(rest[d], rest_to(1, d)) for d in (2, 1, 3)]

time: 105 us -> 100 us (0.952)
  starting transfers between devices: 44.3 us -> 36.5 us
  waiting for transfers between devices: 21.4 us -> 24.1 us
    ppermute x23, starting transfers between devices: 43.7 us -> 35.9 us  [move(): return lax.ppermute(array, AXES, pairs)]
    ppermute x23, waiting for transfers between devices: 21.4 us -> 24.1 us  [move(): return lax.ppermute(array, AXES, pairs)]
  transfers between devices with their start and end apart: 25 -> 25, of which waited for: 11 -> 15; matrix products, arithmetic and copies ran while one was open for 1% -> 1% of each run, Pallas kernels for 22% -> 24%
where the time goes in v5:
time: 100 us; the launch traced here: 99.7 us
  starting transfers between devices  36.5 us (36%)
  Pallas kernels  34.5 us (34%)
  waiting for transfers between devices  24.1 us (24%)
  local copies, waits for them, and re-layouts  4.38 us (4%)
    ppermute x23, starting transfers between devices, move(): return lax.ppermute(array, AXES, pairs)  35.9 us
    ppermute x23, waiting for transfers between devices, move(): return lax.ppermute(array, AXES, pairs)  24.1 us
    pallas_call x8, Pallas kernels, products(): pl.pallas_call(functools.partial(product_kernel, plan, opening, cross_mad...  21.4 us
    pallas_call x1, Pallas kernels, scaled_rows(): pl.pallas_call(first_pick_kernel, out_shape=[jax.ShapeDtypeStruct((2 * un...  5.13 us
    unnamed x8, local copies, waits for them, and re-layouts  3.64 us
    pallas_call x1, Pallas kernels, scaled_rows(): pl.pallas_call(second_pick_kernel, out_shape=part, in_specs=[smem, vmem],...  3.44 us
    pallas_call x1, Pallas kernels, local(): pl.pallas_call(turn_kernel, out_shape=[jax.ShapeDtypeStruct((half[1], 2 *...  2.16 us
  transfers between devices with their start and end apart: 25, of which 15 were waited for; matrix products, arithmetic and copies ran while one was open for 1% of the time, Pallas kernels for 24%

profile of v5, /device:TPU:6, one launch (start us, length us, event | category | flops | bytes accessed | tf_op | source)
XLA Modules:
  0.0 99.7 jit_solution(3275591029477951182)
XLA Ops:
  0.0 1.6 %copy-done = bf16[256,4096]{1,0:T(8,128)(2,1)S(1)} copy-done((bf16[256,4096]{1,0:T(8,128)(2,1)S(1)}, bf16[256,4096]{1,0:T(8,128)(2,1)}, u32[]{:S(2)}) %copy-start) | copy-done | bytes 2097176
  1.6 0.7 copy-done.1
  2.3 0.7 copy-done.2
  3.0 0.7 copy-done.3
  3.6 5.1 %shard_map.55 = (f32[8192,128]{1,0:T(8,128)S(1)}, bf16[2048,256]{1,0:T(8,128)(2,1)S(1)}) custom-call(s32[4096]{0:T(1024)S(1)} %copy-done.1, s32[8]{0:T(128)S(1)} %copy-done.3, f32[1,256]{1,0:T(1,128)S(1)} %bitcast.3, bf16[256,4096]{1,0:T(8,128)(2,1)S(1)} %copy-done), custom_call_target="tpu_custom_call" | custom-call | bytes 8388608 | tf_op jit(solution)/shard_map/pallas_call | solution.py:155
  8.8 0.1 collective-permute-start
  8.9 3.4 %shard_map.56.own_high.refs_1_ = bf16[2048,256]{1,0:T(8,128)(2,1)S(1)} custom-call(s32[4096]{0:T(1024)S(1)} %copy-done.1, f32[8192,128]{1,0:T(8,128)S(1)} %get-tuple-element.66.columns), custom_call_target="tpu_custom_call" | custom-call | bytes 8388608 | tf_op jit(solution)/shard_map/pallas_call | solution.py:164
  12.3 0.6 collective-permute-start.1
  12.9 0.7 dynamic-slice_reduce_fusion.table
  13.6 0.0 collective-permute-done.other_low.refs_2_
  13.7 2.2 %shard_map.57 = (bf16[256,4096]{1,0:T(8,128)(2,1)S(1)}, bf16[256,2048]{1,0:T(8,128)(2,1)S(1)}) custom-call(bf16[2048,256]{1,0:T(8,128)(2,1)S(1)} %get-tuple-element.65.own_low.refs_0_, bf16[2048,256]{1,0:T(8,128)(2,1)S(1)} %shard_map.56.own_high.refs_1_, bf16[2048,256]{1,0:T(8,128)(2,1)S(1)} %collective-permute-done.other_low.refs_2_), custom_call_target="tpu_custom_call" | custom-call | bytes 1048576 | tf_op jit(solution)/shard_map/pallas_call | solution.py:419
  15.8 0.0 collective-permute-done.1.refs_3_
  15.8 4.2 %shard_map.58 = (bf16[1296,256]{1,0:T(8,128)(2,1)S(1)}, f32[16,256]{1,0:T(8,128)S(1)}, bf16[4096,512]{1,0:T(8,128)(2,1)S(1)}, bf16[512,4096]{1,0:T(8,128)(2,1)S(1)}) custom-call(s32[528]{0:T(1024)S(1)} %dynamic-slice_reduce_fusion.table, bf16[2048,256]{1,0:T(8,128)(2,1)S(1)} %get-tuple-element.65.own_low.refs_0_, ...), custom_call_target="tpu_custom_call" | custom-call | bytes 1048576 | tf_op jit(solution)/shard_map/pallas_call | solution.py:300
  20.1 2.5 %collective-permute-start.2 = (bf16[1296,256]{1,0:T(8,128)(2,1)S(1)}, bf16[1296,256]{1,0:T(8,128)(2,1)S(1)}, u32[]{:S(2)}, u32[]{:S(2)}) collective-permute-start(bf16[1296,256]{1,0:T(8,128)(2,1)S(1)} %get-tuple-element.78), channel_id=1, source_target_pairs={{0,8},{1,25},{2,10},{3,27},{4,12},{5,29},{6,14},{7,31},{8,16},{9,1... | collective-permute-start | bytes 1990664 | tf_op jit(solution)/shard_map/ppermute | solution.py:405
  22.6 2.4 %shard_map.59 = (bf16[8,176,256]{2,1,0:T(8,128)(2,1)S(1)}, bf16[8,176,256]{2,1,0:T(8,128)(2,1)S(1)}) custom-call(s32[528]{0:T(1024)S(1)} %dynamic-slice_reduce_fusion.table, bf16[4096,512]{1,0:T(8,128)(2,1)S(1)} %get-tuple-element.108.refs_0_, bf16[512,4096]{1,0:T(8,128)(2,1)S(1)} %get-tuple-element.109.refs_1_), custom_call_target="tpu_custom_call" | custom-call | bytes 1048576 | tf_op jit(solution)/shard_map/pallas_call | solution.py:300
  25.0 0.5 collective-permute-start.3
  25.5 1.5 %collective-permute-start.4 = (bf16[8,176,256]{2,1,0:T(8,128)(2,1)S(1)}, bf16[8,176,256]{2,1,0:T(8,128)(2,1)S(1)}, u32[]{:S(2)}, u32[]{:S(2)}) collective-permute-start(bf16[8,176,256]{2,1,0:T(8,128)(2,1)S(1)} %get-tuple-element.81), channel_id=1, source_target_pairs={{0,6},{1,97},{2,0},{3,99},{4,2},{5,101},{6,4},{7,103},{8,14},{9,10... | collective-permute-start | bytes 2162696 | tf_op jit(solution)/shard_map/ppermute | solution.py:405
  27.1 1.8 %shard_map.60 = (bf16[8,176,256]{2,1,0:T(8,128)(2,1)S(1)}, bf16[8,176,256]{2,1,0:T(8,128)(2,1)S(1)}) custom-call(s32[528]{0:T(1024)S(1)} %dynamic-slice_reduce_fusion.table, bf16[4096,512]{1,0:T(8,128)(2,1)S(1)} %get-tuple-element.108.refs_0_, bf16[512,4096]{1,0:T(8,128)(2,1)S(1)} %get-tuple-element.109.refs_1_), custom_call_target="tpu_custom_call" | custom-call | bytes 1048576 | tf_op jit(solution)/shard_map/pallas_call | solution.py:300
  28.9 1.8 %collective-permute-start.5 = (bf16[8,176,256]{2,1,0:T(8,128)(2,1)S(1)}, bf16[8,176,256]{2,1,0:T(8,128)(2,1)S(1)}, u32[]{:S(2)}, u32[]{:S(2)}) collective-permute-start(bf16[8,176,256]{2,1,0:T(8,128)(2,1)S(1)} %get-tuple-element.74), channel_id=1, source_target_pairs={{0,2},{1,33},{2,4},{3,35},{4,6},{5,37},{6,0},{7,39},{8,10},{9,41},... | collective-permute-start | bytes 2162696 | tf_op jit(solution)/shard_map/ppermute | solution.py:405
  30.7 0.5 collective-permute-start.6
  31.1 0.9 collective-permute-done.2.refs_3_
  32.0 1.8 %shard_map.61 = bf16[1296,256]{1,0:T(8,128)(2,1)S(1)} custom-call(s32[528]{0:T(1024)S(1)} %dynamic-slice_reduce_fusion.table, bf16[4096,512]{1,0:T(8,128)(2,1)S(1)} %get-tuple-element.108.refs_0_, bf16[512,4096]{1,0:T(8,128)(2,1)S(1)} %get-tuple-element.109.refs_1_, f32[16,256]{1,0:T(8,128)S(1)} %get-tuple-element.77.refs_2_, ...), custom_call_target="tpu_custom_call" | custom-call | bytes 1048576 | tf_op jit(solution)/shard_map/pallas_call | solution.py:300
  33.8 1.3 %collective-permute-start.7 = (bf16[1296,256]{1,0:T(8,128)(2,1)S(1)}, bf16[1296,256]{1,0:T(8,128)(2,1)S(1)}, u32[]{:S(2)}, u32[]{:S(2)}) collective-permute-start(bf16[1296,256]{1,0:T(8,128)(2,1)S(1)} %shard_map.61), channel_id=1, source_target_pairs={{0,8},{1,25},{2,10},{3,27},{4,12},{5,29},{6,14},{7,31},{8,16},{9,1... | collective-permute-start | bytes 1990664 | tf_op jit(solution)/shard_map/ppermute | solution.py:405
  35.1 1.2 %collective-permute-done.3.refs_2_ = bf16[8,176,256]{2,1,0:T(8,128)(2,1)S(1)} collective-permute-done((bf16[8,176,256]{2,1,0:T(8,128)(2,1)S(1)}, bf16[8,176,256]{2,1,0:T(8,128)(2,1)S(1)}, u32[]{:S(2)}, u32[]{:S(2)}) %collective-permute-start.3) | collective-permute-done | bytes 720928 | tf_op jit(solution)/shard_map/ppermute | solution.py:405
  36.3 1.7 %collective-permute-done.4.refs_3_ = bf16[8,176,256]{2,1,0:T(8,128)(2,1)S(1)} collective-permute-done((bf16[8,176,256]{2,1,0:T(8,128)(2,1)S(1)}, bf16[8,176,256]{2,1,0:T(8,128)(2,1)S(1)}, u32[]{:S(2)}, u32[]{:S(2)}) %collective-permute-start.4) | collective-permute-done | bytes 720928 | tf_op jit(solution)/shard_map/ppermute | solution.py:405
  38.0 2.9 %shard_map.62 = (bf16[8,176,256]{2,1,0:T(8,128)(2,1)S(1)}, bf16[8,176,256]{2,1,0:T(8,128)(2,1)S(1)}) custom-call(s32[528]{0:T(1024)S(1)} %dynamic-slice_reduce_fusion.table, bf16[4096,512]{1,0:T(8,128)(2,1)S(1)} %get-tuple-element.108.refs_0_, bf16[512,4096]{1,0:T(8,128)(2,1)S(1)} %get-tuple-element.109.refs_1_, ...), custom_call_target="tpu_custom_call" | custom-call | bytes 1048576 | tf_op jit(solution)/shard_map/pallas_call | solution.py:300
  41.0 0.4 collective-permute-start.8
  41.3 1.7 %collective-permute-start.9 = (bf16[8,176,256]{2,1,0:T(8,128)(2,1)S(1)}, bf16[8,176,256]{2,1,0:T(8,128)(2,1)S(1)}, u32[]{:S(2)}, u32[]{:S(2)}) collective-permute-start(bf16[8,176,256]{2,1,0:T(8,128)(2,1)S(1)} %get-tuple-element.98), channel_id=1, source_target_pairs={{0,6},{1,97},{2,0},{3,99},{4,2},{5,101},{6,4},{7,103},{8,14},{9,10... | collective-permute-start | bytes 2162696 | tf_op jit(solution)/shard_map/ppermute | solution.py:405
  43.1 1.0 collective-permute-done.5.refs_6_
  44.1 1.7 %collective-permute-done.6.refs_5_ = bf16[8,176,256]{2,1,0:T(8,128)(2,1)S(1)} collective-permute-done((bf16[8,176,256]{2,1,0:T(8,128)(2,1)S(1)}, bf16[8,176,256]{2,1,0:T(8,128)(2,1)S(1)}, u32[]{:S(2)}, u32[]{:S(2)}) %collective-permute-start.6) | collective-permute-done | bytes 720928 | tf_op jit(solution)/shard_map/ppermute | solution.py:405
  45.7 2.6 %shard_map.63.own = f32[1296,256]{1,0:T(8,128)S(1)} custom-call(s32[528]{0:T(1024)S(1)} %dynamic-slice_reduce_fusion.table, bf16[4096,512]{1,0:T(8,128)(2,1)S(1)} %get-tuple-element.108.refs_0_, bf16[512,4096]{1,0:T(8,128)(2,1)S(1)} %get-tuple-element.109.refs_1_, f32[16,256]{1,0:T(8,128)S(1)} %get-tuple-element.77.refs_2_), custom_call_target="tpu_custom_call" | custom-call | bytes 20971520 | tf_op jit(solution)/shard_map/pallas_call | solution.py:300
  48.4 0.1 shard_map.64
  48.5 0.8 collective-permute-start.16
  49.3 2.7 %shard_map.65 = (f32[4,176,256]{2,1,0:T(8,128)S(1)}, f32[4,176,256]{2,1,0:T(8,128)S(1)}, f32[4,176,256]{2,1,0:T(8,128)S(1)}, f32[4,176,256]{2,1,0:T(8,128)S(1)}) custom-call(s32[528]{0:T(1024)S(1)} %dynamic-slice_reduce_fusion.table, bf16[4096,512]{1,0:T(8,128)(2,1)S(1)} %get-tuple-element.108.refs_0_, bf16[512,4096]{1,0:T(8,128)(2,1)S(1)} %get-tuple-element.109.refs_1_), custom_call_target="tpu_custom_call" | custom-call | bytes 20971520 | tf_op jit(solution)/shard_map/pallas_call | solution.py:300
  52.0 0.3 collective-permute-done.8.refs_4_
  52.3 1.5 %collective-permute-done.9.refs_7_ = bf16[8,176,256]{2,1,0:T(8,128)(2,1)S(1)} collective-permute-done((bf16[8,176,256]{2,1,0:T(8,128)(2,1)S(1)}, bf16[8,176,256]{2,1,0:T(8,128)(2,1)S(1)}, u32[]{:S(2)}, u32[]{:S(2)}) %collective-permute-start.9) | collective-permute-done | bytes 720928 | tf_op jit(solution)/shard_map/ppermute | solution.py:405
  53.8 0.4 shard_map.66
  54.3 3.6 %collective-permute-start.10 = (bf16[4,176,256]{2,1,0:T(8,128)(2,1)S(1)}, bf16[4,176,256]{2,1,0:T(8,128)(2,1)S(1)}, u32[]{:S(2)}, u32[]{:S(2)}) collective-permute-start(bf16[4,176,256]{2,1,0:T(8,128)(2,1)S(1)} %get-tuple-element.100), channel_id=1, source_target_pairs={{0,64},{1,17},{2,66},{3,19},{4,68},{5,21},{6,70},{7,23},{8,72},{9,... | collective-permute-start | bytes 1081352 | tf_op jit(solution)/shard_map/ppermute | solution.py:405
  57.8 1.2 %collective-permute-start.11 = (bf16[4,176,256]{2,1,0:T(8,128)(2,1)S(1)}, bf16[4,176,256]{2,1,0:T(8,128)(2,1)S(1)}, u32[]{:S(2)}, u32[]{:S(2)}) collective-permute-start(bf16[4,176,256]{2,1,0:T(8,128)(2,1)S(1)} %get-tuple-element.101), channel_id=1, source_target_pairs={{0,32},{1,9},{2,34},{3,11},{4,36},{5,13},{6,38},{7,15},{8,40},{9,1... | collective-permute-start | bytes 1081352 | tf_op jit(solution)/shard_map/ppermute | solution.py:405
  59.0 2.0 %collective-permute-start.12 = (bf16[4,176,256]{2,1,0:T(8,128)(2,1)S(1)}, bf16[4,176,256]{2,1,0:T(8,128)(2,1)S(1)}, u32[]{:S(2)}, u32[]{:S(2)}) collective-permute-start(bf16[4,176,256]{2,1,0:T(8,128)(2,1)S(1)} %get-tuple-element.102), channel_id=1, source_target_pairs={{0,96},{1,25},{2,98},{3,27},{4,100},{5,29},{6,102},{7,31},{8,104},... | collective-permute-start | bytes 1081352 | tf_op jit(solution)/shard_map/ppermute | solution.py:405
  61.1 2.8 %shard_map.69 = (f32[336,256]{1,0:T(8,128)S(1)}, f32[336,256]{1,0:T(8,128)S(1)}, f32[336,256]{1,0:T(8,128)S(1)}, f32[336,256]{1,0:T(8,128)S(1)}) custom-call(s32[528]{0:T(1024)S(1)} %dynamic-slice_reduce_fusion.table, bf16[4096,512]{1,0:T(8,128)(2,1)S(1)} %get-tuple-element.108.refs_0_, bf16[512,4096]{1,0:T(8,128)(2,1)S(1)} %get-tuple-element.109.refs_1_, ...), custom_call_target="tpu_custom_call" | custom-call | bytes 20971520 | tf_op jit(solution)/shard_map/pallas_call | solution.py:300
  63.9 2.2 %collective-permute-done.16.refs_4_ = bf16[1296,256]{1,0:T(8,128)(2,1)S(1)} collective-permute-done((bf16[1296,256]{1,0:T(8,128)(2,1)S(1)}, bf16[1296,256]{1,0:T(8,128)(2,1)S(1)}, u32[]{:S(2)}, u32[]{:S(2)}) %collective-permute-start.16) | collective-permute-done | bytes 663584 | tf_op jit(solution)/shard_map/ppermute | solution.py:405
  66.1 0.1 shard_map.70
  66.2 1.2 %collective-permute-start.17 = (bf16[336,256]{1,0:T(8,128)(2,1)S(1)}, bf16[336,256]{1,0:T(8,128)(2,1)S(1)}, u32[]{:S(2)}, u32[]{:S(2)}) collective-permute-start(bf16[336,256]{1,0:T(8,128)(2,1)S(1)} %get-tuple-element.115), channel_id=1, source_target_pairs={{0,4},{1,5},{2,6},{3,7},{4,0},{5,1},{6,2},{7,3},{8,12},{9,13},{10,... | collective-permute-start | bytes 516104 | tf_op jit(solution)/shard_map/ppermute | solution.py:405
  67.4 0.9 collective-permute-done.12.third
  68.3 0.1 shard_map.67
  68.4 2.1 %collective-permute-start.13 = (f32[176,256]{1,0:T(8,128)S(1)}, f32[176,256]{1,0:T(8,128)S(1)}, u32[]{:S(2)}, u32[]{:S(2)}) collective-permute-start(f32[176,256]{1,0:T(8,128)S(1)} %get-tuple-element.104), channel_id=1, source_target_pairs={{0,16},{1,5},{2,18},{3,7},{4,20},{5,1},{6,22},{7,3},{8,24},{9,13},... | collective-permute-start | bytes 540680 | tf_op jit(solution)/shard_map/ppermute | solution.py:405
  70.6 0.1 collective-permute-start.18
  70.7 1.9 %collective-permute-start.19 = (bf16[336,256]{1,0:T(8,128)(2,1)S(1)}, bf16[336,256]{1,0:T(8,128)(2,1)S(1)}, u32[]{:S(2)}, u32[]{:S(2)}) collective-permute-start(bf16[336,256]{1,0:T(8,128)(2,1)S(1)} %get-tuple-element.117), channel_id=1, source_target_pairs={{0,6},{1,3},{2,0},{3,5},{4,2},{5,7},{6,4},{7,1},{8,14},{9,11},{10,... | collective-permute-start | bytes 516104 | tf_op jit(solution)/shard_map/ppermute | solution.py:405
  72.6 1.6 %collective-permute-done.17.second = bf16[336,256]{1,0:T(8,128)(2,1)S(1)} collective-permute-done((bf16[336,256]{1,0:T(8,128)(2,1)S(1)}, bf16[336,256]{1,0:T(8,128)(2,1)S(1)}, u32[]{:S(2)}, u32[]{:S(2)}) %collective-permute-start.17) | collective-permute-done | bytes 172064 | tf_op jit(solution)/shard_map/ppermute | solution.py:405
  74.2 1.7 %collective-permute-start.15 = (f32[176,256]{1,0:T(8,128)S(1)}, f32[176,256]{1,0:T(8,128)S(1)}, u32[]{:S(2)}, u32[]{:S(2)}) collective-permute-start(f32[176,256]{1,0:T(8,128)S(1)} %get-tuple-element.106), channel_id=1, source_target_pairs={{0,24},{1,7},{2,26},{3,1},{4,28},{5,3},{6,30},{7,5},{8,0},{9,15},{... | collective-permute-start | bytes 540680 | tf_op jit(solution)/shard_map/ppermute | solution.py:405
  75.8 2.0 %collective-permute-done.18.first = bf16[336,256]{1,0:T(8,128)(2,1)S(1)} collective-permute-done((bf16[336,256]{1,0:T(8,128)(2,1)S(1)}, bf16[336,256]{1,0:T(8,128)(2,1)S(1)}, u32[]{:S(2)}, u32[]{:S(2)}) %collective-permute-start.18) | collective-permute-done | bytes 172064 | tf_op jit(solution)/shard_map/ppermute | solution.py:405
  77.9 1.3 %collective-permute-done.19.third = bf16[336,256]{1,0:T(8,128)(2,1)S(1)} collective-permute-done((bf16[336,256]{1,0:T(8,128)(2,1)S(1)}, bf16[336,256]{1,0:T(8,128)(2,1)S(1)}, u32[]{:S(2)}, u32[]{:S(2)}) %collective-permute-start.19) | collective-permute-done | bytes 172064 | tf_op jit(solution)/shard_map/ppermute | solution.py:405
  79.1 0.1 shard_map.71
  79.2 4.7 %collective-permute-start.20 = (f32[88,256]{1,0:T(8,128)S(1)}, f32[88,256]{1,0:T(8,128)S(1)}, u32[]{:S(2)}, u32[]{:S(2)}) collective-permute-start(f32[88,256]{1,0:T(8,128)S(1)} %get-tuple-element.119), channel_id=1, source_target_pairs={{0,64},{1,65},{2,66},{3,67},{4,68},{5,69},{6,70},{7,71},{8,72},{9,... | collective-permute-start | bytes 270344 | tf_op jit(solution)/shard_map/ppermute | solution.py:405
  83.9 1.1 %collective-permute-start.21 = (f32[88,256]{1,0:T(8,128)S(1)}, f32[88,256]{1,0:T(8,128)S(1)}, u32[]{:S(2)}, u32[]{:S(2)}) collective-permute-start(f32[88,256]{1,0:T(8,128)S(1)} %get-tuple-element.120), channel_id=1, source_target_pairs={{0,32},{1,97},{2,34},{3,99},{4,36},{5,101},{6,38},{7,103},{8,40},{... | collective-permute-start | bytes 270344 | tf_op jit(solution)/shard_map/ppermute | solution.py:405
  85.0 2.1 %collective-permute-start.22 = (f32[88,256]{1,0:T(8,128)S(1)}, f32[88,256]{1,0:T(8,128)S(1)}, u32[]{:S(2)}, u32[]{:S(2)}) collective-permute-start(f32[88,256]{1,0:T(8,128)S(1)} %get-tuple-element.121), channel_id=1, source_target_pairs={{0,96},{1,33},{2,98},{3,35},{4,100},{5,37},{6,102},{7,39},{8,104},... | collective-permute-start | bytes 270344 | tf_op jit(solution)/shard_map/ppermute | solution.py:405
  87.2 0.1 collective-permute-start.23
  87.3 2.4 %collective-permute-done.21.first = f32[88,256]{1,0:T(8,128)S(1)} collective-permute-done((f32[88,256]{1,0:T(8,128)S(1)}, f32[88,256]{1,0:T(8,128)S(1)}, u32[]{:S(2)}, u32[]{:S(2)}) %collective-permute-start.21) | collective-permute-done | bytes 90144 | tf_op jit(solution)/shard_map/ppermute | solution.py:405
  89.6 3.1 %collective-permute-start.24 = (bf16[80,256]{1,0:T(8,128)(2,1)S(1)}, bf16[80,256]{1,0:T(8,128)(2,1)S(1)}, u32[]{:S(2)}, u32[]{:S(2)}) collective-permute-start(bf16[80,256]{1,0:T(8,128)(2,1)S(1)} %get-tuple-element.124), channel_id=1, source_target_pairs={{0,8},{1,16},{2,32},{3,48},{4,64},{5,80},{6,96},{7,112},{8,0},{9,2... | collective-permute-start | bytes 122888 | tf_op jit(solution)/shard_map/ppermute | solution.py:405
  92.8 0.1 pad_add_fusion.refs_0_
  92.8 4.9 %collective-permute-done.23.refs_3_ = bf16[176,256]{1,0:T(8,128)(2,1)S(1)} collective-permute-done((bf16[176,256]{1,0:T(8,128)(2,1)S(1)}, bf16[176,256]{1,0:T(8,128)(2,1)S(1)}, u32[]{:S(2)}, u32[]{:S(2)}) %collective-permute-start.23) | collective-permute-done | bytes 90144 | tf_op jit(solution)/shard_map/ppermute | solution.py:405
  97.7 0.6 collective-permute-done.24.refs_4_
  98.3 1.5 %shard_map.73 = f32[256,512]{1,0:T(8,128)} custom-call(s32[2]{0:T(128)S(1)} %pad_add_fusion.refs_0_, f32[176,256]{1,0:T(8,128)S(1)} %get-tuple-element.107.refs_1_, f32[88,256]{1,0:T(8,128)S(1)} %get-tuple-element.122.refs_2_, bf16[176,256]{1,0:T(8,128)(2,1)S(1)} %collective-permute-done.23.refs_3_, bf16[80,256]{1,0:T(8,128)(2,1)S(1)} %collective-permute-done.24.refs_4_), custom_call_target="tpu_custom_call" | custom-call | tf_op jit(solution)/shard_map/pallas_call | solution.py:505
  (15 shorter events, 0.1 us)
Async XLA Ops:
  0.0 1.6 %copy-start = (bf16[256,4096]{1,0:T(8,128)(2,1)S(1)}, bf16[256,4096]{1,0:T(8,128)(2,1)}, u32[]{:S(2)}) copy-start(bf16[256,4096]{1,0:T(8,128)(2,1)} %design_ref.1) | copy-start | bytes 6291460
  1.6 0.7 copy-start.1
  2.3 0.7 copy-start.2
  3.0 0.7 copy-start.3
  8.8 4.9 %collective-permute-start = (bf16[2048,256]{1,0:T(8,128)(2,1)S(1)}, bf16[2048,256]{1,0:T(8,128)(2,1)S(1)}, u32[]{:S(2)}, u32[]{:S(2)}) collective-permute-start(bf16[2048,256]{1,0:T(8,128)(2,1)S(1)} %get-tuple-element.65.own_low.refs_0_), channel_id=1, source_target_pairs={{0,1},{1,0},{2,3},{3,2},{4,5},{5,4},{6,7},{7,6},{8,9},{9,8},{10,11... | collective-permute-start | bytes 3145736 | tf_op jit(solution)/shard_map/ppermute | solution.py:416
  12.3 3.5 %collective-permute-start.1 = (bf16[2048,256]{1,0:T(8,128)(2,1)S(1)}, bf16[2048,256]{1,0:T(8,128)(2,1)}, u32[]{:S(2)}, u32[]{:S(2)}) collective-permute-start(bf16[2048,256]{1,0:T(8,128)(2,1)S(1)} %shard_map.56.own_high.refs_1_), channel_id=1, source_target_pairs={{0,1},{1,0},{2,3},{3,2},{4,5},{5,4},{6,7},{7,6},{8,9},{9,8},{10,11... | collective-permute-start | bytes 3145736 | tf_op jit(solution)/shard_map/ppermute | solution.py:417
  20.1 12.0 %collective-permute-start.2 = (bf16[1296,256]{1,0:T(8,128)(2,1)S(1)}, bf16[1296,256]{1,0:T(8,128)(2,1)S(1)}, u32[]{:S(2)}, u32[]{:S(2)}) collective-permute-start(bf16[1296,256]{1,0:T(8,128)(2,1)S(1)} %get-tuple-element.78), channel_id=1, source_target_pairs={{0,8},{1,25},{2,10},{3,27},{4,12},{5,29},{6,14},{7,31},{8,16},{9,1... | collective-permute-start | bytes 1990664 | tf_op jit(solution)/shard_map/ppermute | solution.py:405
  25.0 11.4 %collective-permute-start.3 = (bf16[8,176,256]{2,1,0:T(8,128)(2,1)S(1)}, bf16[8,176,256]{2,1,0:T(8,128)(2,1)S(1)}, u32[]{:S(2)}, u32[]{:S(2)}) collective-permute-start(bf16[8,176,256]{2,1,0:T(8,128)(2,1)S(1)} %get-tuple-element.71), channel_id=1, source_target_pairs={{0,2},{1,33},{2,4},{3,35},{4,6},{5,37},{6,0},{7,39},{8,10},{9,41},... | collective-permute-start | bytes 2162696 | tf_op jit(solution)/shard_map/ppermute | solution.py:405
  25.5 12.5 %collective-permute-start.4 = (bf16[8,176,256]{2,1,0:T(8,128)(2,1)S(1)}, bf16[8,176,256]{2,1,0:T(8,128)(2,1)S(1)}, u32[]{:S(2)}, u32[]{:S(2)}) collective-permute-start(bf16[8,176,256]{2,1,0:T(8,128)(2,1)S(1)} %get-tuple-element.81), channel_id=1, source_target_pairs={{0,6},{1,97},{2,0},{3,99},{4,2},{5,101},{6,4},{7,103},{8,14},{9,10... | collective-permute-start | bytes 2162696 | tf_op jit(solution)/shard_map/ppermute | solution.py:405
  28.9 15.1 %collective-permute-start.5 = (bf16[8,176,256]{2,1,0:T(8,128)(2,1)S(1)}, bf16[8,176,256]{2,1,0:T(8,128)(2,1)S(1)}, u32[]{:S(2)}, u32[]{:S(2)}) collective-permute-start(bf16[8,176,256]{2,1,0:T(8,128)(2,1)S(1)} %get-tuple-element.74), channel_id=1, source_target_pairs={{0,2},{1,33},{2,4},{3,35},{4,6},{5,37},{6,0},{7,39},{8,10},{9,41},... | collective-permute-start | bytes 2162696 | tf_op jit(solution)/shard_map/ppermute | solution.py:405
  30.7 15.1 %collective-permute-start.6 = (bf16[8,176,256]{2,1,0:T(8,128)(2,1)S(1)}, bf16[8,176,256]{2,1,0:T(8,128)(2,1)S(1)}, u32[]{:S(2)}, u32[]{:S(2)}) collective-permute-start(bf16[8,176,256]{2,1,0:T(8,128)(2,1)S(1)} %get-tuple-element.83), channel_id=1, source_target_pairs={{0,6},{1,97},{2,0},{3,99},{4,2},{5,101},{6,4},{7,103},{8,14},{9,10... | collective-permute-start | bytes 2162696 | tf_op jit(solution)/shard_map/ppermute | solution.py:405
  33.8 14.6 %collective-permute-start.7 = (bf16[1296,256]{1,0:T(8,128)(2,1)S(1)}, bf16[1296,256]{1,0:T(8,128)(2,1)S(1)}, u32[]{:S(2)}, u32[]{:S(2)}) collective-permute-start(bf16[1296,256]{1,0:T(8,128)(2,1)S(1)} %shard_map.61), channel_id=1, source_target_pairs={{0,8},{1,25},{2,10},{3,27},{4,12},{5,29},{6,14},{7,31},{8,16},{9,1... | collective-permute-start | bytes 1990664 | tf_op jit(solution)/shard_map/ppermute | solution.py:405
  41.0 11.4 %collective-permute-start.8 = (bf16[8,176,256]{2,1,0:T(8,128)(2,1)S(1)}, bf16[8,176,256]{2,1,0:T(8,128)(2,1)S(1)}, u32[]{:S(2)}, u32[]{:S(2)}) collective-permute-start(bf16[8,176,256]{2,1,0:T(8,128)(2,1)S(1)} %get-tuple-element.82), channel_id=1, source_target_pairs={{0,2},{1,33},{2,4},{3,35},{4,6},{5,37},{6,0},{7,39},{8,10},{9,41},... | collective-permute-start | bytes 2162696 | tf_op jit(solution)/shard_map/ppermute | solution.py:405
  41.3 12.5 %collective-permute-start.9 = (bf16[8,176,256]{2,1,0:T(8,128)(2,1)S(1)}, bf16[8,176,256]{2,1,0:T(8,128)(2,1)S(1)}, u32[]{:S(2)}, u32[]{:S(2)}) collective-permute-start(bf16[8,176,256]{2,1,0:T(8,128)(2,1)S(1)} %get-tuple-element.98), channel_id=1, source_target_pairs={{0,6},{1,97},{2,0},{3,99},{4,2},{5,101},{6,4},{7,103},{8,14},{9,10... | collective-permute-start | bytes 2162696 | tf_op jit(solution)/shard_map/ppermute | solution.py:405
  48.5 17.6 %collective-permute-start.16 = (bf16[1296,256]{1,0:T(8,128)(2,1)S(1)}, bf16[1296,256]{1,0:T(8,128)(2,1)S(1)}, u32[]{:S(2)}, u32[]{:S(2)}) collective-permute-start(bf16[1296,256]{1,0:T(8,128)(2,1)S(1)} %shard_map.64), channel_id=1, source_target_pairs={{0,8},{1,25},{2,10},{3,27},{4,12},{5,29},{6,14},{7,31},{8,16},{9,1... | collective-permute-start | bytes 1990664 | tf_op jit(solution)/shard_map/ppermute | solution.py:405
  54.3 13.1 %collective-permute-start.10 = (bf16[4,176,256]{2,1,0:T(8,128)(2,1)S(1)}, bf16[4,176,256]{2,1,0:T(8,128)(2,1)S(1)}, u32[]{:S(2)}, u32[]{:S(2)}) collective-permute-start(bf16[4,176,256]{2,1,0:T(8,128)(2,1)S(1)} %get-tuple-element.100), channel_id=1, source_target_pairs={{0,64},{1,17},{2,66},{3,19},{4,68},{5,21},{6,70},{7,23},{8,72},{9,... | collective-permute-start | bytes 1081352 | tf_op jit(solution)/shard_map/ppermute | solution.py:405
  57.8 9.6 %collective-permute-start.11 = (bf16[4,176,256]{2,1,0:T(8,128)(2,1)S(1)}, bf16[4,176,256]{2,1,0:T(8,128)(2,1)S(1)}, u32[]{:S(2)}, u32[]{:S(2)}) collective-permute-start(bf16[4,176,256]{2,1,0:T(8,128)(2,1)S(1)} %get-tuple-element.101), channel_id=1, source_target_pairs={{0,32},{1,9},{2,34},{3,11},{4,36},{5,13},{6,38},{7,15},{8,40},{9,1... | collective-permute-start | bytes 1081352 | tf_op jit(solution)/shard_map/ppermute | solution.py:405
  59.0 9.3 %collective-permute-start.12 = (bf16[4,176,256]{2,1,0:T(8,128)(2,1)S(1)}, bf16[4,176,256]{2,1,0:T(8,128)(2,1)S(1)}, u32[]{:S(2)}, u32[]{:S(2)}) collective-permute-start(bf16[4,176,256]{2,1,0:T(8,128)(2,1)S(1)} %get-tuple-element.102), channel_id=1, source_target_pairs={{0,96},{1,25},{2,98},{3,27},{4,100},{5,29},{6,102},{7,31},{8,104},... | collective-permute-start | bytes 1081352 | tf_op jit(solution)/shard_map/ppermute | solution.py:405
  66.2 8.0 %collective-permute-start.17 = (bf16[336,256]{1,0:T(8,128)(2,1)S(1)}, bf16[336,256]{1,0:T(8,128)(2,1)S(1)}, u32[]{:S(2)}, u32[]{:S(2)}) collective-permute-start(bf16[336,256]{1,0:T(8,128)(2,1)S(1)} %get-tuple-element.115), channel_id=1, source_target_pairs={{0,4},{1,5},{2,6},{3,7},{4,0},{5,1},{6,2},{7,3},{8,12},{9,13},{10,... | collective-permute-start | bytes 516104 | tf_op jit(solution)/shard_map/ppermute | solution.py:405
  68.4 16.5 %collective-permute-start.13 = (f32[176,256]{1,0:T(8,128)S(1)}, f32[176,256]{1,0:T(8,128)S(1)}, u32[]{:S(2)}, u32[]{:S(2)}) collective-permute-start(f32[176,256]{1,0:T(8,128)S(1)} %get-tuple-element.104), channel_id=1, source_target_pairs={{0,16},{1,5},{2,18},{3,7},{4,20},{5,1},{6,22},{7,3},{8,24},{9,13},... | collective-permute-start | bytes 540680 | tf_op jit(solution)/shard_map/ppermute | solution.py:405
  70.6 7.3 %collective-permute-start.18 = (bf16[336,256]{1,0:T(8,128)(2,1)S(1)}, bf16[336,256]{1,0:T(8,128)(2,1)S(1)}, u32[]{:S(2)}, u32[]{:S(2)}) collective-permute-start(bf16[336,256]{1,0:T(8,128)(2,1)S(1)} %get-tuple-element.116), channel_id=1, source_target_pairs={{0,2},{1,7},{2,4},{3,1},{4,6},{5,3},{6,0},{7,5},{8,10},{9,15},{10,... | collective-permute-start | bytes 516104 | tf_op jit(solution)/shard_map/ppermute | solution.py:405
  70.7 8.5 %collective-permute-start.19 = (bf16[336,256]{1,0:T(8,128)(2,1)S(1)}, bf16[336,256]{1,0:T(8,128)(2,1)S(1)}, u32[]{:S(2)}, u32[]{:S(2)}) collective-permute-start(bf16[336,256]{1,0:T(8,128)(2,1)S(1)} %get-tuple-element.117), channel_id=1, source_target_pairs={{0,6},{1,3},{2,0},{3,5},{4,2},{5,7},{6,4},{7,1},{8,14},{9,11},{10,... | collective-permute-start | bytes 516104 | tf_op jit(solution)/shard_map/ppermute | solution.py:405
  72.6 14.5 %collective-permute-start.14 = (f32[176,256]{1,0:T(8,128)S(1)}, f32[176,256]{1,0:T(8,128)S(1)}, u32[]{:S(2)}, u32[]{:S(2)}) collective-permute-start(f32[176,256]{1,0:T(8,128)S(1)} %get-tuple-element.105), channel_id=1, source_target_pairs={{0,8},{1,3},{2,10},{3,5},{4,12},{5,7},{6,14},{7,1},{8,16},{9,11},{... | collective-permute-start | bytes 540680 | tf_op jit(solution)/shard_map/ppermute | solution.py:405
  74.2 13.0 %collective-permute-start.15 = (f32[176,256]{1,0:T(8,128)S(1)}, f32[176,256]{1,0:T(8,128)S(1)}, u32[]{:S(2)}, u32[]{:S(2)}) collective-permute-start(f32[176,256]{1,0:T(8,128)S(1)} %get-tuple-element.106), channel_id=1, source_target_pairs={{0,24},{1,7},{2,26},{3,1},{4,28},{5,3},{6,30},{7,5},{8,0},{9,15},{... | collective-permute-start | bytes 540680 | tf_op jit(solution)/shard_map/ppermute | solution.py:405
  79.2 8.0 %collective-permute-start.20 = (f32[88,256]{1,0:T(8,128)S(1)}, f32[88,256]{1,0:T(8,128)S(1)}, u32[]{:S(2)}, u32[]{:S(2)}) collective-permute-start(f32[88,256]{1,0:T(8,128)S(1)} %get-tuple-element.119), channel_id=1, source_target_pairs={{0,64},{1,65},{2,66},{3,67},{4,68},{5,69},{6,70},{7,71},{8,72},{9,... | collective-permute-start | bytes 270344 | tf_op jit(solution)/shard_map/ppermute | solution.py:405
  83.9 5.7 %collective-permute-start.21 = (f32[88,256]{1,0:T(8,128)S(1)}, f32[88,256]{1,0:T(8,128)S(1)}, u32[]{:S(2)}, u32[]{:S(2)}) collective-permute-start(f32[88,256]{1,0:T(8,128)S(1)} %get-tuple-element.120), channel_id=1, source_target_pairs={{0,32},{1,97},{2,34},{3,99},{4,36},{5,101},{6,38},{7,103},{8,40},{... | collective-permute-start | bytes 270344 | tf_op jit(solution)/shard_map/ppermute | solution.py:405
  85.0 4.6 %collective-permute-start.22 = (f32[88,256]{1,0:T(8,128)S(1)}, f32[88,256]{1,0:T(8,128)S(1)}, u32[]{:S(2)}, u32[]{:S(2)}) collective-permute-start(f32[88,256]{1,0:T(8,128)S(1)} %get-tuple-element.121), channel_id=1, source_target_pairs={{0,96},{1,33},{2,98},{3,35},{4,100},{5,37},{6,102},{7,39},{8,104},... | collective-permute-start | bytes 270344 | tf_op jit(solution)/shard_map/ppermute | solution.py:405
  87.2 10.5 %collective-permute-start.23 = (bf16[176,256]{1,0:T(8,128)(2,1)S(1)}, bf16[176,256]{1,0:T(8,128)(2,1)S(1)}, u32[]{:S(2)}, u32[]{:S(2)}) collective-permute-start(bf16[176,256]{1,0:T(8,128)(2,1)S(1)} %get-tuple-element.123), channel_id=1, source_target_pairs={{0,8},{1,16},{2,32},{3,48},{4,64},{5,80},{6,96},{7,112},{8,0},{9,2... | collective-permute-start | bytes 270344 | tf_op jit(solution)/shard_map/ppermute | solution.py:405
  89.6 8.6 %collective-permute-start.24 = (bf16[80,256]{1,0:T(8,128)(2,1)S(1)}, bf16[80,256]{1,0:T(8,128)(2,1)S(1)}, u32[]{:S(2)}, u32[]{:S(2)}) collective-permute-start(bf16[80,256]{1,0:T(8,128)(2,1)S(1)} %get-tuple-element.124), channel_id=1, source_target_pairs={{0,8},{1,16},{2,32},{3,48},{4,64},{5,80},{6,96},{7,112},{8,0},{9,2... | collective-permute-start | bytes 122888 | tf_op jit(solution)/shard_map/ppermute | solution.py:405

commit v6 on v5

--- a/solution.py
+++ b/solution.py
@@ -492,8 +492,8 @@
 
     got = [move(part[d], main_to(2, d)) for d in (2, 1, 3)]
     got_r = [move(rest[d], rest_to(2, d)) for d in (2, 1, 3)]
-    main_3, main_sent = call_sum(last_sum_kernel, [((MAIN, BLK), F32), ((MAIN, BLK), BF)], part[0], *got)
-    rest_3, rest_sent = call_sum(last_sum_kernel, [((REST + 8, BLK), F32), ((REST, BLK), BF)], rest[0], *got_r)
+    main_3, main_sent = call_sum(last_sum_kernel, [((MAIN, BLK), F32), ((MAIN, BLK), F32)], part[0], *got)
+    rest_3, rest_sent = call_sum(last_sum_kernel, [((REST + 8, BLK), F32), ((REST, BLK), F32)], rest[0], *got_r)
     got_main = move(main_sent, mirror_pairs())
     got_rest = move(rest_sent, mirror_pairs())
 

time: 100 us -> 107 us (1.070)
  waiting for transfers between devices: 24.1 us -> 31.1 us
    ppermute x23, waiting for transfers between devices: 24.1 us -> 31.1 us  [move(): return lax.ppermute(array, AXES, pairs)]
  transfers between devices with their start and end apart: 25 -> 25, of which waited for: 15 -> 15; matrix products, arithmetic and copies ran while one was open for 1% -> 1% of each run, Pallas kernels for 24% -> 22%
where the time goes in v6:
time: 107 us
  starting transfers between devices  36.5 us (34%)
  Pallas kernels  34.5 us (32%)
  waiting for transfers between devices  31.1 us (29%)
  local copies, waits for them, and re-layouts  4.38 us (4%)
    ppermute x23, starting transfers between devices, move(): return lax.ppermute(array, AXES, pairs)  35.9 us
    ppermute x23, waiting for transfers between devices, move(): return lax.ppermute(array, AXES, pairs)  31.1 us
    pallas_call x8, Pallas kernels, products(): pl.pallas_call(functools.partial(product_kernel, plan, opening, cross_mad...  21.4 us
    pallas_call x1, Pallas kernels, scaled_rows(): pl.pallas_call(first_pick_kernel, out_shape=[jax.ShapeDtypeStruct((2 * un...  5.13 us
    unnamed x8, local copies, waits for them, and re-layouts  3.64 us
    pallas_call x1, Pallas kernels, scaled_rows(): pl.pallas_call(second_pick_kernel, out_shape=part, in_specs=[smem, vmem],...  3.44 us
    pallas_call x1, Pallas kernels, local(): pl.pallas_call(turn_kernel, out_shape=[jax.ShapeDtypeStruct((half[1], 2 *...  2.16 us
  transfers between devices with their start and end apart: 25, of which 15 were waited for; matrix products, arithmetic and copies ran while one was open for 1% of the time, Pallas kernels for 22%

profile of v6, /device:TPU:6, one launch (start us, length us, event | category | flops | bytes accessed | tf_op | source)
XLA Modules:
  0.0 106.8 jit_solution(1502712189327425683)
XLA Ops:
  0.0 1.6 %copy-done = bf16[256,4096]{1,0:T(8,128)(2,1)S(1)} copy-done((bf16[256,4096]{1,0:T(8,128)(2,1)S(1)}, bf16[256,4096]{1,0:T(8,128)(2,1)}, u32[]{:S(2)}) %copy-start) | copy-done | bytes 2097176
  1.6 0.7 copy-done.1
  2.3 0.7 copy-done.2
  3.0 0.7 copy-done.3
  3.6 5.1 %shard_map.55 = (f32[8192,128]{1,0:T(8,128)S(1)}, bf16[2048,256]{1,0:T(8,128)(2,1)S(1)}) custom-call(s32[4096]{0:T(1024)S(1)} %copy-done.1, s32[8]{0:T(128)S(1)} %copy-done.3, f32[1,256]{1,0:T(1,128)S(1)} %bitcast.3, bf16[256,4096]{1,0:T(8,128)(2,1)S(1)} %copy-done), custom_call_target="tpu_custom_call" | custom-call | bytes 8388608 | tf_op jit(solution)/shard_map/pallas_call | solution.py:155
  8.8 0.1 collective-permute-start
  8.9 3.4 %shard_map.56.own_high.refs_1_ = bf16[2048,256]{1,0:T(8,128)(2,1)S(1)} custom-call(s32[4096]{0:T(1024)S(1)} %copy-done.1, f32[8192,128]{1,0:T(8,128)S(1)} %get-tuple-element.66.columns), custom_call_target="tpu_custom_call" | custom-call | bytes 8388608 | tf_op jit(solution)/shard_map/pallas_call | solution.py:164
  12.3 0.6 collective-permute-start.1
  12.9 0.7 dynamic-slice_reduce_fusion.table
  13.6 0.0 collective-permute-done.other_low.refs_2_
  13.7 2.2 %shard_map.57 = (bf16[256,4096]{1,0:T(8,128)(2,1)S(1)}, bf16[256,2048]{1,0:T(8,128)(2,1)S(1)}) custom-call(bf16[2048,256]{1,0:T(8,128)(2,1)S(1)} %get-tuple-element.65.own_low.refs_0_, bf16[2048,256]{1,0:T(8,128)(2,1)S(1)} %shard_map.56.own_high.refs_1_, bf16[2048,256]{1,0:T(8,128)(2,1)S(1)} %collective-permute-done.other_low.refs_2_), custom_call_target="tpu_custom_call" | custom-call | bytes 1048576 | tf_op jit(solution)/shard_map/pallas_call | solution.py:419
  15.8 4.2 %shard_map.58 = (bf16[1296,256]{1,0:T(8,128)(2,1)S(1)}, f32[16,256]{1,0:T(8,128)S(1)}, bf16[4096,512]{1,0:T(8,128)(2,1)S(1)}, bf16[512,4096]{1,0:T(8,128)(2,1)S(1)}) custom-call(s32[528]{0:T(1024)S(1)} %dynamic-slice_reduce_fusion.table, bf16[2048,256]{1,0:T(8,128)(2,1)S(1)} %get-tuple-element.65.own_low.refs_0_, ...), custom_call_target="tpu_custom_call" | custom-call | bytes 1048576 | tf_op jit(solution)/shard_map/pallas_call | solution.py:300
  20.1 2.5 %collective-permute-start.2 = (bf16[1296,256]{1,0:T(8,128)(2,1)S(1)}, bf16[1296,256]{1,0:T(8,128)(2,1)S(1)}, u32[]{:S(2)}, u32[]{:S(2)}) collective-permute-start(bf16[1296,256]{1,0:T(8,128)(2,1)S(1)} %get-tuple-element.78), channel_id=1, source_target_pairs={{0,8},{1,25},{2,10},{3,27},{4,12},{5,29},{6,14},{7,31},{8,16},{9,1... | collective-permute-start | bytes 1990664 | tf_op jit(solution)/shard_map/ppermute | solution.py:405
  22.6 2.4 %shard_map.59 = (bf16[8,176,256]{2,1,0:T(8,128)(2,1)S(1)}, bf16[8,176,256]{2,1,0:T(8,128)(2,1)S(1)}) custom-call(s32[528]{0:T(1024)S(1)} %dynamic-slice_reduce_fusion.table, bf16[4096,512]{1,0:T(8,128)(2,1)S(1)} %get-tuple-element.108.refs_0_, bf16[512,4096]{1,0:T(8,128)(2,1)S(1)} %get-tuple-element.109.refs_1_), custom_call_target="tpu_custom_call" | custom-call | bytes 1048576 | tf_op jit(solution)/shard_map/pallas_call | solution.py:300
  25.0 0.5 collective-permute-start.3
  25.5 1.5 %collective-permute-start.4 = (bf16[8,176,256]{2,1,0:T(8,128)(2,1)S(1)}, bf16[8,176,256]{2,1,0:T(8,128)(2,1)S(1)}, u32[]{:S(2)}, u32[]{:S(2)}) collective-permute-start(bf16[8,176,256]{2,1,0:T(8,128)(2,1)S(1)} %get-tuple-element.81), channel_id=1, source_target_pairs={{0,6},{1,97},{2,0},{3,99},{4,2},{5,101},{6,4},{7,103},{8,14},{9,10... | collective-permute-start | bytes 2162696 | tf_op jit(solution)/shard_map/ppermute | solution.py:405
  27.1 1.8 %shard_map.60 = (bf16[8,176,256]{2,1,0:T(8,128)(2,1)S(1)}, bf16[8,176,256]{2,1,0:T(8,128)(2,1)S(1)}) custom-call(s32[528]{0:T(1024)S(1)} %dynamic-slice_reduce_fusion.table, bf16[4096,512]{1,0:T(8,128)(2,1)S(1)} %get-tuple-element.108.refs_0_, bf16[512,4096]{1,0:T(8,128)(2,1)S(1)} %get-tuple-element.109.refs_1_), custom_call_target="tpu_custom_call" | custom-call | bytes 1048576 | tf_op jit(solution)/shard_map/pallas_call | solution.py:300
  28.9 1.8 %collective-permute-start.5 = (bf16[8,176,256]{2,1,0:T(8,128)(2,1)S(1)}, bf16[8,176,256]{2,1,0:T(8,128)(2,1)S(1)}, u32[]{:S(2)}, u32[]{:S(2)}) collective-permute-start(bf16[8,176,256]{2,1,0:T(8,128)(2,1)S(1)} %get-tuple-element.74), channel_id=1, source_target_pairs={{0,2},{1,33},{2,4},{3,35},{4,6},{5,37},{6,0},{7,39},{8,10},{9,41},... | collective-permute-start | bytes 2162696 | tf_op jit(solution)/shard_map/ppermute | solution.py:405
  30.7 0.5 collective-permute-start.6
  31.1 0.9 collective-permute-done.2.refs_3_
  32.0 1.8 %shard_map.61 = bf16[1296,256]{1,0:T(8,128)(2,1)S(1)} custom-call(s32[528]{0:T(1024)S(1)} %dynamic-slice_reduce_fusion.table, bf16[4096,512]{1,0:T(8,128)(2,1)S(1)} %get-tuple-element.108.refs_0_, bf16[512,4096]{1,0:T(8,128)(2,1)S(1)} %get-tuple-element.109.refs_1_, f32[16,256]{1,0:T(8,128)S(1)} %get-tuple-element.77.refs_2_, ...), custom_call_target="tpu_custom_call" | custom-call | bytes 1048576 | tf_op jit(solution)/shard_map/pallas_call | solution.py:300
  33.8 1.3 %collective-permute-start.7 = (bf16[1296,256]{1,0:T(8,128)(2,1)S(1)}, bf16[1296,256]{1,0:T(8,128)(2,1)S(1)}, u32[]{:S(2)}, u32[]{:S(2)}) collective-permute-start(bf16[1296,256]{1,0:T(8,128)(2,1)S(1)} %shard_map.61), channel_id=1, source_target_pairs={{0,8},{1,25},{2,10},{3,27},{4,12},{5,29},{6,14},{7,31},{8,16},{9,1... | collective-permute-start | bytes 1990664 | tf_op jit(solution)/shard_map/ppermute | solution.py:405
  35.1 1.2 %collective-permute-done.3.refs_2_ = bf16[8,176,256]{2,1,0:T(8,128)(2,1)S(1)} collective-permute-done((bf16[8,176,256]{2,1,0:T(8,128)(2,1)S(1)}, bf16[8,176,256]{2,1,0:T(8,128)(2,1)S(1)}, u32[]{:S(2)}, u32[]{:S(2)}) %collective-permute-start.3) | collective-permute-done | bytes 720928 | tf_op jit(solution)/shard_map/ppermute | solution.py:405
  36.3 1.7 %collective-permute-done.4.refs_3_ = bf16[8,176,256]{2,1,0:T(8,128)(2,1)S(1)} collective-permute-done((bf16[8,176,256]{2,1,0:T(8,128)(2,1)S(1)}, bf16[8,176,256]{2,1,0:T(8,128)(2,1)S(1)}, u32[]{:S(2)}, u32[]{:S(2)}) %collective-permute-start.4) | collective-permute-done | bytes 720928 | tf_op jit(solution)/shard_map/ppermute | solution.py:405
  38.0 2.9 %shard_map.62 = (bf16[8,176,256]{2,1,0:T(8,128)(2,1)S(1)}, bf16[8,176,256]{2,1,0:T(8,128)(2,1)S(1)}) custom-call(s32[528]{0:T(1024)S(1)} %dynamic-slice_reduce_fusion.table, bf16[4096,512]{1,0:T(8,128)(2,1)S(1)} %get-tuple-element.108.refs_0_, bf16[512,4096]{1,0:T(8,128)(2,1)S(1)} %get-tuple-element.109.refs_1_, ...), custom_call_target="tpu_custom_call" | custom-call | bytes 1048576 | tf_op jit(solution)/shard_map/pallas_call | solution.py:300
  41.0 0.4 collective-permute-start.8
  41.3 1.7 %collective-permute-start.9 = (bf16[8,176,256]{2,1,0:T(8,128)(2,1)S(1)}, bf16[8,176,256]{2,1,0:T(8,128)(2,1)S(1)}, u32[]{:S(2)}, u32[]{:S(2)}) collective-permute-start(bf16[8,176,256]{2,1,0:T(8,128)(2,1)S(1)} %get-tuple-element.98), channel_id=1, source_target_pairs={{0,6},{1,97},{2,0},{3,99},{4,2},{5,101},{6,4},{7,103},{8,14},{9,10... | collective-permute-start | bytes 2162696 | tf_op jit(solution)/shard_map/ppermute | solution.py:405
  43.1 1.0 collective-permute-done.5.refs_6_
  44.1 1.7 %collective-permute-done.6.refs_5_ = bf16[8,176,256]{2,1,0:T(8,128)(2,1)S(1)} collective-permute-done((bf16[8,176,256]{2,1,0:T(8,128)(2,1)S(1)}, bf16[8,176,256]{2,1,0:T(8,128)(2,1)S(1)}, u32[]{:S(2)}, u32[]{:S(2)}) %collective-permute-start.6) | collective-permute-done | bytes 720928 | tf_op jit(solution)/shard_map/ppermute | solution.py:405
  45.7 2.6 %shard_map.63.own = f32[1296,256]{1,0:T(8,128)S(1)} custom-call(s32[528]{0:T(1024)S(1)} %dynamic-slice_reduce_fusion.table, bf16[4096,512]{1,0:T(8,128)(2,1)S(1)} %get-tuple-element.108.refs_0_, bf16[512,4096]{1,0:T(8,128)(2,1)S(1)} %get-tuple-element.109.refs_1_, f32[16,256]{1,0:T(8,128)S(1)} %get-tuple-element.77.refs_2_), custom_call_target="tpu_custom_call" | custom-call | bytes 20971520 | tf_op jit(solution)/shard_map/pallas_call | solution.py:300
  48.4 0.1 shard_map.64
  48.5 0.8 collective-permute-start.16
  49.3 2.7 %shard_map.65 = (f32[4,176,256]{2,1,0:T(8,128)S(1)}, f32[4,176,256]{2,1,0:T(8,128)S(1)}, f32[4,176,256]{2,1,0:T(8,128)S(1)}, f32[4,176,256]{2,1,0:T(8,128)S(1)}) custom-call(s32[528]{0:T(1024)S(1)} %dynamic-slice_reduce_fusion.table, bf16[4096,512]{1,0:T(8,128)(2,1)S(1)} %get-tuple-element.108.refs_0_, bf16[512,4096]{1,0:T(8,128)(2,1)S(1)} %get-tuple-element.109.refs_1_), custom_call_target="tpu_custom_call" | custom-call | bytes 20971520 | tf_op jit(solution)/shard_map/pallas_call | solution.py:300
  52.0 0.3 collective-permute-done.8.refs_4_
  52.3 1.5 %collective-permute-done.9.refs_7_ = bf16[8,176,256]{2,1,0:T(8,128)(2,1)S(1)} collective-permute-done((bf16[8,176,256]{2,1,0:T(8,128)(2,1)S(1)}, bf16[8,176,256]{2,1,0:T(8,128)(2,1)S(1)}, u32[]{:S(2)}, u32[]{:S(2)}) %collective-permute-start.9) | collective-permute-done | bytes 720928 | tf_op jit(solution)/shard_map/ppermute | solution.py:405
  53.8 0.4 shard_map.66
  54.3 3.6 %collective-permute-start.10 = (bf16[4,176,256]{2,1,0:T(8,128)(2,1)S(1)}, bf16[4,176,256]{2,1,0:T(8,128)(2,1)S(1)}, u32[]{:S(2)}, u32[]{:S(2)}) collective-permute-start(bf16[4,176,256]{2,1,0:T(8,128)(2,1)S(1)} %get-tuple-element.100), channel_id=1, source_target_pairs={{0,64},{1,17},{2,66},{3,19},{4,68},{5,21},{6,70},{7,23},{8,72},{9,... | collective-permute-start | bytes 1081352 | tf_op jit(solution)/shard_map/ppermute | solution.py:405
  57.8 1.2 %collective-permute-start.11 = (bf16[4,176,256]{2,1,0:T(8,128)(2,1)S(1)}, bf16[4,176,256]{2,1,0:T(8,128)(2,1)S(1)}, u32[]{:S(2)}, u32[]{:S(2)}) collective-permute-start(bf16[4,176,256]{2,1,0:T(8,128)(2,1)S(1)} %get-tuple-element.101), channel_id=1, source_target_pairs={{0,32},{1,9},{2,34},{3,11},{4,36},{5,13},{6,38},{7,15},{8,40},{9,1... | collective-permute-start | bytes 1081352 | tf_op jit(solution)/shard_map/ppermute | solution.py:405
  59.0 2.0 %collective-permute-start.12 = (bf16[4,176,256]{2,1,0:T(8,128)(2,1)S(1)}, bf16[4,176,256]{2,1,0:T(8,128)(2,1)S(1)}, u32[]{:S(2)}, u32[]{:S(2)}) collective-permute-start(bf16[4,176,256]{2,1,0:T(8,128)(2,1)S(1)} %get-tuple-element.102), channel_id=1, source_target_pairs={{0,96},{1,25},{2,98},{3,27},{4,100},{5,29},{6,102},{7,31},{8,104},... | collective-permute-start | bytes 1081352 | tf_op jit(solution)/shard_map/ppermute | solution.py:405
  61.1 2.8 %shard_map.69 = (f32[336,256]{1,0:T(8,128)S(1)}, f32[336,256]{1,0:T(8,128)S(1)}, f32[336,256]{1,0:T(8,128)S(1)}, f32[336,256]{1,0:T(8,128)S(1)}) custom-call(s32[528]{0:T(1024)S(1)} %dynamic-slice_reduce_fusion.table, bf16[4096,512]{1,0:T(8,128)(2,1)S(1)} %get-tuple-element.108.refs_0_, bf16[512,4096]{1,0:T(8,128)(2,1)S(1)} %get-tuple-element.109.refs_1_, ...), custom_call_target="tpu_custom_call" | custom-call | bytes 20971520 | tf_op jit(solution)/shard_map/pallas_call | solution.py:300
  63.9 2.2 %collective-permute-done.16.refs_4_ = bf16[1296,256]{1,0:T(8,128)(2,1)S(1)} collective-permute-done((bf16[1296,256]{1,0:T(8,128)(2,1)S(1)}, bf16[1296,256]{1,0:T(8,128)(2,1)S(1)}, u32[]{:S(2)}, u32[]{:S(2)}) %collective-permute-start.16) | collective-permute-done | bytes 663584 | tf_op jit(solution)/shard_map/ppermute | solution.py:405
  66.1 0.1 shard_map.70
  66.2 1.2 %collective-permute-start.17 = (bf16[336,256]{1,0:T(8,128)(2,1)S(1)}, bf16[336,256]{1,0:T(8,128)(2,1)S(1)}, u32[]{:S(2)}, u32[]{:S(2)}) collective-permute-start(bf16[336,256]{1,0:T(8,128)(2,1)S(1)} %get-tuple-element.115), channel_id=1, source_target_pairs={{0,4},{1,5},{2,6},{3,7},{4,0},{5,1},{6,2},{7,3},{8,12},{9,13},{10,... | collective-permute-start | bytes 516104 | tf_op jit(solution)/shard_map/ppermute | solution.py:405
  67.4 0.0 collective-permute-done.10.second
  67.4 0.9 collective-permute-done.12.third
  68.3 0.1 shard_map.67
  68.4 2.1 %collective-permute-start.13 = (f32[176,256]{1,0:T(8,128)S(1)}, f32[176,256]{1,0:T(8,128)S(1)}, u32[]{:S(2)}, u32[]{:S(2)}) collective-permute-start(f32[176,256]{1,0:T(8,128)S(1)} %get-tuple-element.104), channel_id=1, source_target_pairs={{0,16},{1,5},{2,18},{3,7},{4,20},{5,1},{6,22},{7,3},{8,24},{9,13},... | collective-permute-start | bytes 540680 | tf_op jit(solution)/shard_map/ppermute | solution.py:405
  70.6 0.1 collective-permute-start.18
  70.7 1.9 %collective-permute-start.19 = (bf16[336,256]{1,0:T(8,128)(2,1)S(1)}, bf16[336,256]{1,0:T(8,128)(2,1)S(1)}, u32[]{:S(2)}, u32[]{:S(2)}) collective-permute-start(bf16[336,256]{1,0:T(8,128)(2,1)S(1)} %get-tuple-element.117), channel_id=1, source_target_pairs={{0,6},{1,3},{2,0},{3,5},{4,2},{5,7},{6,4},{7,1},{8,14},{9,11},{10,... | collective-permute-start | bytes 516104 | tf_op jit(solution)/shard_map/ppermute | solution.py:405
  72.6 1.6 %collective-permute-done.17.second = bf16[336,256]{1,0:T(8,128)(2,1)S(1)} collective-permute-done((bf16[336,256]{1,0:T(8,128)(2,1)S(1)}, bf16[336,256]{1,0:T(8,128)(2,1)S(1)}, u32[]{:S(2)}, u32[]{:S(2)}) %collective-permute-start.17) | collective-permute-done | bytes 172064 | tf_op jit(solution)/shard_map/ppermute | solution.py:405
  74.2 1.7 %collective-permute-start.15 = (f32[176,256]{1,0:T(8,128)S(1)}, f32[176,256]{1,0:T(8,128)S(1)}, u32[]{:S(2)}, u32[]{:S(2)}) collective-permute-start(f32[176,256]{1,0:T(8,128)S(1)} %get-tuple-element.106), channel_id=1, source_target_pairs={{0,24},{1,7},{2,26},{3,1},{4,28},{5,3},{6,30},{7,5},{8,0},{9,15},{... | collective-permute-start | bytes 540680 | tf_op jit(solution)/shard_map/ppermute | solution.py:405
  75.8 2.0 %collective-permute-done.18.first = bf16[336,256]{1,0:T(8,128)(2,1)S(1)} collective-permute-done((bf16[336,256]{1,0:T(8,128)(2,1)S(1)}, bf16[336,256]{1,0:T(8,128)(2,1)S(1)}, u32[]{:S(2)}, u32[]{:S(2)}) %collective-permute-start.18) | collective-permute-done | bytes 172064 | tf_op jit(solution)/shard_map/ppermute | solution.py:405
  77.9 1.3 %collective-permute-done.19.third = bf16[336,256]{1,0:T(8,128)(2,1)S(1)} collective-permute-done((bf16[336,256]{1,0:T(8,128)(2,1)S(1)}, bf16[336,256]{1,0:T(8,128)(2,1)S(1)}, u32[]{:S(2)}, u32[]{:S(2)}) %collective-permute-start.19) | collective-permute-done | bytes 172064 | tf_op jit(solution)/shard_map/ppermute | solution.py:405
  79.1 0.1 shard_map.71
  79.2 4.7 %collective-permute-start.20 = (f32[88,256]{1,0:T(8,128)S(1)}, f32[88,256]{1,0:T(8,128)S(1)}, u32[]{:S(2)}, u32[]{:S(2)}) collective-permute-start(f32[88,256]{1,0:T(8,128)S(1)} %get-tuple-element.119), channel_id=1, source_target_pairs={{0,64},{1,65},{2,66},{3,67},{4,68},{5,69},{6,70},{7,71},{8,72},{9,... | collective-permute-start | bytes 270344 | tf_op jit(solution)/shard_map/ppermute | solution.py:405
  83.9 1.1 %collective-permute-start.21 = (f32[88,256]{1,0:T(8,128)S(1)}, f32[88,256]{1,0:T(8,128)S(1)}, u32[]{:S(2)}, u32[]{:S(2)}) collective-permute-start(f32[88,256]{1,0:T(8,128)S(1)} %get-tuple-element.120), channel_id=1, source_target_pairs={{0,32},{1,97},{2,34},{3,99},{4,36},{5,101},{6,38},{7,103},{8,40},{... | collective-permute-start | bytes 270344 | tf_op jit(solution)/shard_map/ppermute | solution.py:405
  85.0 2.1 %collective-permute-start.22 = (f32[88,256]{1,0:T(8,128)S(1)}, f32[88,256]{1,0:T(8,128)S(1)}, u32[]{:S(2)}, u32[]{:S(2)}) collective-permute-start(f32[88,256]{1,0:T(8,128)S(1)} %get-tuple-element.121), channel_id=1, source_target_pairs={{0,96},{1,33},{2,98},{3,35},{4,100},{5,37},{6,102},{7,39},{8,104},... | collective-permute-start | bytes 270344 | tf_op jit(solution)/shard_map/ppermute | solution.py:405
  87.2 0.1 collective-permute-start.23
  87.3 2.3 %collective-permute-done.21.first = f32[88,256]{1,0:T(8,128)S(1)} collective-permute-done((f32[88,256]{1,0:T(8,128)S(1)}, f32[88,256]{1,0:T(8,128)S(1)}, u32[]{:S(2)}, u32[]{:S(2)}) %collective-permute-start.21) | collective-permute-done | bytes 90144 | tf_op jit(solution)/shard_map/ppermute | solution.py:405
  89.6 3.1 %collective-permute-start.24 = (f32[80,256]{1,0:T(8,128)S(1)}, f32[80,256]{1,0:T(8,128)S(1)}, u32[]{:S(2)}, u32[]{:S(2)}) collective-permute-start(f32[80,256]{1,0:T(8,128)S(1)} %get-tuple-element.124), channel_id=1, source_target_pairs={{0,8},{1,16},{2,32},{3,48},{4,64},{5,80},{6,96},{7,112},{8,0},{9,2... | collective-permute-start | bytes 245768 | tf_op jit(solution)/shard_map/ppermute | solution.py:405
  92.8 0.1 pad_add_fusion.refs_0_
  92.8 10.9 %collective-permute-done.23.refs_3_ = f32[176,256]{1,0:T(8,128)S(1)} collective-permute-done((f32[176,256]{1,0:T(8,128)S(1)}, f32[176,256]{1,0:T(8,128)S(1)}, u32[]{:S(2)}, u32[]{:S(2)}) %collective-permute-start.23) | collective-permute-done | bytes 180256 | tf_op jit(solution)/shard_map/ppermute | solution.py:405
  103.7 1.6 %collective-permute-done.24.refs_4_ = f32[80,256]{1,0:T(8,128)S(1)} collective-permute-done((f32[80,256]{1,0:T(8,128)S(1)}, f32[80,256]{1,0:T(8,128)S(1)}, u32[]{:S(2)}, u32[]{:S(2)}) %collective-permute-start.24) | collective-permute-done | bytes 81952 | tf_op jit(solution)/shard_map/ppermute | solution.py:405
  105.3 1.5 %shard_map.73 = f32[256,512]{1,0:T(8,128)} custom-call(s32[2]{0:T(128)S(1)} %pad_add_fusion.refs_0_, f32[176,256]{1,0:T(8,128)S(1)} %get-tuple-element.107.refs_1_, f32[88,256]{1,0:T(8,128)S(1)} %get-tuple-element.122.refs_2_, f32[176,256]{1,0:T(8,128)S(1)} %collective-permute-done.23.refs_3_, f32[80,256]{1,0:T(8,128)S(1)} %collective-permute-done.24.refs_4_), custom_call_target="tpu_custom_call" | custom-call | tf_op jit(solution)/shard_map/pallas_call | solution.py:505
  (15 shorter events, 0.1 us)
Async XLA Ops:
  0.0 1.6 %copy-start = (bf16[256,4096]{1,0:T(8,128)(2,1)S(1)}, bf16[256,4096]{1,0:T(8,128)(2,1)}, u32[]{:S(2)}) copy-start(bf16[256,4096]{1,0:T(8,128)(2,1)} %design_ref.1) | copy-start | bytes 6291460
  1.6 0.7 copy-start.1
  2.3 0.7 copy-start.2
  3.0 0.7 copy-start.3
  8.8 4.9 %collective-permute-start = (bf16[2048,256]{1,0:T(8,128)(2,1)S(1)}, bf16[2048,256]{1,0:T(8,128)(2,1)S(1)}, u32[]{:S(2)}, u32[]{:S(2)}) collective-permute-start(bf16[2048,256]{1,0:T(8,128)(2,1)S(1)} %get-tuple-element.65.own_low.refs_0_), channel_id=1, source_target_pairs={{0,1},{1,0},{2,3},{3,2},{4,5},{5,4},{6,7},{7,6},{8,9},{9,8},{10,11... | collective-permute-start | bytes 3145736 | tf_op jit(solution)/shard_map/ppermute | solution.py:416
  12.3 3.5 %collective-permute-start.1 = (bf16[2048,256]{1,0:T(8,128)(2,1)S(1)}, bf16[2048,256]{1,0:T(8,128)(2,1)}, u32[]{:S(2)}, u32[]{:S(2)}) collective-permute-start(bf16[2048,256]{1,0:T(8,128)(2,1)S(1)} %shard_map.56.own_high.refs_1_), channel_id=1, source_target_pairs={{0,1},{1,0},{2,3},{3,2},{4,5},{5,4},{6,7},{7,6},{8,9},{9,8},{10,11... | collective-permute-start | bytes 3145736 | tf_op jit(solution)/shard_map/ppermute | solution.py:417
  20.1 12.0 %collective-permute-start.2 = (bf16[1296,256]{1,0:T(8,128)(2,1)S(1)}, bf16[1296,256]{1,0:T(8,128)(2,1)S(1)}, u32[]{:S(2)}, u32[]{:S(2)}) collective-permute-start(bf16[1296,256]{1,0:T(8,128)(2,1)S(1)} %get-tuple-element.78), channel_id=1, source_target_pairs={{0,8},{1,25},{2,10},{3,27},{4,12},{5,29},{6,14},{7,31},{8,16},{9,1... | collective-permute-start | bytes 1990664 | tf_op jit(solution)/shard_map/ppermute | solution.py:405
  25.0 11.4 %collective-permute-start.3 = (bf16[8,176,256]{2,1,0:T(8,128)(2,1)S(1)}, bf16[8,176,256]{2,1,0:T(8,128)(2,1)S(1)}, u32[]{:S(2)}, u32[]{:S(2)}) collective-permute-start(bf16[8,176,256]{2,1,0:T(8,128)(2,1)S(1)} %get-tuple-element.71), channel_id=1, source_target_pairs={{0,2},{1,33},{2,4},{3,35},{4,6},{5,37},{6,0},{7,39},{8,10},{9,41},... | collective-permute-start | bytes 2162696 | tf_op jit(solution)/shard_map/ppermute | solution.py:405
  25.5 12.5 %collective-permute-start.4 = (bf16[8,176,256]{2,1,0:T(8,128)(2,1)S(1)}, bf16[8,176,256]{2,1,0:T(8,128)(2,1)S(1)}, u32[]{:S(2)}, u32[]{:S(2)}) collective-permute-start(bf16[8,176,256]{2,1,0:T(8,128)(2,1)S(1)} %get-tuple-element.81), channel_id=1, source_target_pairs={{0,6},{1,97},{2,0},{3,99},{4,2},{5,101},{6,4},{7,103},{8,14},{9,10... | collective-permute-start | bytes 2162696 | tf_op jit(solution)/shard_map/ppermute | solution.py:405
  28.9 15.1 %collective-permute-start.5 = (bf16[8,176,256]{2,1,0:T(8,128)(2,1)S(1)}, bf16[8,176,256]{2,1,0:T(8,128)(2,1)S(1)}, u32[]{:S(2)}, u32[]{:S(2)}) collective-permute-start(bf16[8,176,256]{2,1,0:T(8,128)(2,1)S(1)} %get-tuple-element.74), channel_id=1, source_target_pairs={{0,2},{1,33},{2,4},{3,35},{4,6},{5,37},{6,0},{7,39},{8,10},{9,41},... | collective-permute-start | bytes 2162696 | tf_op jit(solution)/shard_map/ppermute | solution.py:405
  30.7 15.1 %collective-permute-start.6 = (bf16[8,176,256]{2,1,0:T(8,128)(2,1)S(1)}, bf16[8,176,256]{2,1,0:T(8,128)(2,1)S(1)}, u32[]{:S(2)}, u32[]{:S(2)}) collective-permute-start(bf16[8,176,256]{2,1,0:T(8,128)(2,1)S(1)} %get-tuple-element.83), channel_id=1, source_target_pairs={{0,6},{1,97},{2,0},{3,99},{4,2},{5,101},{6,4},{7,103},{8,14},{9,10... | collective-permute-start | bytes 2162696 | tf_op jit(solution)/shard_map/ppermute | solution.py:405
  33.8 14.6 %collective-permute-start.7 = (bf16[1296,256]{1,0:T(8,128)(2,1)S(1)}, bf16[1296,256]{1,0:T(8,128)(2,1)S(1)}, u32[]{:S(2)}, u32[]{:S(2)}) collective-permute-start(bf16[1296,256]{1,0:T(8,128)(2,1)S(1)} %shard_map.61), channel_id=1, source_target_pairs={{0,8},{1,25},{2,10},{3,27},{4,12},{5,29},{6,14},{7,31},{8,16},{9,1... | collective-permute-start | bytes 1990664 | tf_op jit(solution)/shard_map/ppermute | solution.py:405
  41.0 11.4 %collective-permute-start.8 = (bf16[8,176,256]{2,1,0:T(8,128)(2,1)S(1)}, bf16[8,176,256]{2,1,0:T(8,128)(2,1)S(1)}, u32[]{:S(2)}, u32[]{:S(2)}) collective-permute-start(bf16[8,176,256]{2,1,0:T(8,128)(2,1)S(1)} %get-tuple-element.82), channel_id=1, source_target_pairs={{0,2},{1,33},{2,4},{3,35},{4,6},{5,37},{6,0},{7,39},{8,10},{9,41},... | collective-permute-start | bytes 2162696 | tf_op jit(solution)/shard_map/ppermute | solution.py:405
  41.3 12.5 %collective-permute-start.9 = (bf16[8,176,256]{2,1,0:T(8,128)(2,1)S(1)}, bf16[8,176,256]{2,1,0:T(8,128)(2,1)S(1)}, u32[]{:S(2)}, u32[]{:S(2)}) collective-permute-start(bf16[8,176,256]{2,1,0:T(8,128)(2,1)S(1)} %get-tuple-element.98), channel_id=1, source_target_pairs={{0,6},{1,97},{2,0},{3,99},{4,2},{5,101},{6,4},{7,103},{8,14},{9,10... | collective-permute-start | bytes 2162696 | tf_op jit(solution)/shard_map/ppermute | solution.py:405
  48.5 17.6 %collective-permute-start.16 = (bf16[1296,256]{1,0:T(8,128)(2,1)S(1)}, bf16[1296,256]{1,0:T(8,128)(2,1)S(1)}, u32[]{:S(2)}, u32[]{:S(2)}) collective-permute-start(bf16[1296,256]{1,0:T(8,128)(2,1)S(1)} %shard_map.64), channel_id=1, source_target_pairs={{0,8},{1,25},{2,10},{3,27},{4,12},{5,29},{6,14},{7,31},{8,16},{9,1... | collective-permute-start | bytes 1990664 | tf_op jit(solution)/shard_map/ppermute | solution.py:405
  54.3 13.1 %collective-permute-start.10 = (bf16[4,176,256]{2,1,0:T(8,128)(2,1)S(1)}, bf16[4,176,256]{2,1,0:T(8,128)(2,1)S(1)}, u32[]{:S(2)}, u32[]{:S(2)}) collective-permute-start(bf16[4,176,256]{2,1,0:T(8,128)(2,1)S(1)} %get-tuple-element.100), channel_id=1, source_target_pairs={{0,64},{1,17},{2,66},{3,19},{4,68},{5,21},{6,70},{7,23},{8,72},{9,... | collective-permute-start | bytes 1081352 | tf_op jit(solution)/shard_map/ppermute | solution.py:405
  57.8 9.6 %collective-permute-start.11 = (bf16[4,176,256]{2,1,0:T(8,128)(2,1)S(1)}, bf16[4,176,256]{2,1,0:T(8,128)(2,1)S(1)}, u32[]{:S(2)}, u32[]{:S(2)}) collective-permute-start(bf16[4,176,256]{2,1,0:T(8,128)(2,1)S(1)} %get-tuple-element.101), channel_id=1, source_target_pairs={{0,32},{1,9},{2,34},{3,11},{4,36},{5,13},{6,38},{7,15},{8,40},{9,1... | collective-permute-start | bytes 1081352 | tf_op jit(solution)/shard_map/ppermute | solution.py:405
  59.0 9.3 %collective-permute-start.12 = (bf16[4,176,256]{2,1,0:T(8,128)(2,1)S(1)}, bf16[4,176,256]{2,1,0:T(8,128)(2,1)S(1)}, u32[]{:S(2)}, u32[]{:S(2)}) collective-permute-start(bf16[4,176,256]{2,1,0:T(8,128)(2,1)S(1)} %get-tuple-element.102), channel_id=1, source_target_pairs={{0,96},{1,25},{2,98},{3,27},{4,100},{5,29},{6,102},{7,31},{8,104},... | collective-permute-start | bytes 1081352 | tf_op jit(solution)/shard_map/ppermute | solution.py:405
  66.2 8.0 %collective-permute-start.17 = (bf16[336,256]{1,0:T(8,128)(2,1)S(1)}, bf16[336,256]{1,0:T(8,128)(2,1)S(1)}, u32[]{:S(2)}, u32[]{:S(2)}) collective-permute-start(bf16[336,256]{1,0:T(8,128)(2,1)S(1)} %get-tuple-element.115), channel_id=1, source_target_pairs={{0,4},{1,5},{2,6},{3,7},{4,0},{5,1},{6,2},{7,3},{8,12},{9,13},{10,... | collective-permute-start | bytes 516104 | tf_op jit(solution)/shard_map/ppermute | solution.py:405
  68.4 16.5 %collective-permute-start.13 = (f32[176,256]{1,0:T(8,128)S(1)}, f32[176,256]{1,0:T(8,128)S(1)}, u32[]{:S(2)}, u32[]{:S(2)}) collective-permute-start(f32[176,256]{1,0:T(8,128)S(1)} %get-tuple-element.104), channel_id=1, source_target_pairs={{0,16},{1,5},{2,18},{3,7},{4,20},{5,1},{6,22},{7,3},{8,24},{9,13},... | collective-permute-start | bytes 540680 | tf_op jit(solution)/shard_map/ppermute | solution.py:405
  70.6 7.3 %collective-permute-start.18 = (bf16[336,256]{1,0:T(8,128)(2,1)S(1)}, bf16[336,256]{1,0:T(8,128)(2,1)S(1)}, u32[]{:S(2)}, u32[]{:S(2)}) collective-permute-start(bf16[336,256]{1,0:T(8,128)(2,1)S(1)} %get-tuple-element.116), channel_id=1, source_target_pairs={{0,2},{1,7},{2,4},{3,1},{4,6},{5,3},{6,0},{7,5},{8,10},{9,15},{10,... | collective-permute-start | bytes 516104 | tf_op jit(solution)/shard_map/ppermute | solution.py:405
  70.7 8.5 %collective-permute-start.19 = (bf16[336,256]{1,0:T(8,128)(2,1)S(1)}, bf16[336,256]{1,0:T(8,128)(2,1)S(1)}, u32[]{:S(2)}, u32[]{:S(2)}) collective-permute-start(bf16[336,256]{1,0:T(8,128)(2,1)S(1)} %get-tuple-element.117), channel_id=1, source_target_pairs={{0,6},{1,3},{2,0},{3,5},{4,2},{5,7},{6,4},{7,1},{8,14},{9,11},{10,... | collective-permute-start | bytes 516104 | tf_op jit(solution)/shard_map/ppermute | solution.py:405
  72.6 14.5 %collective-permute-start.14 = (f32[176,256]{1,0:T(8,128)S(1)}, f32[176,256]{1,0:T(8,128)S(1)}, u32[]{:S(2)}, u32[]{:S(2)}) collective-permute-start(f32[176,256]{1,0:T(8,128)S(1)} %get-tuple-element.105), channel_id=1, source_target_pairs={{0,8},{1,3},{2,10},{3,5},{4,12},{5,7},{6,14},{7,1},{8,16},{9,11},{... | collective-permute-start | bytes 540680 | tf_op jit(solution)/shard_map/ppermute | solution.py:405
  74.2 13.0 %collective-permute-start.15 = (f32[176,256]{1,0:T(8,128)S(1)}, f32[176,256]{1,0:T(8,128)S(1)}, u32[]{:S(2)}, u32[]{:S(2)}) collective-permute-start(f32[176,256]{1,0:T(8,128)S(1)} %get-tuple-element.106), channel_id=1, source_target_pairs={{0,24},{1,7},{2,26},{3,1},{4,28},{5,3},{6,30},{7,5},{8,0},{9,15},{... | collective-permute-start | bytes 540680 | tf_op jit(solution)/shard_map/ppermute | solution.py:405
  79.2 8.1 %collective-permute-start.20 = (f32[88,256]{1,0:T(8,128)S(1)}, f32[88,256]{1,0:T(8,128)S(1)}, u32[]{:S(2)}, u32[]{:S(2)}) collective-permute-start(f32[88,256]{1,0:T(8,128)S(1)} %get-tuple-element.119), channel_id=1, source_target_pairs={{0,64},{1,65},{2,66},{3,67},{4,68},{5,69},{6,70},{7,71},{8,72},{9,... | collective-permute-start | bytes 270344 | tf_op jit(solution)/shard_map/ppermute | solution.py:405
  83.9 5.7 %collective-permute-start.21 = (f32[88,256]{1,0:T(8,128)S(1)}, f32[88,256]{1,0:T(8,128)S(1)}, u32[]{:S(2)}, u32[]{:S(2)}) collective-permute-start(f32[88,256]{1,0:T(8,128)S(1)} %get-tuple-element.120), channel_id=1, source_target_pairs={{0,32},{1,97},{2,34},{3,99},{4,36},{5,101},{6,38},{7,103},{8,40},{... | collective-permute-start | bytes 270344 | tf_op jit(solution)/shard_map/ppermute | solution.py:405
  85.0 4.6 %collective-permute-start.22 = (f32[88,256]{1,0:T(8,128)S(1)}, f32[88,256]{1,0:T(8,128)S(1)}, u32[]{:S(2)}, u32[]{:S(2)}) collective-permute-start(f32[88,256]{1,0:T(8,128)S(1)} %get-tuple-element.121), channel_id=1, source_target_pairs={{0,96},{1,33},{2,98},{3,35},{4,100},{5,37},{6,102},{7,39},{8,104},... | collective-permute-start | bytes 270344 | tf_op jit(solution)/shard_map/ppermute | solution.py:405
  87.2 16.5 %collective-permute-start.23 = (f32[176,256]{1,0:T(8,128)S(1)}, f32[176,256]{1,0:T(8,128)S(1)}, u32[]{:S(2)}, u32[]{:S(2)}) collective-permute-start(f32[176,256]{1,0:T(8,128)S(1)} %get-tuple-element.123), channel_id=1, source_target_pairs={{0,8},{1,16},{2,32},{3,48},{4,64},{5,80},{6,96},{7,112},{8,0},{9,2... | collective-permute-start | bytes 540680 | tf_op jit(solution)/shard_map/ppermute | solution.py:405
  89.6 15.7 %collective-permute-start.24 = (f32[80,256]{1,0:T(8,128)S(1)}, f32[80,256]{1,0:T(8,128)S(1)}, u32[]{:S(2)}, u32[]{:S(2)}) collective-permute-start(f32[80,256]{1,0:T(8,128)S(1)} %get-tuple-element.124), channel_id=1, source_target_pairs={{0,8},{1,16},{2,32},{3,48},{4,64},{5,80},{6,96},{7,112},{8,0},{9,2... | collective-permute-start | bytes 245768 | tf_op jit(solution)/shard_map/ppermute | solution.py:405

commit v7 on v6

--- a/solution.py
+++ b/solution.py
@@ -57,8 +57,8 @@
     return pairs
 
 
-MAIN_ORDER = (("x", "z", "y"), ("z", "y", "x"), 1)
-REST_ORDER = (("y", "x", "z"), ("y", "x", "z"), -1)
+MAIN_ORDER = (("x", "z", "y"), ("z", "x", "y"), 1)
+REST_ORDER = (("y", "x", "z"), ("y", "z", "x"), -1)
 
 
 def block_table(order, offsets):
@@ -81,9 +81,11 @@
 def cross_table():
     rows = []
     for device in range(128):
-        x, core = device // 2 % 4, device % 2
+        place = {"z": device // 32, "x": device // 2 % 4}
+        core = device % 2
         for d in range(4):
-            first = 2 * (2 * ((x + d * (1, REST_ORDER[2])[core]) % 4) + core)
+            lead = place[REST_ORDER[core][1]] + d * (1, REST_ORDER[2])[core]
+            first = 2 * (2 * (lead % 4) + core)
             rows += [first, first + 1, 0, 0]
     return np.asarray(rows, np.int32).reshape(128, -1)
 
@@ -367,16 +369,20 @@
         out[pl.ds(REST, 8), :] = cross
 
 
-def last_sum_kernel(own, second, first, third, out, sent):
-    total = own[...] + second[...] + first[...] + third[...]
-    out[...] = total
-    sent[...] = total[: sent.shape[0]].astype(sent.dtype)
-
-
-def finish_kernel(state, scale, main_ref, rest_ref, got_main_ref, got_rest_ref, out_ref):
+def last_sum_kernel(*refs):
+    mains, rests, (out, sent) = refs[:4], refs[4:8], refs[8:]
+    main = mains[0][...] + mains[1][...] + mains[2][...] + mains[3][...]
+    rest = rests[0][...] + rests[1][...] + rests[2][...] + rests[3][...]
+    out[pl.ds(0, MAIN), :] = main
+    out[pl.ds(MAIN, REST + 8), :] = rest
+    sent[pl.ds(0, MAIN), :] = main.astype(sent.dtype)
+    sent[pl.ds(MAIN, REST), :] = rest[:REST].astype(sent.dtype)
+
+
+def finish_kernel(state, scale, here_ref, got_ref, out_ref):
     s, fold = state[0], state[1]
-    here = jnp.concatenate([main_ref[...], rest_ref[0:REST, :]], axis=0) * scale
-    got = jnp.concatenate([got_main_ref[...], got_rest_ref[...]], axis=0).T.astype(F32) * scale
+    here = here_ref[pl.ds(0, BLK), :] * scale
+    got = got_ref[...].T.astype(F32) * scale
     first_at, second_at = pl.multiple_of(s * BLK, BLK), pl.multiple_of((1 - s) * BLK, BLK)
 
     @pl.when(fold == 0)
@@ -388,7 +394,7 @@
     def _():
         i = lax.broadcasted_iota(jnp.int32, (BLK, BLK), 0)
         j = lax.broadcasted_iota(jnp.int32, (BLK, BLK), 1)
-        cross = rest_ref[REST : REST + 1, :] * scale
+        cross = here_ref[pl.ds(BLK, 8), :][0:1] * scale
         out_ref[:, pl.ds(first_at, BLK)] = jnp.where(i >= j, here, here.T)
         out_ref[:, pl.ds(second_at, BLK)] = jnp.where(i == j, cross, jnp.where(i > j, got, here))
 
@@ -487,15 +493,17 @@
 
     got = [move(part[d], main_to(1, d)) for d in (2, 1, 3)]
     got_r = [move(rest[d], rest_to(1, d)) for d in (2, 1, 3)]
+    got, got_r = lax.optimization_barrier((got, got_r))
     part = call_sum(main_sum_kernel, [((MAIN, BLK), F32)] * 4, part[0], *got)
+    part, got_r = lax.optimization_barrier((part, got_r))
     rest = call_sum(rest_sum_kernel, [((REST + 8, BLK), F32)] * 4, rest[0], *got_r)
 
     got = [move(part[d], main_to(2, d)) for d in (2, 1, 3)]
     got_r = [move(rest[d], rest_to(2, d)) for d in (2, 1, 3)]
-    main_3, main_sent = call_sum(last_sum_kernel, [((MAIN, BLK), F32), ((MAIN, BLK), F32)], part[0], *got)
-    rest_3, rest_sent = call_sum(last_sum_kernel, [((REST + 8, BLK), F32), ((REST, BLK), F32)], rest[0], *got_r)
-    got_main = move(main_sent, mirror_pairs())
-    got_rest = move(rest_sent, mirror_pairs())
+    here, sent = call_sum(
+        last_sum_kernel, [((BLK + 8, BLK), F32), ((BLK, BLK), F32)], part[0], *got, rest[0], *got_r
+    )
+    got = move(sent, mirror_pairs())
 
     r, c = 4 * place["z"] + place["y"], 2 * place["x"] + core
     i, h = r // 2, r % 2
@@ -505,10 +513,10 @@
     return pl.pallas_call(
         lambda *refs: finish_kernel(refs[0], 1.0 / total_rows, *refs[1:]),
         out_shape=jax.ShapeDtypeStruct((BLK, 2 * BLK), F32),
-        in_specs=[pl.BlockSpec(memory_space=pltpu.SMEM)] + [vmem] * 4,
+        in_specs=[pl.BlockSpec(memory_space=pltpu.SMEM)] + [vmem] * 2,
         out_specs=vmem,
         compiler_params=pltpu.CompilerParams(vmem_limit_bytes=16 * 1024 * 1024),
-    )(state, main_3, rest_3, got_main, got_rest)
+    )(state, here, got)
 
 
 def solution(mesh):

time: 107 us -> 108 us (level)
  waiting for transfers between devices: 31.1 us -> 35.6 us
  starting transfers between devices: 36.5 us -> 33.4 us
    ppermute x23 -> x22, waiting for transfers between devices: 31.1 us -> 35.6 us  [move(): return lax.ppermute(array, AXES, pairs)]
    ppermute x23 -> x22, starting transfers between devices: 35.9 us -> 32.8 us  [move(): return lax.ppermute(array, AXES, pairs)]
  transfers between devices with their start and end apart: 25 -> 24, of which waited for: 15 -> 13; matrix products, arithmetic and copies ran while one was open for 1% -> 1% of each run, Pallas kernels for 22% -> 22%
where the time goes in v7:
time: 108 us
  waiting for transfers between devices  35.6 us (33%)
  Pallas kernels  34.5 us (32%)
  starting transfers between devices  33.4 us (31%)
  local copies, waits for them, and re-layouts  4.38 us (4%)
    ppermute x22, waiting for transfers between devices, move(): return lax.ppermute(array, AXES, pairs)  35.6 us
    ppermute x22, starting transfers between devices, move(): return lax.ppermute(array, AXES, pairs)  32.8 us
    pallas_call x8, Pallas kernels, products(): pl.pallas_call(functools.partial(product_kernel, plan, opening, cross_mad...  21.4 us
    pallas_call x1, Pallas kernels, scaled_rows(): pl.pallas_call(first_pick_kernel, out_shape=[jax.ShapeDtypeStruct((2 * un...  5.13 us
    unnamed x8, local copies, waits for them, and re-layouts  3.64 us
    pallas_call x1, Pallas kernels, scaled_rows(): pl.pallas_call(second_pick_kernel, out_shape=part, in_specs=[smem, vmem],...  3.44 us
  transfers between devices with their start and end apart: 24, of which 13 were waited for; matrix products, arithmetic and copies ran while one was open for 1% of the time, Pallas kernels for 22%

profile of v7, /device:TPU:6, one launch (start us, length us, event | category | flops | bytes accessed | tf_op | source)
XLA Modules:
  0.0 108.2 jit_solution(5241826855649548985)
XLA Ops:
  0.0 1.6 %copy-done = bf16[256,4096]{1,0:T(8,128)(2,1)S(1)} copy-done((bf16[256,4096]{1,0:T(8,128)(2,1)S(1)}, bf16[256,4096]{1,0:T(8,128)(2,1)}, u32[]{:S(2)}) %copy-start) | copy-done | bytes 2097176
  1.6 0.7 copy-done.1
  2.3 0.7 copy-done.2
  3.0 0.7 copy-done.3
  3.6 5.1 %shard_map.55 = (f32[8192,128]{1,0:T(8,128)S(1)}, bf16[2048,256]{1,0:T(8,128)(2,1)S(1)}) custom-call(s32[4096]{0:T(1024)S(1)} %copy-done.1, s32[8]{0:T(128)S(1)} %copy-done.3, f32[1,256]{1,0:T(1,128)S(1)} %bitcast.3, bf16[256,4096]{1,0:T(8,128)(2,1)S(1)} %copy-done), custom_call_target="tpu_custom_call" | custom-call | bytes 8388608 | tf_op jit(solution)/shard_map/pallas_call | solution.py:157
  8.8 0.1 collective-permute-start
  8.9 3.4 %shard_map.56.own_high.refs_1_ = bf16[2048,256]{1,0:T(8,128)(2,1)S(1)} custom-call(s32[4096]{0:T(1024)S(1)} %copy-done.1, f32[8192,128]{1,0:T(8,128)S(1)} %get-tuple-element.77.columns), custom_call_target="tpu_custom_call" | custom-call | bytes 8388608 | tf_op jit(solution)/shard_map/pallas_call | solution.py:166
  12.3 0.6 collective-permute-start.1
  12.9 0.7 dynamic-slice_reduce_fusion.table
  13.6 0.0 collective-permute-done.other_low.refs_2_
  13.7 2.2 %shard_map.57 = (bf16[256,4096]{1,0:T(8,128)(2,1)S(1)}, bf16[256,2048]{1,0:T(8,128)(2,1)S(1)}) custom-call(bf16[2048,256]{1,0:T(8,128)(2,1)S(1)} %get-tuple-element.76.own_low.refs_0_, bf16[2048,256]{1,0:T(8,128)(2,1)S(1)} %shard_map.56.own_high.refs_1_, bf16[2048,256]{1,0:T(8,128)(2,1)S(1)} %collective-permute-done.other_low.refs_2_), custom_call_target="tpu_custom_call" | custom-call | bytes 1048576 | tf_op jit(solution)/shard_map/pallas_call | solution.py:425
  15.8 4.2 %shard_map.58 = (bf16[1296,256]{1,0:T(8,128)(2,1)S(1)}, f32[16,256]{1,0:T(8,128)S(1)}, bf16[4096,512]{1,0:T(8,128)(2,1)S(1)}, bf16[512,4096]{1,0:T(8,128)(2,1)S(1)}) custom-call(s32[528]{0:T(1024)S(1)} %dynamic-slice_reduce_fusion.table, bf16[2048,256]{1,0:T(8,128)(2,1)S(1)} %get-tuple-element.76.own_low.refs_0_, ...), custom_call_target="tpu_custom_call" | custom-call | bytes 1048576 | tf_op jit(solution)/shard_map/pallas_call | solution.py:302
  20.1 2.5 %collective-permute-start.2 = (bf16[1296,256]{1,0:T(8,128)(2,1)S(1)}, bf16[1296,256]{1,0:T(8,128)(2,1)S(1)}, u32[]{:S(2)}, u32[]{:S(2)}) collective-permute-start(bf16[1296,256]{1,0:T(8,128)(2,1)S(1)} %get-tuple-element.89), channel_id=1, source_target_pairs={{0,8},{1,25},{2,10},{3,27},{4,12},{5,29},{6,14},{7,31},{8,16},{9,1... | collective-permute-start | bytes 1990664 | tf_op jit(solution)/shard_map/ppermute | solution.py:411
  22.6 2.4 %shard_map.59 = (bf16[8,176,256]{2,1,0:T(8,128)(2,1)S(1)}, bf16[8,176,256]{2,1,0:T(8,128)(2,1)S(1)}) custom-call(s32[528]{0:T(1024)S(1)} %dynamic-slice_reduce_fusion.table, bf16[4096,512]{1,0:T(8,128)(2,1)S(1)} %get-tuple-element.114.refs_0_, bf16[512,4096]{1,0:T(8,128)(2,1)S(1)} %get-tuple-element.115.refs_1_), custom_call_target="tpu_custom_call" | custom-call | bytes 1048576 | tf_op jit(solution)/shard_map/pallas_call | solution.py:302
  25.0 0.5 collective-permute-start.3
  25.5 1.5 %collective-permute-start.4 = (bf16[8,176,256]{2,1,0:T(8,128)(2,1)S(1)}, bf16[8,176,256]{2,1,0:T(8,128)(2,1)S(1)}, u32[]{:S(2)}, u32[]{:S(2)}) collective-permute-start(bf16[8,176,256]{2,1,0:T(8,128)(2,1)S(1)} %get-tuple-element.92), channel_id=1, source_target_pairs={{0,6},{1,97},{2,0},{3,99},{4,2},{5,101},{6,4},{7,103},{8,14},{9,10... | collective-permute-start | bytes 2162696 | tf_op jit(solution)/shard_map/ppermute | solution.py:411
  27.1 1.8 %shard_map.60 = (bf16[8,176,256]{2,1,0:T(8,128)(2,1)S(1)}, bf16[8,176,256]{2,1,0:T(8,128)(2,1)S(1)}) custom-call(s32[528]{0:T(1024)S(1)} %dynamic-slice_reduce_fusion.table, bf16[4096,512]{1,0:T(8,128)(2,1)S(1)} %get-tuple-element.114.refs_0_, bf16[512,4096]{1,0:T(8,128)(2,1)S(1)} %get-tuple-element.115.refs_1_), custom_call_target="tpu_custom_call" | custom-call | bytes 1048576 | tf_op jit(solution)/shard_map/pallas_call | solution.py:302
  28.9 1.8 %collective-permute-start.5 = (bf16[8,176,256]{2,1,0:T(8,128)(2,1)S(1)}, bf16[8,176,256]{2,1,0:T(8,128)(2,1)S(1)}, u32[]{:S(2)}, u32[]{:S(2)}) collective-permute-start(bf16[8,176,256]{2,1,0:T(8,128)(2,1)S(1)} %get-tuple-element.85), channel_id=1, source_target_pairs={{0,2},{1,33},{2,4},{3,35},{4,6},{5,37},{6,0},{7,39},{8,10},{9,41},... | collective-permute-start | bytes 2162696 | tf_op jit(solution)/shard_map/ppermute | solution.py:411
  30.7 0.5 collective-permute-start.6
  31.1 0.9 collective-permute-done.2.refs_3_
  32.0 1.8 %shard_map.61 = bf16[1296,256]{1,0:T(8,128)(2,1)S(1)} custom-call(s32[528]{0:T(1024)S(1)} %dynamic-slice_reduce_fusion.table, bf16[4096,512]{1,0:T(8,128)(2,1)S(1)} %get-tuple-element.114.refs_0_, bf16[512,4096]{1,0:T(8,128)(2,1)S(1)} %get-tuple-element.115.refs_1_, f32[16,256]{1,0:T(8,128)S(1)} %get-tuple-element.88.refs_2_, ...), custom_call_target="tpu_custom_call" | custom-call | bytes 1048576 | tf_op jit(solution)/shard_map/pallas_call | solution.py:302
  33.8 1.3 %collective-permute-start.7 = (bf16[1296,256]{1,0:T(8,128)(2,1)S(1)}, bf16[1296,256]{1,0:T(8,128)(2,1)S(1)}, u32[]{:S(2)}, u32[]{:S(2)}) collective-permute-start(bf16[1296,256]{1,0:T(8,128)(2,1)S(1)} %shard_map.61), channel_id=1, source_target_pairs={{0,8},{1,25},{2,10},{3,27},{4,12},{5,29},{6,14},{7,31},{8,16},{9,1... | collective-permute-start | bytes 1990664 | tf_op jit(solution)/shard_map/ppermute | solution.py:411
  35.1 1.2 %collective-permute-done.3.refs_2_ = bf16[8,176,256]{2,1,0:T(8,128)(2,1)S(1)} collective-permute-done((bf16[8,176,256]{2,1,0:T(8,128)(2,1)S(1)}, bf16[8,176,256]{2,1,0:T(8,128)(2,1)S(1)}, u32[]{:S(2)}, u32[]{:S(2)}) %collective-permute-start.3) | collective-permute-done | bytes 720928 | tf_op jit(solution)/shard_map/ppermute | solution.py:411
  36.3 1.7 %collective-permute-done.4.refs_3_ = bf16[8,176,256]{2,1,0:T(8,128)(2,1)S(1)} collective-permute-done((bf16[8,176,256]{2,1,0:T(8,128)(2,1)S(1)}, bf16[8,176,256]{2,1,0:T(8,128)(2,1)S(1)}, u32[]{:S(2)}, u32[]{:S(2)}) %collective-permute-start.4) | collective-permute-done | bytes 720928 | tf_op jit(solution)/shard_map/ppermute | solution.py:411
  38.0 2.9 %shard_map.62 = (bf16[8,176,256]{2,1,0:T(8,128)(2,1)S(1)}, bf16[8,176,256]{2,1,0:T(8,128)(2,1)S(1)}) custom-call(s32[528]{0:T(1024)S(1)} %dynamic-slice_reduce_fusion.table, bf16[4096,512]{1,0:T(8,128)(2,1)S(1)} %get-tuple-element.114.refs_0_, bf16[512,4096]{1,0:T(8,128)(2,1)S(1)} %get-tuple-element.115.refs_1_, ...), custom_call_target="tpu_custom_call" | custom-call | bytes 1048576 | tf_op jit(solution)/shard_map/pallas_call | solution.py:302
  41.0 0.4 collective-permute-start.8
  41.3 1.7 %collective-permute-start.9 = (bf16[8,176,256]{2,1,0:T(8,128)(2,1)S(1)}, bf16[8,176,256]{2,1,0:T(8,128)(2,1)S(1)}, u32[]{:S(2)}, u32[]{:S(2)}) collective-permute-start(bf16[8,176,256]{2,1,0:T(8,128)(2,1)S(1)} %get-tuple-element.109), channel_id=1, source_target_pairs={{0,6},{1,97},{2,0},{3,99},{4,2},{5,101},{6,4},{7,103},{8,14},{9,10... | collective-permute-start | bytes 2162696 | tf_op jit(solution)/shard_map/ppermute | solution.py:411
  43.1 1.0 collective-permute-done.5.refs_6_
  44.1 1.7 %collective-permute-done.6.refs_5_ = bf16[8,176,256]{2,1,0:T(8,128)(2,1)S(1)} collective-permute-done((bf16[8,176,256]{2,1,0:T(8,128)(2,1)S(1)}, bf16[8,176,256]{2,1,0:T(8,128)(2,1)S(1)}, u32[]{:S(2)}, u32[]{:S(2)}) %collective-permute-start.6) | collective-permute-done | bytes 720928 | tf_op jit(solution)/shard_map/ppermute | solution.py:411
  45.7 2.6 %shard_map.63.own = f32[1296,256]{1,0:T(8,128)S(1)} custom-call(s32[528]{0:T(1024)S(1)} %dynamic-slice_reduce_fusion.table, bf16[4096,512]{1,0:T(8,128)(2,1)S(1)} %get-tuple-element.114.refs_0_, bf16[512,4096]{1,0:T(8,128)(2,1)S(1)} %get-tuple-element.115.refs_1_, f32[16,256]{1,0:T(8,128)S(1)} %get-tuple-element.88.refs_2_), custom_call_target="tpu_custom_call" | custom-call | bytes 20971520 | tf_op jit(solution)/shard_map/pallas_call | solution.py:302
  48.4 0.1 shard_map.64
  48.5 0.8 collective-permute-start.13
  49.3 2.7 %shard_map.65 = (f32[4,176,256]{2,1,0:T(8,128)S(1)}, f32[4,176,256]{2,1,0:T(8,128)S(1)}, f32[4,176,256]{2,1,0:T(8,128)S(1)}, f32[4,176,256]{2,1,0:T(8,128)S(1)}) custom-call(s32[528]{0:T(1024)S(1)} %dynamic-slice_reduce_fusion.table, bf16[4096,512]{1,0:T(8,128)(2,1)S(1)} %get-tuple-element.114.refs_0_, bf16[512,4096]{1,0:T(8,128)(2,1)S(1)} %get-tuple-element.115.refs_1_), custom_call_target="tpu_custom_call" | custom-call | bytes 20971520 | tf_op jit(solution)/shard_map/pallas_call | solution.py:302
  52.0 0.3 collective-permute-done.8.refs_4_
  52.3 1.5 %collective-permute-done.9.refs_7_ = bf16[8,176,256]{2,1,0:T(8,128)(2,1)S(1)} collective-permute-done((bf16[8,176,256]{2,1,0:T(8,128)(2,1)S(1)}, bf16[8,176,256]{2,1,0:T(8,128)(2,1)S(1)}, u32[]{:S(2)}, u32[]{:S(2)}) %collective-permute-start.9) | collective-permute-done | bytes 720928 | tf_op jit(solution)/shard_map/ppermute | solution.py:411
  53.8 0.4 shard_map.66
  54.3 3.6 %collective-permute-start.10 = (bf16[4,176,256]{2,1,0:T(8,128)(2,1)S(1)}, bf16[4,176,256]{2,1,0:T(8,128)(2,1)S(1)}, u32[]{:S(2)}, u32[]{:S(2)}) collective-permute-start(bf16[4,176,256]{2,1,0:T(8,128)(2,1)S(1)} %get-tuple-element.111), channel_id=1, source_target_pairs={{0,64},{1,5},{2,66},{3,7},{4,68},{5,1},{6,70},{7,3},{8,72},{9,13},... | collective-permute-start | bytes 1081352 | tf_op jit(solution)/shard_map/ppermute | solution.py:411
  57.8 1.2 %collective-permute-start.11 = (bf16[4,176,256]{2,1,0:T(8,128)(2,1)S(1)}, bf16[4,176,256]{2,1,0:T(8,128)(2,1)S(1)}, u32[]{:S(2)}, u32[]{:S(2)}) collective-permute-start(bf16[4,176,256]{2,1,0:T(8,128)(2,1)S(1)} %get-tuple-element.112), channel_id=1, source_target_pairs={{0,32},{1,3},{2,34},{3,5},{4,36},{5,7},{6,38},{7,1},{8,40},{9,11},... | collective-permute-start | bytes 1081352 | tf_op jit(solution)/shard_map/ppermute | solution.py:411
  59.0 2.0 %collective-permute-start.12 = (bf16[4,176,256]{2,1,0:T(8,128)(2,1)S(1)}, bf16[4,176,256]{2,1,0:T(8,128)(2,1)S(1)}, u32[]{:S(2)}, u32[]{:S(2)}) collective-permute-start(bf16[4,176,256]{2,1,0:T(8,128)(2,1)S(1)} %get-tuple-element.113), channel_id=1, source_target_pairs={{0,96},{1,7},{2,98},{3,1},{4,100},{5,3},{6,102},{7,5},{8,104},{9,1... | collective-permute-start | bytes 1081352 | tf_op jit(solution)/shard_map/ppermute | solution.py:411
  61.1 2.8 %shard_map.67 = (f32[336,256]{1,0:T(8,128)S(1)}, f32[336,256]{1,0:T(8,128)S(1)}, f32[336,256]{1,0:T(8,128)S(1)}, f32[336,256]{1,0:T(8,128)S(1)}) custom-call(s32[528]{0:T(1024)S(1)} %dynamic-slice_reduce_fusion.table, bf16[4096,512]{1,0:T(8,128)(2,1)S(1)} %get-tuple-element.114.refs_0_, bf16[512,4096]{1,0:T(8,128)(2,1)S(1)} %get-tuple-element.115.refs_1_, ...), custom_call_target="tpu_custom_call" | custom-call | bytes 20971520 | tf_op jit(solution)/shard_map/pallas_call | solution.py:302
  63.9 0.1 shard_map.68
  64.0 1.4 %collective-permute-start.14 = (bf16[336,256]{1,0:T(8,128)(2,1)S(1)}, bf16[336,256]{1,0:T(8,128)(2,1)S(1)}, u32[]{:S(2)}, u32[]{:S(2)}) collective-permute-start(bf16[336,256]{1,0:T(8,128)(2,1)S(1)} %get-tuple-element.120), channel_id=1, source_target_pairs={{0,4},{1,65},{2,6},{3,67},{4,0},{5,69},{6,2},{7,71},{8,12},{9,73},... | collective-permute-start | bytes 516104 | tf_op jit(solution)/shard_map/ppermute | solution.py:411
  65.4 1.7 %collective-permute-start.15 = (bf16[336,256]{1,0:T(8,128)(2,1)S(1)}, bf16[336,256]{1,0:T(8,128)(2,1)S(1)}, u32[]{:S(2)}, u32[]{:S(2)}) collective-permute-start(bf16[336,256]{1,0:T(8,128)(2,1)S(1)} %get-tuple-element.121), channel_id=1, source_target_pairs={{0,2},{1,97},{2,4},{3,99},{4,6},{5,101},{6,0},{7,103},{8,10},{9,10... | collective-permute-start | bytes 516104 | tf_op jit(solution)/shard_map/ppermute | solution.py:411
  67.1 0.3 collective-permute-start.16
  67.4 3.4 %collective-permute-done.11.first = bf16[4,176,256]{2,1,0:T(8,128)(2,1)S(1)} collective-permute-done((bf16[4,176,256]{2,1,0:T(8,128)(2,1)S(1)}, bf16[4,176,256]{2,1,0:T(8,128)(2,1)S(1)}, u32[]{:S(2)}, u32[]{:S(2)}) %collective-permute-start.11) | collective-permute-done | bytes 360480 | tf_op jit(solution)/shard_map/ppermute | solution.py:411
  70.8 1.2 %collective-permute-done.12.third = bf16[4,176,256]{2,1,0:T(8,128)(2,1)S(1)} collective-permute-done((bf16[4,176,256]{2,1,0:T(8,128)(2,1)S(1)}, bf16[4,176,256]{2,1,0:T(8,128)(2,1)S(1)}, u32[]{:S(2)}, u32[]{:S(2)}) %collective-permute-start.12) | collective-permute-done | bytes 360480 | tf_op jit(solution)/shard_map/ppermute | solution.py:411
  72.0 1.7 %collective-permute-done.16.third = bf16[336,256]{1,0:T(8,128)(2,1)S(1)} collective-permute-done((bf16[336,256]{1,0:T(8,128)(2,1)S(1)}, bf16[336,256]{1,0:T(8,128)(2,1)S(1)}, u32[]{:S(2)}, u32[]{:S(2)}) %collective-permute-start.16) | collective-permute-done | bytes 172064 | tf_op jit(solution)/shard_map/ppermute | solution.py:411
  73.8 0.1 shard_map.69
  73.9 0.1 shard_map.70
  74.0 0.5 collective-permute-start.20
  74.5 1.9 %collective-permute-start.17 = (f32[176,256]{1,0:T(8,128)S(1)}, f32[176,256]{1,0:T(8,128)S(1)}, u32[]{:S(2)}, u32[]{:S(2)}) collective-permute-start(f32[176,256]{1,0:T(8,128)S(1)} %get-tuple-element.134), channel_id=1, source_target_pairs={{0,16},{1,17},{2,18},{3,19},{4,20},{5,21},{6,22},{7,23},{8,24},{9,... | collective-permute-start | bytes 540680 | tf_op jit(solution)/shard_map/ppermute | solution.py:411
  76.4 1.3 %collective-permute-start.18 = (f32[176,256]{1,0:T(8,128)S(1)}, f32[176,256]{1,0:T(8,128)S(1)}, u32[]{:S(2)}, u32[]{:S(2)}) collective-permute-start(f32[176,256]{1,0:T(8,128)S(1)} %get-tuple-element.135), channel_id=1, source_target_pairs={{0,8},{1,9},{2,10},{3,11},{4,12},{5,13},{6,14},{7,15},{8,16},{9,17... | collective-permute-start | bytes 540680 | tf_op jit(solution)/shard_map/ppermute | solution.py:411
  77.7 2.7 %collective-permute-start.19 = (f32[176,256]{1,0:T(8,128)S(1)}, f32[176,256]{1,0:T(8,128)S(1)}, u32[]{:S(2)}, u32[]{:S(2)}) collective-permute-start(f32[176,256]{1,0:T(8,128)S(1)} %get-tuple-element.136), channel_id=1, source_target_pairs={{0,24},{1,25},{2,26},{3,27},{4,28},{5,29},{6,30},{7,31},{8,0},{9,1... | collective-permute-start | bytes 540680 | tf_op jit(solution)/shard_map/ppermute | solution.py:411
  80.4 1.5 %collective-permute-start.21 = (f32[88,256]{1,0:T(8,128)S(1)}, f32[88,256]{1,0:T(8,128)S(1)}, u32[]{:S(2)}, u32[]{:S(2)}) collective-permute-start(f32[88,256]{1,0:T(8,128)S(1)} %get-tuple-element.143), channel_id=1, source_target_pairs={{0,32},{1,7},{2,34},{3,1},{4,36},{5,3},{6,38},{7,5},{8,40},{9,15},... | collective-permute-start | bytes 270344 | tf_op jit(solution)/shard_map/ppermute | solution.py:411
  81.9 0.0 collective-permute-done.20.refs_5_
  81.9 1.7 %collective-permute-start.22 = (f32[88,256]{1,0:T(8,128)S(1)}, f32[88,256]{1,0:T(8,128)S(1)}, u32[]{:S(2)}, u32[]{:S(2)}) collective-permute-start(f32[88,256]{1,0:T(8,128)S(1)} %get-tuple-element.144), channel_id=1, source_target_pairs={{0,96},{1,3},{2,98},{3,5},{4,100},{5,7},{6,102},{7,1},{8,104},{9,1... | collective-permute-start | bytes 270344 | tf_op jit(solution)/shard_map/ppermute | solution.py:411
  83.6 2.5 %collective-permute-done.21.refs_6_ = f32[88,256]{1,0:T(8,128)S(1)} collective-permute-done((f32[88,256]{1,0:T(8,128)S(1)}, f32[88,256]{1,0:T(8,128)S(1)}, u32[]{:S(2)}, u32[]{:S(2)}) %collective-permute-start.21) | collective-permute-done | bytes 90144 | tf_op jit(solution)/shard_map/ppermute | solution.py:411
  86.1 0.3 collective-permute-done.22.refs_7_
  86.4 0.0 collective-permute-done.17.refs_1_
  86.5 0.1 shard_map.71
  86.5 2.0 %collective-permute-start.23 = (f32[256,256]{1,0:T(8,128)S(1)}, f32[256,256]{1,0:T(8,128)S(1)}, u32[]{:S(2)}, u32[]{:S(2)}) collective-permute-start(f32[256,256]{1,0:T(8,128)S(1)} %get-tuple-element.146), channel_id=1, source_target_pairs={{0,8},{1,16},{2,32},{3,48},{4,64},{5,80},{6,96},{7,112},{8,0},{9,2... | collective-permute-start | bytes 786440 | tf_op jit(solution)/shard_map/ppermute | solution.py:411
  88.5 0.1 pad_add_fusion.refs_0_
  88.6 18.1 %collective-permute-done.23.refs_2_ = f32[256,256]{1,0:T(8,128)S(1)} collective-permute-done((f32[256,256]{1,0:T(8,128)S(1)}, f32[256,256]{1,0:T(8,128)S(1)}, u32[]{:S(2)}, u32[]{:S(2)}) %collective-permute-start.23) | collective-permute-done | bytes 262176 | tf_op jit(solution)/shard_map/ppermute | solution.py:411
  106.7 1.5 %shard_map.72 = f32[256,512]{1,0:T(8,128)} custom-call(s32[2]{0:T(128)S(1)} %pad_add_fusion.refs_0_, f32[264,256]{1,0:T(8,128)S(1)} %get-tuple-element.145.refs_1_, f32[256,256]{1,0:T(8,128)S(1)} %collective-permute-done.23.refs_2_), custom_call_target="tpu_custom_call" | custom-call | tf_op jit(solution)/shard_map/pallas_call | solution.py:513
  (12 shorter events, 0.0 us)
Async XLA Ops:
  0.0 1.6 %copy-start = (bf16[256,4096]{1,0:T(8,128)(2,1)S(1)}, bf16[256,4096]{1,0:T(8,128)(2,1)}, u32[]{:S(2)}) copy-start(bf16[256,4096]{1,0:T(8,128)(2,1)} %design_ref.1) | copy-start | bytes 6291460
  1.6 0.7 copy-start.1
  2.3 0.7 copy-start.2
  3.0 0.7 copy-start.3
  8.8 4.9 %collective-permute-start = (bf16[2048,256]{1,0:T(8,128)(2,1)S(1)}, bf16[2048,256]{1,0:T(8,128)(2,1)S(1)}, u32[]{:S(2)}, u32[]{:S(2)}) collective-permute-start(bf16[2048,256]{1,0:T(8,128)(2,1)S(1)} %get-tuple-element.76.own_low.refs_0_), channel_id=1, source_target_pairs={{0,1},{1,0},{2,3},{3,2},{4,5},{5,4},{6,7},{7,6},{8,9},{9,8},{10,11... | collective-permute-start | bytes 3145736 | tf_op jit(solution)/shard_map/ppermute | solution.py:422
  12.3 3.5 %collective-permute-start.1 = (bf16[2048,256]{1,0:T(8,128)(2,1)S(1)}, bf16[2048,256]{1,0:T(8,128)(2,1)}, u32[]{:S(2)}, u32[]{:S(2)}) collective-permute-start(bf16[2048,256]{1,0:T(8,128)(2,1)S(1)} %shard_map.56.own_high.refs_1_), channel_id=1, source_target_pairs={{0,1},{1,0},{2,3},{3,2},{4,5},{5,4},{6,7},{7,6},{8,9},{9,8},{10,11... | collective-permute-start | bytes 3145736 | tf_op jit(solution)/shard_map/ppermute | solution.py:423
  20.1 12.0 %collective-permute-start.2 = (bf16[1296,256]{1,0:T(8,128)(2,1)S(1)}, bf16[1296,256]{1,0:T(8,128)(2,1)S(1)}, u32[]{:S(2)}, u32[]{:S(2)}) collective-permute-start(bf16[1296,256]{1,0:T(8,128)(2,1)S(1)} %get-tuple-element.89), channel_id=1, source_target_pairs={{0,8},{1,25},{2,10},{3,27},{4,12},{5,29},{6,14},{7,31},{8,16},{9,1... | collective-permute-start | bytes 1990664 | tf_op jit(solution)/shard_map/ppermute | solution.py:411
  25.0 11.4 %collective-permute-start.3 = (bf16[8,176,256]{2,1,0:T(8,128)(2,1)S(1)}, bf16[8,176,256]{2,1,0:T(8,128)(2,1)S(1)}, u32[]{:S(2)}, u32[]{:S(2)}) collective-permute-start(bf16[8,176,256]{2,1,0:T(8,128)(2,1)S(1)} %get-tuple-element.82), channel_id=1, source_target_pairs={{0,2},{1,33},{2,4},{3,35},{4,6},{5,37},{6,0},{7,39},{8,10},{9,41},... | collective-permute-start | bytes 2162696 | tf_op jit(solution)/shard_map/ppermute | solution.py:411
  25.5 12.5 %collective-permute-start.4 = (bf16[8,176,256]{2,1,0:T(8,128)(2,1)S(1)}, bf16[8,176,256]{2,1,0:T(8,128)(2,1)S(1)}, u32[]{:S(2)}, u32[]{:S(2)}) collective-permute-start(bf16[8,176,256]{2,1,0:T(8,128)(2,1)S(1)} %get-tuple-element.92), channel_id=1, source_target_pairs={{0,6},{1,97},{2,0},{3,99},{4,2},{5,101},{6,4},{7,103},{8,14},{9,10... | collective-permute-start | bytes 2162696 | tf_op jit(solution)/shard_map/ppermute | solution.py:411
  28.9 15.1 %collective-permute-start.5 = (bf16[8,176,256]{2,1,0:T(8,128)(2,1)S(1)}, bf16[8,176,256]{2,1,0:T(8,128)(2,1)S(1)}, u32[]{:S(2)}, u32[]{:S(2)}) collective-permute-start(bf16[8,176,256]{2,1,0:T(8,128)(2,1)S(1)} %get-tuple-element.85), channel_id=1, source_target_pairs={{0,2},{1,33},{2,4},{3,35},{4,6},{5,37},{6,0},{7,39},{8,10},{9,41},... | collective-permute-start | bytes 2162696 | tf_op jit(solution)/shard_map/ppermute | solution.py:411
  30.7 15.1 %collective-permute-start.6 = (bf16[8,176,256]{2,1,0:T(8,128)(2,1)S(1)}, bf16[8,176,256]{2,1,0:T(8,128)(2,1)S(1)}, u32[]{:S(2)}, u32[]{:S(2)}) collective-permute-start(bf16[8,176,256]{2,1,0:T(8,128)(2,1)S(1)} %get-tuple-element.94), channel_id=1, source_target_pairs={{0,6},{1,97},{2,0},{3,99},{4,2},{5,101},{6,4},{7,103},{8,14},{9,10... | collective-permute-start | bytes 2162696 | tf_op jit(solution)/shard_map/ppermute | solution.py:411
  33.8 14.6 %collective-permute-start.7 = (bf16[1296,256]{1,0:T(8,128)(2,1)S(1)}, bf16[1296,256]{1,0:T(8,128)(2,1)S(1)}, u32[]{:S(2)}, u32[]{:S(2)}) collective-permute-start(bf16[1296,256]{1,0:T(8,128)(2,1)S(1)} %shard_map.61), channel_id=1, source_target_pairs={{0,8},{1,25},{2,10},{3,27},{4,12},{5,29},{6,14},{7,31},{8,16},{9,1... | collective-permute-start | bytes 1990664 | tf_op jit(solution)/shard_map/ppermute | solution.py:411
  41.0 11.4 %collective-permute-start.8 = (bf16[8,176,256]{2,1,0:T(8,128)(2,1)S(1)}, bf16[8,176,256]{2,1,0:T(8,128)(2,1)S(1)}, u32[]{:S(2)}, u32[]{:S(2)}) collective-permute-start(bf16[8,176,256]{2,1,0:T(8,128)(2,1)S(1)} %get-tuple-element.93), channel_id=1, source_target_pairs={{0,2},{1,33},{2,4},{3,35},{4,6},{5,37},{6,0},{7,39},{8,10},{9,41},... | collective-permute-start | bytes 2162696 | tf_op jit(solution)/shard_map/ppermute | solution.py:411
  41.3 12.5 %collective-permute-start.9 = (bf16[8,176,256]{2,1,0:T(8,128)(2,1)S(1)}, bf16[8,176,256]{2,1,0:T(8,128)(2,1)S(1)}, u32[]{:S(2)}, u32[]{:S(2)}) collective-permute-start(bf16[8,176,256]{2,1,0:T(8,128)(2,1)S(1)} %get-tuple-element.109), channel_id=1, source_target_pairs={{0,6},{1,97},{2,0},{3,99},{4,2},{5,101},{6,4},{7,103},{8,14},{9,10... | collective-permute-start | bytes 2162696 | tf_op jit(solution)/shard_map/ppermute | solution.py:411
  48.5 15.4 %collective-permute-start.13 = (bf16[1296,256]{1,0:T(8,128)(2,1)S(1)}, bf16[1296,256]{1,0:T(8,128)(2,1)S(1)}, u32[]{:S(2)}, u32[]{:S(2)}) collective-permute-start(bf16[1296,256]{1,0:T(8,128)(2,1)S(1)} %shard_map.64), channel_id=1, source_target_pairs={{0,8},{1,25},{2,10},{3,27},{4,12},{5,29},{6,14},{7,31},{8,16},{9,1... | collective-permute-start | bytes 1990664 | tf_op jit(solution)/shard_map/ppermute | solution.py:411
  54.3 12.9 %collective-permute-start.10 = (bf16[4,176,256]{2,1,0:T(8,128)(2,1)S(1)}, bf16[4,176,256]{2,1,0:T(8,128)(2,1)S(1)}, u32[]{:S(2)}, u32[]{:S(2)}) collective-permute-start(bf16[4,176,256]{2,1,0:T(8,128)(2,1)S(1)} %get-tuple-element.111), channel_id=1, source_target_pairs={{0,64},{1,5},{2,66},{3,7},{4,68},{5,1},{6,70},{7,3},{8,72},{9,13},... | collective-permute-start | bytes 1081352 | tf_op jit(solution)/shard_map/ppermute | solution.py:411
  57.8 13.0 %collective-permute-start.11 = (bf16[4,176,256]{2,1,0:T(8,128)(2,1)S(1)}, bf16[4,176,256]{2,1,0:T(8,128)(2,1)S(1)}, u32[]{:S(2)}, u32[]{:S(2)}) collective-permute-start(bf16[4,176,256]{2,1,0:T(8,128)(2,1)S(1)} %get-tuple-element.112), channel_id=1, source_target_pairs={{0,32},{1,3},{2,34},{3,5},{4,36},{5,7},{6,38},{7,1},{8,40},{9,11},... | collective-permute-start | bytes 1081352 | tf_op jit(solution)/shard_map/ppermute | solution.py:411
  59.0 13.0 %collective-permute-start.12 = (bf16[4,176,256]{2,1,0:T(8,128)(2,1)S(1)}, bf16[4,176,256]{2,1,0:T(8,128)(2,1)S(1)}, u32[]{:S(2)}, u32[]{:S(2)}) collective-permute-start(bf16[4,176,256]{2,1,0:T(8,128)(2,1)S(1)} %get-tuple-element.113), channel_id=1, source_target_pairs={{0,96},{1,7},{2,98},{3,1},{4,100},{5,3},{6,102},{7,5},{8,104},{9,1... | collective-permute-start | bytes 1081352 | tf_op jit(solution)/shard_map/ppermute | solution.py:411
  64.0 8.0 %collective-permute-start.14 = (bf16[336,256]{1,0:T(8,128)(2,1)S(1)}, bf16[336,256]{1,0:T(8,128)(2,1)S(1)}, u32[]{:S(2)}, u32[]{:S(2)}) collective-permute-start(bf16[336,256]{1,0:T(8,128)(2,1)S(1)} %get-tuple-element.120), channel_id=1, source_target_pairs={{0,4},{1,65},{2,6},{3,67},{4,0},{5,69},{6,2},{7,71},{8,12},{9,73},... | collective-permute-start | bytes 516104 | tf_op jit(solution)/shard_map/ppermute | solution.py:411
  65.4 6.6 %collective-permute-start.15 = (bf16[336,256]{1,0:T(8,128)(2,1)S(1)}, bf16[336,256]{1,0:T(8,128)(2,1)S(1)}, u32[]{:S(2)}, u32[]{:S(2)}) collective-permute-start(bf16[336,256]{1,0:T(8,128)(2,1)S(1)} %get-tuple-element.121), channel_id=1, source_target_pairs={{0,2},{1,97},{2,4},{3,99},{4,6},{5,101},{6,0},{7,103},{8,10},{9,10... | collective-permute-start | bytes 516104 | tf_op jit(solution)/shard_map/ppermute | solution.py:411
  67.1 6.6 %collective-permute-start.16 = (bf16[336,256]{1,0:T(8,128)(2,1)S(1)}, bf16[336,256]{1,0:T(8,128)(2,1)S(1)}, u32[]{:S(2)}, u32[]{:S(2)}) collective-permute-start(bf16[336,256]{1,0:T(8,128)(2,1)S(1)} %get-tuple-element.122), channel_id=1, source_target_pairs={{0,6},{1,33},{2,0},{3,35},{4,2},{5,37},{6,4},{7,39},{8,14},{9,41},... | collective-permute-start | bytes 516104 | tf_op jit(solution)/shard_map/ppermute | solution.py:411
  74.0 7.9 %collective-permute-start.20 = (f32[88,256]{1,0:T(8,128)S(1)}, f32[88,256]{1,0:T(8,128)S(1)}, u32[]{:S(2)}, u32[]{:S(2)}) collective-permute-start(f32[88,256]{1,0:T(8,128)S(1)} %get-tuple-element.142), channel_id=1, source_target_pairs={{0,64},{1,5},{2,66},{3,7},{4,68},{5,1},{6,70},{7,3},{8,72},{9,13},... | collective-permute-start | bytes 270344 | tf_op jit(solution)/shard_map/ppermute | solution.py:411
  74.5 12.0 %collective-permute-start.17 = (f32[176,256]{1,0:T(8,128)S(1)}, f32[176,256]{1,0:T(8,128)S(1)}, u32[]{:S(2)}, u32[]{:S(2)}) collective-permute-start(f32[176,256]{1,0:T(8,128)S(1)} %get-tuple-element.134), channel_id=1, source_target_pairs={{0,16},{1,17},{2,18},{3,19},{4,20},{5,21},{6,22},{7,23},{8,24},{9,... | collective-permute-start | bytes 540680 | tf_op jit(solution)/shard_map/ppermute | solution.py:411
  76.4 10.0 %collective-permute-start.18 = (f32[176,256]{1,0:T(8,128)S(1)}, f32[176,256]{1,0:T(8,128)S(1)}, u32[]{:S(2)}, u32[]{:S(2)}) collective-permute-start(f32[176,256]{1,0:T(8,128)S(1)} %get-tuple-element.135), channel_id=1, source_target_pairs={{0,8},{1,9},{2,10},{3,11},{4,12},{5,13},{6,14},{7,15},{8,16},{9,17... | collective-permute-start | bytes 540680 | tf_op jit(solution)/shard_map/ppermute | solution.py:411
  77.7 8.7 %collective-permute-start.19 = (f32[176,256]{1,0:T(8,128)S(1)}, f32[176,256]{1,0:T(8,128)S(1)}, u32[]{:S(2)}, u32[]{:S(2)}) collective-permute-start(f32[176,256]{1,0:T(8,128)S(1)} %get-tuple-element.136), channel_id=1, source_target_pairs={{0,24},{1,25},{2,26},{3,27},{4,28},{5,29},{6,30},{7,31},{8,0},{9,1... | collective-permute-start | bytes 540680 | tf_op jit(solution)/shard_map/ppermute | solution.py:411
  80.4 5.7 %collective-permute-start.21 = (f32[88,256]{1,0:T(8,128)S(1)}, f32[88,256]{1,0:T(8,128)S(1)}, u32[]{:S(2)}, u32[]{:S(2)}) collective-permute-start(f32[88,256]{1,0:T(8,128)S(1)} %get-tuple-element.143), channel_id=1, source_target_pairs={{0,32},{1,7},{2,34},{3,1},{4,36},{5,3},{6,38},{7,5},{8,40},{9,15},... | collective-permute-start | bytes 270344 | tf_op jit(solution)/shard_map/ppermute | solution.py:411
  81.9 4.5 %collective-permute-start.22 = (f32[88,256]{1,0:T(8,128)S(1)}, f32[88,256]{1,0:T(8,128)S(1)}, u32[]{:S(2)}, u32[]{:S(2)}) collective-permute-start(f32[88,256]{1,0:T(8,128)S(1)} %get-tuple-element.144), channel_id=1, source_target_pairs={{0,96},{1,3},{2,98},{3,5},{4,100},{5,7},{6,102},{7,1},{8,104},{9,1... | collective-permute-start | bytes 270344 | tf_op jit(solution)/shard_map/ppermute | solution.py:411
  86.5 20.1 %collective-permute-start.23 = (f32[256,256]{1,0:T(8,128)S(1)}, f32[256,256]{1,0:T(8,128)S(1)}, u32[]{:S(2)}, u32[]{:S(2)}) collective-permute-start(f32[256,256]{1,0:T(8,128)S(1)} %get-tuple-element.146), channel_id=1, source_target_pairs={{0,8},{1,16},{2,32},{3,48},{4,64},{5,80},{6,96},{7,112},{8,0},{9,2... | collective-permute-start | bytes 786440 | tf_op jit(solution)/shard_map/ppermute | solution.py:411
